TPU v7x, 128 devices: a whole 4x4x4 slice. The times are simulated.
128 devices in a mesh: dp: 8 (over x, core), expert: 16 (over z, y).
Axes of the slice: x: 4, y: 4, z: 4, core: 2. Of those that a mesh axis runs over, the one named last changes fastest.
Arguments:
- activations: bfloat16 [16384, 2048], P(('dp', 'expert')), may hold values from -6 to 6
- out_grad: bfloat16 [16384, 2048], P(('dp', 'expert')), may hold values from -4 to 4
- gate_probs: bfloat16 [16384, 8], P(('dp', 'expert')), may hold values from 0.019897461 to 0.29882812
- expert_ids: int32 [16384, 8], P('dp'), may hold values from 0 to 31, all different within a row; in each aligned block of 128 rows (0 to 127, 128 to 255, ...) at most 48 rows name the same one
- w_gate: bfloat16 [32, 2048, 512], P('expert'), may hold values from -0.125 to 0.125
- w_up: bfloat16 [32, 2048, 512], P('expert'), may hold values from -0.125 to 0.125
- w_down: bfloat16 [32, 512, 2048], P('expert'), may hold values from -0.25 to 0.25
Outputs:
- grad_act: bfloat16 [16384, 2048], P(('dp', 'expert'))
- grad_prob: float32 [16384, 8], P(('dp', 'expert'))
- grad_gate: bfloat16 [32, 2048, 512], P('expert', 'dp')
- grad_up: bfloat16 [32, 2048, 512], P('expert', 'dp')
- grad_down: bfloat16 [32, 512, 2048], P('expert', 'dp')
Inputs may be any that keep to these rules, and one draw needn't show every extreme that they name: `expert_ids`: each row names 8 different experts. In every aligned block of 128 rows (the tokens of one device) no expert is named by more than 48 rows, and in some blocks one is named by exactly 48 rows.
All inputs are finite; a program needn't handle non-finite values.
Results may differ from a plain program's by a relative error of at most 0.017.
Values may be sent and summed in bfloat16 or wider, within the bound.
No kernel may reach another device: no remote copies, remote signals or barrier semaphores. Data moves between devices by JAX's collectives and lax.ppermute only.
A program may use at most 192 MiB of HBM per device.

v0:
```python
import jax
import jax.numpy as jnp
from jax import lax
from jax.sharding import PartitionSpec as P

TOP = 8


def to_half(value):
    return lax.optimization_barrier(value.astype(jnp.bfloat16)).astype(jnp.float32)


def slot_table(routes, experts, tok_dev, peer_slots):
    hit_count = jnp.sum((routes[:, :, None] == experts[None, None, :]).astype(jnp.int32), axis=1)
    blocks = routes.shape[0] // tok_dev
    hit_count = hit_count.reshape(blocks, tok_dev, -1)
    slot_rank = jnp.cumsum(hit_count, axis=1) - hit_count
    counts = jnp.sum(hit_count, axis=1)
    target = jnp.where(hit_count > 0, slot_rank, peer_slots)
    places = jnp.arange(peer_slots, dtype=jnp.int32)
    local_rows = jnp.arange(tok_dev, dtype=jnp.int32)
    slot_token = jnp.sum(
        jnp.where(
            target[:, :, :, None] == places[None, None, None, :],
            local_rows[None, :, None, None],
            jnp.int32(0),
        ),
        axis=1,
    )
    slot_token = slot_token + (jnp.arange(blocks, dtype=jnp.int32) * tok_dev)[:, None, None]
    live_slot = places[None, None, :] < counts[:, :, None]
    expert_count = experts.shape[0]
    slot_token = jnp.transpose(slot_token, (1, 0, 2)).reshape(expert_count, blocks * peer_slots)
    live_slot = jnp.transpose(live_slot, (1, 0, 2)).reshape(expert_count, blocks * peer_slots)
    return (slot_token, live_slot)


def expert_pass(rows_x, rows_dy, slot_gate, gate_w, up_w, down_w):
    single = jnp.float32
    pre_gate = jnp.einsum("ecd,edf->ecf", rows_x, gate_w, preferred_element_type=single)
    pre_up = jnp.einsum("ecd,edf->ecf", rows_x, up_w, preferred_element_type=single)
    sigmoid_gate = jax.nn.sigmoid(pre_gate)
    hidden_act = (pre_gate * sigmoid_gate * pre_up).astype(jnp.bfloat16)
    expert_out = jnp.einsum("ecf,efd->ecd", hidden_act, down_w, preferred_element_type=single)
    slot_dot = jnp.einsum("ecd,ecd->ec", rows_dy.astype(single), expert_out)
    scaled = (slot_gate[:, :, None] * rows_dy).astype(jnp.bfloat16)
    hidden_grad = jnp.einsum("ecd,efd->ecf", scaled, down_w, preferred_element_type=single)
    gate_grad = (
        hidden_grad * pre_up * sigmoid_gate * (1.0 + pre_gate * (1.0 - sigmoid_gate))
    ).astype(jnp.bfloat16)
    up_grad = (hidden_grad * pre_gate * sigmoid_gate).astype(jnp.bfloat16)
    sum_down = jnp.einsum("ecf,ecd->efd", hidden_act, scaled, preferred_element_type=single)
    sum_gate = jnp.einsum("ecd,ecf->edf", rows_x, gate_grad, preferred_element_type=single)
    sum_up = jnp.einsum("ecd,ecf->edf", rows_x, up_grad, preferred_element_type=single)
    row_grad = jnp.einsum("ecf,edf->ecd", gate_grad, gate_w, preferred_element_type=single)
    row_grad = row_grad + jnp.einsum("ecf,edf->ecd", up_grad, up_w, preferred_element_type=single)
    return (slot_dot, row_grad, sum_gate, sum_up, sum_down)


def on_device(activations, out_grad, gate_probs, expert_ids, w_gate, w_up, w_down):
    dev_count = lax.axis_size("expert")
    my_index = lax.axis_index("expert")
    tok_dev = activations.shape[0]
    model_width = activations.shape[1]
    exp_dev = w_gate.shape[0]
    group_rows = expert_ids.shape[0]
    peer_slots = 3 * tok_dev * TOP // (2 * exp_dev * dev_count)
    my_experts = my_index * exp_dev + jnp.arange(exp_dev, dtype=jnp.int32)
    slot_token, live_slot = slot_table(expert_ids, my_experts, tok_dev, peer_slots)
    expert_lane = jnp.broadcast_to(jnp.arange(exp_dev, dtype=jnp.int32)[:, None], slot_token.shape)
    whole_x, whole_dy, whole_probs = (
        lax.all_gather(activations, "expert", axis=0, tiled=True),
        lax.all_gather(out_grad, "expert", axis=0, tiled=True),
        lax.all_gather(gate_probs, "expert", axis=0, tiled=True),
    )
    group_sel = jnp.sum(
        jnp.where(
            expert_ids[:, :, None] == my_experts[None, None, :],
            whole_probs.astype(jnp.float32)[:, :, None],
            0.0,
        ),
        axis=1,
    )
    slot_gate = jnp.where(live_slot, group_sel[slot_token, expert_lane], 0.0)
    rows_x = whole_x[slot_token]
    rows_dy = whole_dy[slot_token]
    slot_dot, row_grad, sum_gate, sum_up, sum_down = expert_pass(
        rows_x, rows_dy, slot_gate, w_gate, w_up, w_down
    )
    act_part = (
        jnp.zeros((group_rows, model_width), jnp.float32)
        .at[slot_token.reshape(-1)]
        .add(row_grad.reshape(-1, model_width))
    )
    prob_cols = (
        jnp.zeros((group_rows, exp_dev), jnp.float32)
        .at[slot_token, expert_lane]
        .add(jnp.where(live_slot, slot_dot, 0.0))
    )
    prob_part = jnp.sum(
        jnp.where(expert_ids[:, :, None] == my_experts[None, None, :], prob_cols[:, None, :], 0.0),
        axis=2,
    )
    grad_act = lax.psum_scatter(
        to_half(act_part).astype(jnp.bfloat16), "expert", scatter_dimension=0, tiled=True
    )
    grad_prob = lax.psum_scatter(
        prob_part.astype(jnp.bfloat16), "expert", scatter_dimension=0, tiled=True
    ).astype(jnp.float32)
    grad_gate, grad_up, grad_down = (
        lax.psum_scatter(
            to_half(sum_gate).astype(jnp.bfloat16), "dp", scatter_dimension=1, tiled=True
        ).astype(jnp.float32),
        lax.psum_scatter(
            to_half(sum_up).astype(jnp.bfloat16), "dp", scatter_dimension=1, tiled=True
        ).astype(jnp.float32),
        lax.psum_scatter(
            to_half(sum_down).astype(jnp.bfloat16), "dp", scatter_dimension=1, tiled=True
        ).astype(jnp.float32),
    )
    return (
        grad_act,
        grad_prob,
        grad_gate.astype(jnp.bfloat16),
        grad_up.astype(jnp.bfloat16),
        grad_down.astype(jnp.bfloat16),
    )


def solution(mesh):
    placed = (
        P(("dp", "expert"), None),
        P(("dp", "expert"), None),
        P(("dp", "expert"), None),
        P("dp", None),
        P("expert", None, None),
        P("expert", None, None),
        P("expert", None, None),
    )
    return jax.shard_map(
        on_device,
        mesh=mesh,
        in_specs=placed,
        out_specs=(
            P(("dp", "expert"), None),
            P(("dp", "expert"), None),
            P("expert", "dp", None),
            P("expert", "dp", None),
            P("expert", "dp", None),
        ),
        check_vma=False,
    )
```

profile of v0, /device:TPU:6, one launch (start us, length us, event | category | flops | bytes accessed | tf_op | source)
XLA Modules:
  0.0 503.0 jit_solution(7020023627586829958)
XLA Ops:
  7.2 0.7 all-gather.5.cloned.1.call-update
  8.0 0.7 all-gather.3.cloned.1.call-update
  8.8 1.0 fusion.11
  10.1 24.8 %all_gather.9 = bf16[2048,8]{0,1:T(8,128)(2,1)S(1)} all-gather(bf16[128,8]{0,1:T(8,128)(2,1)} %param.9), channel_id=1, replica_groups=mesh['dp'=8,'expert'=16] {'expert'}, dimensions={0}, use_global_device_ids=true | all-gather | bytes 34816 | tf_op jit(solution)/shard_map/all_gather | solution.py:74
  35.4 23.5 %subtract_select_fusion = s32[16,128,2]{2,0,1:T(8,128)S(1)} fusion(s32[16,128,2]{2,0,1:T(8,128)S(1)} %copy.48), kind=kOutput, calls=%fused_computation.21 | output fusion | flops 532480 | bytes 32768 | tf_op jit(solution)/shard_map/jit(cumsum)/reduce_window_sum | solution.py:17
  59.4 0.6 select_reduce_fusion
  60.5 22.9 %all-gather.5.cloned.1.call-done = bf16[2048,2048]{1,0:T(8,128)(2,1)} async-done(((bf16[128,2048]{1,0:T(8,128)(2,1)}), bf16[2048,2048]{1,0:T(8,128)(2,1)}) %all-gather.5.cloned.1.call-update) | async-done | bytes 8388624 | tf_op jit(solution)/shard_map/all_gather | solution.py:72
  83.5 17.2 %gather_fusion.2 = bf16[1536,2048]{1,0:T(8,128)(2,1)} fusion(bf16[2048,2048]{1,0:T(8,128)(2,1)} %all-gather.5.cloned.1.call-done, s32[2048]{0:T(1024)S(1)} %pad_clamp_fusion), kind=kCustom, calls=%fused_computation.2 | custom fusion | bytes 12589056 | tf_op jit(solution)/shard_map/gather | solution.py:85
  100.6 7.0 %fusion.18 = f32[2,768,512]{2,1,0:T(8,128)S(1)} fusion(bf16[2,768,2048]{2,1,0:T(8,128)(2,1)} %bitcast.38, bf16[2,2048,512]{2,1,0:T(8,128)(2,1)} %param.11), kind=kOutput, calls=%fused_computation.49 | convolution fusion | flops 3221225472 | bytes 13631488 | tf_op jit(solution)/shard_map/ecd,edf->ecf/dot_general | solution.py:40
  107.7 1.7 copy-done.7
  109.4 5.3 %multiply_convert_fusion = (bf16[2,768,512]{2,1,0:T(8,128)(2,1)S(1)}, f32[2,768,512]{2,1,0:T(8,128)}) fusion(f32[2,768,512]{2,1,0:T(8,128)S(1)} %fusion.18, bf16[2,768,2048]{2,1,0:T(8,128)(2,1)S(1)} %bitcast.40, bf16[2,2048,512]{2,1,0:T(8,128)(2,1)S(1)} %copy-done.1), kind=kOutput, calls=%fused_computation.17 | convolution fusion | flops 3225944064 | bytes 18350080 | tf_op jit(solution)/shard_map/ecd,edf->ecf/dot_general | solution.py:41
  114.7 41.4 %all-gather.3.cloned.1.call-done = bf16[2048,2048]{1,0:T(8,128)(2,1)} async-done(((bf16[128,2048]{1,0:T(8,128)(2,1)}), bf16[2048,2048]{1,0:T(8,128)(2,1)}) %all-gather.3.cloned.1.call-update) | async-done | bytes 8388624 | tf_op jit(solution)/shard_map/all_gather | solution.py:73
  156.1 17.1 %gather_fusion.1 = bf16[1536,2048]{1,0:T(8,128)(2,1)} fusion(bf16[2048,2048]{1,0:T(8,128)(2,1)} %all-gather.3.cloned.1.call-done, s32[2048]{0:T(1024)S(1)} %pad_clamp_fusion), kind=kCustom, calls=%fused_computation.1 | custom fusion | bytes 12589056 | tf_op jit(solution)/shard_map/gather | solution.py:86
  173.2 16.5 %fusion.1 = f32[2,768]{1,0:T(2,128)S(1)} fusion(bf16[2,768,2048]{2,1,0:T(8,128)(2,1)} %bitcast.44, bf16[2,768,512]{2,1,0:T(8,128)(2,1)S(1)} %get-tuple-element.13, bf16[2,512,2048]{2,1,0:T(8,128)(2,1)} %param.13), kind=kOutput, calls=%fused_computation.8 | convolution fusion | flops 3230661120 | bytes 12064768 | tf_op jit(solution)/shard_map/ecf,efd->ecd/dot_general | solution.py:44
  189.8 11.2 %scatter_custom_fusion.1 = f32[4096]{0:T(1024)S(1)} fusion(s32[1536]{0:T(1024)S(1)} %reshape.177, f32[1536]{0:T(1024)S(1)} %reshape.179, f32[]{:T(128)} %constant.8.clone.1), kind=kCustom, calls=%fused_computation.38 | custom fusion | flops 1536 | bytes 16388
  201.1 13.4 %gather_fusion = f32[1536]{0:T(1024)S(1)} fusion(f32[2048,2]{0,1:T(2,128)S(1)} %get-tuple-element.6, s32[1536]{0:T(1024)S(1)} %reshape.147), kind=kCustom, calls=%fused_computation | custom fusion | bytes 24576 | tf_op jit(solution)/shard_map/gather | solution.py:84
  214.5 1.0 copy.65
  215.6 8.1 %fusion.8 = bf16[2,512,2048]{2,1,0:T(8,128)(2,1)} fusion(bf16[2,768,512]{2,1,0:T(8,128)(2,1)S(1)} %get-tuple-element.13, bf16[2,768,2048]{2,1,0:T(8,128)(2,1)} %bitcast.45, f32[2,768]{1,0:T(2,128)S(1)} %broadcast_select_fusion.2), kind=kOutput, calls=%fused_computation.14 | convolution fusion | flops 3232759808 | bytes 12064768 | tf_op jit(solution)/shard_map/ecf,ecd->efd/dot_general | solution.py:52
  223.8 11.6 %multiply_convert_fusion.1 = (bf16[2,768,512]{2,1,0:T(8,128)(2,1)S(1)}, bf16[2,768,512]{2,1,0:T(8,128)(2,1)}) fusion(f32[2,768,512]{2,1,0:T(8,128)} %copy-done.7, f32[2,768,512]{2,1,0:T(8,128)} %get-tuple-element.14, bf16[2,512,2048]{2,1,0:T(8,128)(2,1)} %param.13, bf16[2,768,2048]{2,1,0:T(8,128)(2,1)} %bitcast.46, f32[2,768]{1,0:T(2,128)S(1)} %broadcast_select_fusion.2), kind=kOutput, calls=%fused_computation.18 | convolution fusion | flops 3240886272 | bytes 19929088 | tf_op jit(solution)/shard_map/ecd,efd->ecf/dot_general | solution.py:47
  235.4 1.2 copy-done.3
  236.5 5.1 %convolution_convert_fusion = bf16[2,2048,512]{2,1,0:T(8,128)(2,1)} fusion(bf16[2,768,2048]{2,1,0:T(8,128)(2,1)S(1)} %bitcast.43, bf16[2,768,512]{2,1,0:T(8,128)(2,1)S(1)} %get-tuple-element.9), kind=kOutput, calls=%fused_computation.15 | convolution fusion | flops 3223322624 | bytes 12058624 | tf_op jit(solution)/shard_map/ecd,ecf->edf/dot_general | solution.py:54
  241.7 1.3 copy-done.2
  243.0 9.3 %convolution_convert_fusion.1 = bf16[2,2048,512]{2,1,0:T(8,128)(2,1)} fusion(bf16[2,768,2048]{2,1,0:T(8,128)(2,1)} %bitcast.39, bf16[2,768,512]{2,1,0:T(8,128)(2,1)S(1)} %copy-done.2), kind=kOutput, calls=%fused_computation.16 | convolution fusion | flops 3223322624 | bytes 12058624 | tf_op jit(solution)/shard_map/ecd,ecf->edf/dot_general | solution.py:53
  252.5 5.5 %fusion.19 = f32[2,768,2048]{2,1,0:T(8,128)S(1)} fusion(bf16[2,768,512]{2,1,0:T(8,128)(2,1)S(1)} %copy-done.2, bf16[2,2048,512]{2,1,0:T(8,128)(2,1)} %param.11), kind=kOutput, calls=%fused_computation.50 | convolution fusion | flops 3221225472 | bytes 18350080 | tf_op jit(solution)/shard_map/ecf,edf->ecd/dot_general | solution.py:55
  258.0 10.7 %convolution_add_fusion = f32[2,768,2048]{2,1,0:T(8,128)} fusion(f32[2,768,2048]{2,1,0:T(8,128)S(1)} %fusion.19, bf16[2,768,512]{2,1,0:T(8,128)(2,1)} %copy-done.3, bf16[2,2048,512]{2,1,0:T(8,128)(2,1)} %param.12), kind=kOutput, calls=%fused_computation.13 | convolution fusion | flops 3224371200 | bytes 30932992 | tf_op jit(solution)/shard_map/ecf,edf->ecd/dot_general | solution.py:56
  268.7 27.6 %scatter_custom_fusion = f32[2048,2048]{1,0:T(8,128)} fusion(s32[1536]{0:T(1024)S(1)} %fusion.16, f32[1536,2048]{1,0:T(8,128)} %bitcast.37, f32[]{:T(128)} %constant.8.clone.1), kind=kCustom, calls=%fused_computation.9 | custom fusion | flops 3145728 | bytes 16777728 | tf_op jit(solution)/shard_map/scatter-add | solution.py:93
  296.3 10.5 %convert_element_type.60 = bf16[2048,2048]{1,0:T(8,128)(2,1)} convert(f32[2048,2048]{1,0:T(8,128)} %scatter_custom_fusion) | non-fusion elementwise | flops 4194304 | bytes 25165824 | tf_op jit(solution)/shard_map/convert_element_type | solution.py:10
  306.9 0.8 copy.66
  308.4 16.0 %reduce-scatter.14.cloned.1.call-done = bf16[2,64,2048]{2,1,0:T(8,128)(2,1)} async-done(((bf16[2,512,2048]{2,1,0:T(8,128)(2,1)}), bf16[2,64,2048]{2,1,0:T(8,128)(2,1)}) %reduce-scatter.14.cloned.1.call-update) | async-done | bytes 524304 | tf_op jit(solution)/shard_map/reduce_scatter | solution.py:117
  324.3 39.8 %reduce-scatter.12.cloned.1.call-done = bf16[2,256,512]{2,1,0:T(8,128)(2,1)} async-done(((bf16[2,2048,512]{2,1,0:T(8,128)(2,1)}), bf16[2,256,512]{2,1,0:T(8,128)(2,1)}) %reduce-scatter.12.cloned.1.call-update) | async-done | bytes 524304 | tf_op jit(solution)/shard_map/reduce_scatter | solution.py:114
  364.1 39.7 %reduce-scatter.10.cloned.1.call-done = bf16[2,256,512]{2,1,0:T(8,128)(2,1)} async-done(((bf16[2,2048,512]{2,1,0:T(8,128)(2,1)}), bf16[2,256,512]{2,1,0:T(8,128)(2,1)}) %reduce-scatter.10.cloned.1.call-update) | async-done | bytes 524304 | tf_op jit(solution)/shard_map/reduce_scatter | solution.py:111
  403.8 91.9 %reduce-scatter.8.cloned.1.call-done = bf16[128,2048]{1,0:T(8,128)(2,1)} async-done(((bf16[2048,2048]{1,0:T(8,128)(2,1)}), bf16[128,2048]{1,0:T(8,128)(2,1)}) %reduce-scatter.8.cloned.1.call-update) | async-done | bytes 524304 | tf_op jit(solution)/shard_map/reduce_scatter | solution.py:104
  (63 shorter events, 3.1 us)
Async XLA Ops:
  7.2 53.1 %copy-start.6 = (s32[2]{0:T(128)S(1)}, s32[2]{0:T(128)}, u32[]{:S(2)}) copy-start(s32[2]{0:T(128)} %constant.7) | copy-start | bytes 28
  7.2 53.2 %copy-start.5 = (s32[2]{0:T(128)S(1)}, s32[2]{0:T(128)}, u32[]{:S(2)}) copy-start(s32[2]{0:T(128)} %constant.35) | copy-start | bytes 28
  7.2 76.3 %all-gather.5.cloned.1.call-start = ((), (), s32[]{:S(2)}) async-start(), calls=%async_computation.6 | async-start | bytes 8912896 | tf_op jit(solution)/shard_map/all_gather | solution.py:72
  7.9 148.2 %all-gather.3.cloned.1.call-start = ((), (), s32[]{:S(2)}) async-start(), calls=%async_computation.5 | async-start | bytes 8912896 | tf_op jit(solution)/shard_map/all_gather | solution.py:73
  8.7 298.2 %reduce-scatter.16.cloned.1.call-start = ((), (), s32[]{:S(2)}) async-start(), calls=%async_computation.11 | async-start | bytes 557056
  100.6 8.7 %copy-start = (bf16[1536,2048]{1,0:T(8,128)(2,1)S(1)}, bf16[1536,2048]{1,0:T(8,128)(2,1)}, u32[]{:S(2)}) copy-start(bf16[1536,2048]{1,0:T(8,128)(2,1)} %gather_fusion.2) | copy-start | bytes 18874372
  100.6 8.8 %copy-start.1 = (bf16[2,2048,512]{2,1,0:T(8,128)(2,1)S(1)}, bf16[2,2048,512]{2,1,0:T(8,128)(2,1)}, u32[]{:S(2)}) copy-start(bf16[2,2048,512]{2,1,0:T(8,128)(2,1)} %param.12) | copy-start | bytes 12582916
  107.7 1.7 copy-start.7
  173.2 27.7 %copy-start.4 = (s32[2048,8]{0,1:T(8,128)S(1)}, s32[2048,8]{0,1:T(8,128)}, u32[]{:S(2)}) copy-start(s32[2048,8]{0,1:T(8,128)} %param.10) | copy-start | bytes 196612
  215.5 108.8 %reduce-scatter.14.cloned.1.call-start = ((), (), s32[]{:S(2)}) async-start(), calls=%async_computation.10 | async-start | bytes 4718592 | tf_op jit(solution)/shard_map/reduce_scatter | solution.py:117
  223.7 12.8 %slice-start = ((s8[6291456]{0:T(1024)(128)(4,1)}), s8[2097152]{0:T(1024)(128)(4,1)S(1)}, s32[]{:S(2)}) async-start(s8[6291456]{0:T(1024)(128)(4,1)} %bitcast.41), calls=%async_computation.12 | async-start | bytes 4194304
  223.7 140.4 %reduce-scatter.12.cloned.1.call-start = ((), (), s32[]{:S(2)}) async-start(), calls=%async_computation.9 | async-start | bytes 4718592 | tf_op jit(solution)/shard_map/reduce_scatter | solution.py:114
  223.8 12.8 %slice-start.1 = ((s8[6291456]{0:T(1024)(128)(4,1)}), s8[4194304]{0:T(1024)(128)(4,1)S(1)}, s32[]{:S(2)}) async-start(s8[6291456]{0:T(1024)(128)(4,1)} %bitcast.41), calls=%async_computation.13 | async-start | bytes 8388608
  235.4 1.2 copy-start.3
  241.6 1.4 copy-start.2
  241.6 162.2 %reduce-scatter.10.cloned.1.call-start = ((), (), s32[]{:S(2)}) async-start(), calls=%async_computation.8 | async-start | bytes 4718592 | tf_op jit(solution)/shard_map/reduce_scatter | solution.py:111
  252.4 243.4 %reduce-scatter.8.cloned.1.call-start = ((), (), s32[]{:S(2)}) async-start(), calls=%async_computation.7 | async-start | bytes 8912896 | tf_op jit(solution)/shard_map/reduce_scatter | solution.py:104
Sparse Core Ops, SparseCore 0:
  10.2 73.2 all-gather.4
  85.6 70.4 all-gather.2
  215.6 72.0 reduce-scatter.15
  290.7 33.5 reduce-scatter.13
  327.3 36.8 reduce-scatter.11
  367.1 36.6 reduce-scatter.9
  408.2 87.5 reduce-scatter.7
where the time goes:
time: 512 us; the launch traced here: 503 us
  waiting for transfers between devices  253 us (49%)
  matrix products  79.1 us (15%)
  other arithmetic  75.6 us (15%)
  local copies, waits for them, and re-layouts  55.2 us (11%)
  blocking collectives  24.8 us (5%)
  between operations  14.8 us (3%)
    reduce_scatter x1, waiting for transfers between devices, on_device(): lax.psum_scatter(to_half(act_part).astype(jnp.bfloat16), 'expert', scatte...  91.9 us
    all_gather x1, waiting for transfers between devices, on_device(): lax.all_gather(out_grad, 'expert', axis=0, tiled=True)  41.4 us
    reduce_scatter x1, waiting for transfers between devices, on_device(): lax.psum_scatter(to_half(sum_up).astype(jnp.bfloat16), 'dp', scatter_dime...  39.8 us
    reduce_scatter x1, waiting for transfers between devices, on_device(): lax.psum_scatter(to_half(sum_gate).astype(jnp.bfloat16), 'dp', scatter_di...  39.7 us
    scatter-add x1, other arithmetic, on_device(): act_part = jnp.zeros((group_rows, model_width), jnp.float32).at[slot_toke...  27.6 us
    all_gather x1, blocking collectives, on_device(): lax.all_gather(gate_probs, 'expert', axis=0, tiled=True)  24.8 us
    another operation x1, other arithmetic, slot_table(): slot_rank = jnp.cumsum(hit_count, axis=1) - hit_count  23.5 us
    all_gather x1, waiting for transfers between devices, on_device(): lax.all_gather(activations, 'expert', axis=0, tiled=True)  22.9 us
  transfers between devices with their start and end apart: 7, of which 6 were waited for; matrix products, arithmetic and copies ran while one was open for 29% of the time, Pallas kernels for 0%

commit v1 on v0

v1 whole, which is shorter than its diff:
```python
import functools

import jax
import jax.numpy as jnp
from jax import lax
from jax.experimental import pallas as pl
from jax.experimental.pallas import tpu as pltpu
from jax.sharding import PartitionSpec as P

TOP = 8
SRC = 128
CHUNK = 4
PEER = 48
LANES = 128
F32 = jnp.float32
BF16 = jnp.bfloat16

NT = (((1,), (1,)), ((), ()))
TN = (((0,), (0,)), ((), ()))


def dot(a, b, dims=(((1,), (0,)), ((), ()))):
    return lax.dot_general(a, b, dims, preferred_element_type=F32)


def expert_kernel(tgt, rel, dy, x, pr, wg, wu, wd, xs, gs, pa, dh, du, act, dxs, qs, ps):
    pairs = CHUNK // 2
    half = 2 * PEER

    def hot(pair):
        places = lax.broadcasted_iota(jnp.int32, (half, 2 * SRC), 0)
        return jnp.concatenate(
            [(places == tgt[0, e * pairs + pair, :][None, :]).astype(F32).astype(BF16) for e in range(2)], axis=0
        )

    for pair in range(pairs):
        rows = pl.ds(pair * 2 * SRC, 2 * SRC)
        spots = pl.ds(pair * half, half)
        pick = hot(pair)
        got_x = dot(pick, x[rows, :]).astype(BF16)
        got_g = dot(pick, dy[rows, :]).astype(BF16)
        local = rel[rows, :].astype(F32)
        probs = pr[rows, :].astype(F32)
        for e in range(2):
            part = slice(e * half, (e + 1) * half)
            xs[e, spots, :] = got_x[part]
            gs[e, spots, :] = got_g[part]
            mine = jnp.where(local == e, probs, 0.0).astype(BF16)
            col = jnp.sum(dot(pick[part], mine), axis=1, keepdims=True)
            ps[e, spots, :] = jnp.broadcast_to(col, (half, LANES))
    for e in range(2):
        h = dot(xs[e], wg[e])
        u = dot(xs[e], wu[e])
        dap = dot(gs[e], wd[e], NT)
        p = ps[e][:, :1]
        s = 1.0 / (1.0 + jnp.exp(-h))
        hs = h * s
        a = hs * u
        q = jnp.sum(a.astype(BF16).astype(F32) * dap, axis=1, keepdims=True)
        da = p * dap
        pa[e] = (p * a).astype(BF16)
        dh[e] = (da * u * s * (1.0 + h * (1.0 - s))).astype(BF16)
        du[e] = (da * hs).astype(BF16)
        dx = (dot(dh[e], wg[e], NT) + dot(du[e], wu[e], NT)).astype(BF16)
        wide = jnp.broadcast_to(q, (CHUNK * PEER, LANES)).astype(BF16)
        for pair in range(pairs):
            part = slice(pair * half, (pair + 1) * half)
            dxs[pair, pl.ds(e * half, half), :] = dx[part]
            qs[pair, pl.ds(e * half, half), :] = wide[part]
    for pair in range(pairs):
        rows = pl.ds(pair * 2 * SRC, 2 * SRC)
        pick = hot(pair)
        width = x.shape[1]
        act[rows, pl.ds(0, width)] = dot(pick, dxs[pair], TN).astype(BF16)
        local = rel[rows, :].astype(F32)
        ext = jnp.zeros(local.shape, F32)
        for e in range(2):
            part = slice(e * half, (e + 1) * half)
            ext = ext + jnp.where(local == e, dot(pick[part], qs[pair, pl.ds(e * half, half), :], TN), 0.0)
        act[rows, pl.ds(width, LANES)] = ext.astype(BF16)


def expert_pass(tgt, rel, whole, wg, wu, wd):
    rows, width = whole.shape[0], wg.shape[1]
    ff = wg.shape[2]
    n = rows // (SRC * CHUNK)
    span = CHUNK * SRC
    slots = CHUNK * PEER
    once = pl.Buffered(1)
    full = lambda shape: pl.BlockSpec(shape, lambda i: (0,) * len(shape), pipeline_mode=once)
    slot_spec = lambda w: pl.BlockSpec((2, slots, w), lambda i: (0, i, 0))
    slot_out = lambda w: jax.ShapeDtypeStruct((2, n * slots, w), BF16)
    return pl.pallas_call(
        expert_kernel,
        grid=(n,),
        in_specs=[
            pl.BlockSpec((1, CHUNK, 2 * SRC), lambda i: (i, 0, 0)),
            pl.BlockSpec((span, LANES), lambda i: (i, 0)),
            pl.BlockSpec((span, width), lambda i: (i, 0)),
            pl.BlockSpec((span, width), lambda i: (i, 1)),
            pl.BlockSpec((span, LANES), lambda i: (i, 2 * width // LANES)),
            full(wg.shape),
            full(wu.shape),
            full(wd.shape),
        ],
        out_specs=[
            slot_spec(width),
            slot_spec(width),
            slot_spec(ff),
            slot_spec(ff),
            slot_spec(ff),
            pl.BlockSpec((span, width + LANES), lambda i: (i, 0)),
        ],
        out_shape=[
            slot_out(width),
            slot_out(width),
            slot_out(ff),
            slot_out(ff),
            slot_out(ff),
            jax.ShapeDtypeStruct((rows, width + LANES), BF16),
        ],
        scratch_shapes=[
            pltpu.VMEM((CHUNK // 2, 4 * PEER, width), BF16),
            pltpu.VMEM((CHUNK // 2, 4 * PEER, LANES), BF16),
            pltpu.VMEM((2, slots, LANES), F32),
        ],
        compiler_params=pltpu.CompilerParams(vmem_limit_bytes=58 << 20),
        cost_estimate=pl.CostEstimate(flops=24 << 30, bytes_accessed=60 << 20, transcendentals=1 << 20),
        name="experts",
    )(tgt, rel, whole, whole, whole, wg, wu, wd)


def place_chunks(where, total, outs, step):
    my_x, my_c = where[0], where[1]
    for ahead in range(4):
        for own in range(2):
            core = my_c if own else 1 - my_c
            piece = lax.rem(my_x + ahead, 4) * 2 + core
            start = pl.multiple_of(piece * step, step)
            outs[own][ahead, 0] = total[pl.ds(start, step), :].astype(BF16)


def down_kernel(where, pa, gs, other, own, total):
    total[...] = dot(pa[0], gs[0], TN)
    place_chunks(where, total, (other, own), total.shape[0] // 8)


def up_kernel(where, xs, dh, du, other, own, total):
    ff = dh.shape[2]
    total[:, pl.ds(0, ff)] = dot(xs[0], dh[0], TN)
    total[:, pl.ds(ff, ff)] = dot(xs[0], du[0], TN)
    place_chunks(where, total, (other, own), total.shape[0] // 8)


def weight_pass(body, where, args, rows, cols, name):
    slots = args[0].shape[1]
    step = rows // 8
    out = jax.ShapeDtypeStruct((4, 2, step, cols), BF16)
    out_spec = pl.BlockSpec((4, 1, step, cols), lambda e: (0, e, 0, 0))
    return pl.pallas_call(
        body,
        grid=(2,),
        in_specs=[pl.BlockSpec(memory_space=pltpu.SMEM)]
        + [pl.BlockSpec((1, slots, a.shape[2]), lambda e: (e, 0, 0)) for a in args],
        out_specs=[out_spec, out_spec],
        out_shape=[out, out],
        scratch_shapes=[pltpu.VMEM((rows, cols), F32)],
        compiler_params=pltpu.CompilerParams(vmem_limit_bytes=58 << 20),
        cost_estimate=pl.CostEstimate(flops=4 * slots * rows * cols, bytes_accessed=16 << 20, transcendentals=0),
        name=name,
    )(where, *args)


def over_dp(other, own):
    swap = [(x * 2 + c, x * 2 + 1 - c) for x in range(4) for c in range(2)]
    right = [(x * 2 + c, (x + 1) % 4 * 2 + c) for x in range(4) for c in range(2)]
    left = [(x * 2 + c, (x + 3) % 4 * 2 + c) for x in range(4) for c in range(2)]
    got = lax.ppermute(other, "dp", swap)
    both = lambda i, e: own[i, e].astype(F32) + got[i, e].astype(F32)
    far_r = lax.ppermute(both(2, 0).astype(BF16), "dp", right)
    far_l = lax.ppermute(both(2, 1).astype(BF16), "dp", left)
    near_r = jnp.stack([both(1, 0) + far_r.astype(F32), both(1, 1)]).astype(BF16)
    near_l = jnp.stack([both(3, 0), both(3, 1) + far_l.astype(F32)]).astype(BF16)
    near_r = lax.ppermute(near_r, "dp", right)
    near_l = lax.ppermute(near_l, "dp", left)
    return own[0].astype(F32) + got[0].astype(F32) + near_r.astype(F32) + near_l.astype(F32)


def tables(ids, first):
    rows = ids.shape[0]
    mine = first + jnp.arange(2, dtype=jnp.int32)
    hit = jnp.any(ids[None] == mine[:, None, None], axis=2)
    hit = hit.reshape(2, rows // SRC, SRC)
    before = jnp.triu(jnp.ones((SRC, SRC), BF16), 1)
    rank = jnp.einsum("ebr,rs->ebs", hit.astype(BF16), before, preferred_element_type=F32).astype(jnp.int32)
    second = (jnp.arange(rows // SRC, dtype=jnp.int32) % 2 * PEER)[None, :, None]
    tgt = jnp.where(hit, rank + second, -1)
    tgt = tgt.reshape(2, rows // (SRC * CHUNK), CHUNK // 2, 2 * SRC)
    tgt = jnp.transpose(tgt, (1, 0, 2, 3)).reshape(rows // (SRC * CHUNK), CHUNK, 2 * SRC)
    rel = jnp.pad(ids - first, ((0, 0), (0, LANES - TOP)), constant_values=-1).astype(BF16)
    return tgt, rel


def on_device(activations, out_grad, gate_probs, expert_ids, w_gate, w_up, w_down):
    my_index = lax.axis_index("expert")
    dp_index = lax.axis_index("dp")
    width = activations.shape[1]
    ff = w_gate.shape[2]
    payload = jnp.concatenate(
        [out_grad, activations, jnp.pad(gate_probs, ((0, 0), (0, LANES - TOP)))], axis=1
    )
    whole = lax.all_gather(payload, "expert", axis=0, tiled=True)
    tgt, rel = tables(expert_ids, my_index * 2)
    xs, gs, pa, dh, du, act = expert_pass(tgt, rel, whole, w_gate, w_up, w_down)
    act_sum = lax.psum_scatter(act, "expert", scatter_dimension=0, tiled=True)
    where = jnp.stack([dp_index // 2, dp_index % 2]).astype(jnp.int32)
    down = weight_pass(down_kernel, where, (pa, gs), ff, width, "down_grad")
    up = weight_pass(up_kernel, where, (xs, dh, du), width, 2 * ff, "up_grad")
    grad_down = over_dp(*down)
    grad_both = over_dp(*up)
    return (
        act_sum[:, :width],
        act_sum[:, width : width + TOP].astype(F32),
        grad_both[:, :, :ff].astype(BF16),
        grad_both[:, :, ff:].astype(BF16),
        grad_down.astype(BF16),
    )


def solution(mesh):
    placed = (
        P(("dp", "expert"), None),
        P(("dp", "expert"), None),
        P(("dp", "expert"), None),
        P("dp", None),
        P("expert", None, None),
        P("expert", None, None),
        P("expert", None, None),
    )
    return jax.shard_map(
        on_device,
        mesh=mesh,
        in_specs=placed,
        out_specs=(
            P(("dp", "expert"), None),
            P(("dp", "expert"), None),
            P("expert", "dp", None),
            P("expert", "dp", None),
            P("expert", "dp", None),
        ),
        check_vma=False,
    )
```

time: 512 us -> 271 us (0.53); the launches traced: 503 us -> 268 us
  waiting for transfers between devices: 253 us -> 164 us
  matrix products: 79.1 us -> 0.08 us
  other arithmetic: 75.6 us -> 13.7 us
  Pallas kernels: 0 us -> 60.4 us
  local copies, waits for them, and re-layouts: 55.2 us -> 6.29 us
  blocking collectives: 24.8 us -> 0 us
  starting transfers between devices: 0.28 us -> 9.41 us
    reduce_scatter x4 -> x1, waiting for transfers between devices: 187 us -> 0.01 us  [on_device(): act_sum = lax.psum_scatter(act, 'expert', scatter_dimension=0, tiled=True)]
    dot_general x9 -> x1, matrix products: 79.1 us -> 0.08 us  [tables(): jnp.einsum('ebr,rs->ebs', hit.astype(BF16), before, preferred_element_typ...]
    pallas_call x0 -> x3, Pallas kernels: none -> 60.4 us  [the longest x1 40.5 us: expert_pass(): pl.pallas_call(expert_kernel, grid=(n,), in_specs=[pl.BlockSpec((1, CHUNK...]
    all_gather x2 -> x1, waiting for transfers between devices: 64.4 us -> 114 us  [on_device(): whole = lax.all_gather(payload, 'expert', axis=0, tiled=True)]
    ppermute x0 -> x10, waiting for transfers between devices: none -> 49.3 us  [the longest x2 25.3 us: over_dp(): near_r = lax.ppermute(near_r, 'dp', right)]
    gather x4 -> x0, local copies, waits for them, and re-layouts: 47.7 us -> none  [the longest x1 17.2 us: on_device(): rows_x = whole_x[slot_token]]
    scatter-add x1 -> x0, other arithmetic: 27.6 us -> none  [on_device(): act_part = jnp.zeros((group_rows, model_width), jnp.float32).at[slot_toke...]
    all_gather x1 -> x0, blocking collectives: 24.8 us -> none  [on_device(): lax.all_gather(gate_probs, 'expert', axis=0, tiled=True)]
  transfers between devices with their start and end apart: 7 -> 12, of which waited for: 6 -> 8; matrix products, arithmetic and copies ran while one was open for 29% -> 5% of each run, Pallas kernels for 0% -> 7%
where the time goes in v1:
time: 271 us; the launch traced here: 268 us
  waiting for transfers between devices  164 us (61%)
  Pallas kernels  60.4 us (22%)
  between operations  14.2 us (5%)
  other arithmetic  13.7 us (5%)
  starting transfers between devices  9.41 us (3%)
  local copies, waits for them, and re-layouts  6.29 us (2%)
    all_gather x1, waiting for transfers between devices, on_device(): whole = lax.all_gather(payload, 'expert', axis=0, tiled=True)  114 us
    pallas_call x1, Pallas kernels, expert_pass(): pl.pallas_call(expert_kernel, grid=(n,), in_specs=[pl.BlockSpec((1, CHUNK...  40.5 us
    ppermute x2, waiting for transfers between devices, over_dp(): near_r = lax.ppermute(near_r, 'dp', right)  25.3 us
    pallas_call x2, Pallas kernels, weight_pass(): pl.pallas_call(body, grid=(2,), in_specs=[pl.BlockSpec(memory_space=pltpu...  19.9 us
    ppermute x2, waiting for transfers between devices, over_dp(): far_r = lax.ppermute(both(2, 0).astype(BF16), 'dp', right)  10.5 us
    ppermute x2, waiting for transfers between devices, over_dp(): near_l = lax.ppermute(near_l, 'dp', left)  5.64 us
  transfers between devices with their start and end apart: 12, of which 8 were waited for; matrix products, arithmetic and copies ran while one was open for 5% of the time, Pallas kernels for 7%

profile of v1, /device:TPU:6, one launch (start us, length us, event | category | flops | bytes accessed | tf_op | source)
XLA Modules:
  0.0 267.8 jit_solution(8478341537127938979)
XLA Ops:
  7.2 0.8 copy.25
  8.0 2.3 fusion.5
  10.7 0.6 reshape.178.tgt
  11.6 0.9 pad.9.rel
  12.5 114.4 %all-gather.2.cloned.1.call-done.dy.x.pr = bf16[2048,4224]{1,0:T(8,128)(2,1)} async-done(((bf16[128,4224]{1,0:T(8,128)(2,1)}), bf16[2048,4224]{1,0:T(8,128)(2,1)}) %all-gather.2.cloned.1.call-update) | async-done | bytes 17301520 | tf_op jit(solution)/shard_map/all_gather | solution.py:212
  127.0 40.5 %experts.1 = (bf16[2,768,2048]{2,1,0:T(8,128)(2,1)}, bf16[2,768,2048]{2,1,0:T(8,128)(2,1)}, bf16[2,768,512]{2,1,0:T(8,128)(2,1)}, bf16[2,768,512]{2,1,0:T(8,128)...) custom-call(s32[4,4,256]{2,1,0:T(4,128)} %reshape.178.tgt, bf16[2048,128]{1,0:T(8,128)(2,1)} %pad.9.rel, ...), custom_call_target="tpu_custom_call" | custom-call | flops 25769803776 | bytes 62914560 | tf_op jit(solution)/shard_map/experts/pallas_call | solution.py:93
  167.5 0.6 pad_add_fusion.where
  168.1 12.1 %up_grad.1 = (bf16[4,2,256,1024]{3,2,1,0:T(8,128)(2,1)}, bf16[4,2,256,1024]{3,2,1,0:T(8,128)(2,1)}) custom-call(s32[2]{0:T(128)} %pad_add_fusion.where, bf16[2,768,2048]{2,1,0:T(8,128)(2,1)} %get-tuple-element.16.xs, bf16[2,768,512]{2,1,0:T(8,128)(2,1)} %get-tuple-element.17.dh, bf16[2,768,512]{2,1,0:T(8,128)(2,1)} %get-tuple-element.18.du), custom_call_target="tpu_custom_call" | custom-call | flops 6442450944 | bytes 16777216 | tf_op jit(solution)/shard_map/up_grad/pallas_call | solution.py:160
  180.2 7.8 %down_grad.1 = (bf16[4,2,64,2048]{3,2,1,0:T(8,128)(2,1)}, bf16[4,2,64,2048]{3,2,1,0:T(8,128)(2,1)}) custom-call(s32[2]{0:T(128)} %pad_add_fusion.where, bf16[2,768,512]{2,1,0:T(8,128)(2,1)} %get-tuple-element.21.pa, bf16[2,768,2048]{2,1,0:T(8,128)(2,1)} %get-tuple-element.22.gs), custom_call_target="tpu_custom_call" | custom-call | flops 3221225472 | bytes 16777216 | tf_op jit(solution)/shard_map/down_grad/pallas_call | solution.py:160
  188.0 0.6 collective-permute-start.5
  188.5 4.0 %collective-permute-done.5 = bf16[4,2,64,2048]{3,2,1,0:T(8,128)(2,1)S(1)} collective-permute-done((bf16[4,2,64,2048]{3,2,1,0:T(8,128)(2,1)}, bf16[4,2,64,2048]{3,2,1,0:T(8,128)(2,1)S(1)}, u32[]{:S(2)}, u32[]{:S(2)}) %collective-permute-start.5) | collective-permute-done | bytes 2097184 | tf_op jit(solution)/shard_map/ppermute | solution.py:178
  192.5 1.6 fusion.18
  194.1 0.6 collective-permute-start.6
  194.8 1.5 collective-permute-start.8
  196.3 2.7 %fusion.10 = (bf16[256,1024]{1,0:T(8,128)(2,1)S(1)}, bf16[256,1024]{1,0:T(8,128)(2,1)S(1)}, bf16[1,256,1024]{2,1,0:T(8,128)(2,1)S(1)}, bf16[1,256,1024]{2,1,0:T(8,128)(2,1)S(1)}) fusion(bf16[4,2,256,1024]{3,2,1,0:T(8,128)(2,1)} %collective-permute-done, bf16[4,2,256,1024]{3,2,1,0:T(8,128)(2,1)S(1)} %copy-done), kind=kLoop, calls=%fused_computation.22 | loop fusion | flops 4194304 | bytes 6291456 | tf_op jit(solution)/shard_map/convert_element_type | solution.py:180
  198.9 1.8 collective-permute-start.1
  200.8 0.3 collective-permute-start.3
  201.0 2.3 collective-permute-done.6
  203.3 1.0 collective-permute-done.8
  204.7 1.1 collective-permute-start.9
  205.8 8.2 %collective-permute-done.1 = bf16[256,1024]{1,0:T(8,128)(2,1)S(1)} collective-permute-done((bf16[256,1024]{1,0:T(8,128)(2,1)S(1)}, bf16[256,1024]{1,0:T(8,128)(2,1)S(1)}, u32[]{:S(2)}, u32[]{:S(2)}) %collective-permute-start.1) | collective-permute-done | bytes 524320 | tf_op jit(solution)/shard_map/ppermute | solution.py:180
  214.0 2.8 %collective-permute-done.3 = bf16[256,1024]{1,0:T(8,128)(2,1)S(1)} collective-permute-done((bf16[256,1024]{1,0:T(8,128)(2,1)S(1)}, bf16[256,1024]{1,0:T(8,128)(2,1)S(1)}, u32[]{:S(2)}, u32[]{:S(2)}) %collective-permute-start.3) | collective-permute-done | bytes 524320 | tf_op jit(solution)/shard_map/ppermute | solution.py:181
  216.8 1.9 fusion.14
  219.0 3.3 %collective-permute-start.2 = (bf16[2,256,1024]{2,1,0:T(8,128)(2,1)S(1)}, bf16[2,256,1024]{2,1,0:T(8,128)(2,1)S(1)}, u32[]{:S(2)}, u32[]{:S(2)}) collective-permute-start(bf16[2,256,1024]{2,1,0:T(8,128)(2,1)S(1)} %pad_maximum_fusion), channel_id=1, source_target_pairs={{0,32},{16,48},{32,64},{48,80},{64,96},{80,112},{96,0},{112,16},{1... | collective-permute-start | bytes 3145736 | tf_op jit(solution)/shard_map/ppermute | solution.py:184
  222.4 5.6 %collective-permute-done.9 = bf16[2,64,2048]{2,1,0:T(8,128)(2,1)S(1)} collective-permute-done((bf16[2,64,2048]{2,1,0:T(8,128)(2,1)S(1)}, bf16[2,64,2048]{2,1,0:T(8,128)(2,1)S(1)}, u32[]{:S(2)}, u32[]{:S(2)}) %collective-permute-start.9) | collective-permute-done | bytes 524320 | tf_op jit(solution)/shard_map/ppermute | solution.py:185
  228.1 25.3 %collective-permute-done.7 = bf16[2,64,2048]{2,1,0:T(8,128)(2,1)S(1)} collective-permute-done((bf16[2,64,2048]{2,1,0:T(8,128)(2,1)S(1)}, bf16[2,64,2048]{2,1,0:T(8,128)(2,1)S(1)}, u32[]{:S(2)}, u32[]{:S(2)}) %collective-permute-start.7) | collective-permute-done | bytes 524320 | tf_op jit(solution)/shard_map/ppermute | solution.py:184
  253.3 1.1 fusion.7
  254.5 2.1 fusion.2
  256.6 1.1 fusion.34
  257.7 0.8 slice_convert_fusion
  258.4 0.7 copy.26
  259.1 1.9 slice.130
  (30 shorter events, 1.4 us)
Async XLA Ops:
  7.2 3.3 %copy-start.2 = (s32[2048,8]{0,1:T(8,128)S(1)}, s32[2048,8]{0,1:T(8,128)}, u32[]{:S(2)}) copy-start(s32[2048,8]{0,1:T(8,128)} %param.10) | copy-start | bytes 196612
  7.2 119.8 %all-gather.2.cloned.1.call-start = ((), (), s32[]{:S(2)}) async-start(), calls=%async_computation.1 | async-start | bytes 18382848 | tf_op jit(solution)/shard_map/all_gather | solution.py:212
  10.3 247.3 %reduce-scatter.2.cloned.1.call-start = ((), (), s32[]{:S(2)}) async-start(), calls=%async_computation.2 | async-start | bytes 9469952 | tf_op jit(solution)/shard_map/reduce_scatter | solution.py:215
  180.2 16.1 %collective-permute-start = (bf16[4,2,256,1024]{3,2,1,0:T(8,128)(2,1)}, bf16[4,2,256,1024]{3,2,1,0:T(8,128)(2,1)}, u32[]{:S(2)}, u32[]{:S(2)}) collective-permute-start(bf16[4,2,256,1024]{3,2,1,0:T(8,128)(2,1)} %get-tuple-element.20), channel_id=1, source_target_pairs={{0,16},{16,0},{32,48},{48,32},{64,80},{80,64},{96,112},{112,96},{1... | collective-permute-start | bytes 12582920 | tf_op jit(solution)/shard_map/ppermute | solution.py:178
  180.2 16.1 %copy-start = (bf16[4,2,256,1024]{3,2,1,0:T(8,128)(2,1)S(1)}, bf16[4,2,256,1024]{3,2,1,0:T(8,128)(2,1)}, u32[]{:S(2)}) copy-start(bf16[4,2,256,1024]{3,2,1,0:T(8,128)(2,1)} %get-tuple-element.19) | copy-start | bytes 12582916
  188.0 4.5 %collective-permute-start.5 = (bf16[4,2,64,2048]{3,2,1,0:T(8,128)(2,1)}, bf16[4,2,64,2048]{3,2,1,0:T(8,128)(2,1)S(1)}, u32[]{:S(2)}, u32[]{:S(2)}) collective-permute-start(bf16[4,2,64,2048]{3,2,1,0:T(8,128)(2,1)} %get-tuple-element.24), channel_id=1, source_target_pairs={{0,16},{16,0},{32,48},{48,32},{64,80},{80,64},{96,112},{112,96},{1... | collective-permute-start | bytes 6291464 | tf_op jit(solution)/shard_map/ppermute | solution.py:178
  194.1 9.2 %collective-permute-start.6 = (bf16[64,2048]{1,0:T(8,128)(2,1)S(1)}, bf16[64,2048]{1,0:T(8,128)(2,1)S(1)}, u32[]{:S(2)}, u32[]{:S(2)}) collective-permute-start(bf16[64,2048]{1,0:T(8,128)(2,1)S(1)} %get-tuple-element.48), channel_id=1, source_target_pairs={{0,32},{16,48},{32,64},{48,80},{64,96},{80,112},{96,0},{112,16},{1... | collective-permute-start | bytes 786440 | tf_op jit(solution)/shard_map/ppermute | solution.py:180
  194.8 9.6 %collective-permute-start.8 = (bf16[64,2048]{1,0:T(8,128)(2,1)S(1)}, bf16[64,2048]{1,0:T(8,128)(2,1)S(1)}, u32[]{:S(2)}, u32[]{:S(2)}) collective-permute-start(bf16[64,2048]{1,0:T(8,128)(2,1)S(1)} %get-tuple-element.49), channel_id=1, source_target_pairs={{0,96},{16,112},{32,0},{48,16},{64,32},{80,48},{96,64},{112,80},{1... | collective-permute-start | bytes 786440 | tf_op jit(solution)/shard_map/ppermute | solution.py:181
  196.3 8.1 %copy-start.1 = (bf16[4,2,64,2048]{3,2,1,0:T(8,128)(2,1)S(1)}, bf16[4,2,64,2048]{3,2,1,0:T(8,128)(2,1)}, u32[]{:S(2)}) copy-start(bf16[4,2,64,2048]{3,2,1,0:T(8,128)(2,1)} %get-tuple-element.23) | copy-start | bytes 6291460
  198.9 15.1 %collective-permute-start.1 = (bf16[256,1024]{1,0:T(8,128)(2,1)S(1)}, bf16[256,1024]{1,0:T(8,128)(2,1)S(1)}, u32[]{:S(2)}, u32[]{:S(2)}) collective-permute-start(bf16[256,1024]{1,0:T(8,128)(2,1)S(1)} %get-tuple-element.42), channel_id=1, source_target_pairs={{0,32},{16,48},{32,64},{48,80},{64,96},{80,112},{96,0},{112,16},{1... | collective-permute-start | bytes 1572872 | tf_op jit(solution)/shard_map/ppermute | solution.py:180
  200.8 16.1 %collective-permute-start.3 = (bf16[256,1024]{1,0:T(8,128)(2,1)S(1)}, bf16[256,1024]{1,0:T(8,128)(2,1)S(1)}, u32[]{:S(2)}, u32[]{:S(2)}) collective-permute-start(bf16[256,1024]{1,0:T(8,128)(2,1)S(1)} %get-tuple-element.43), channel_id=1, source_target_pairs={{0,96},{16,112},{32,0},{48,16},{64,32},{80,48},{96,64},{112,80},{1... | collective-permute-start | bytes 1572872 | tf_op jit(solution)/shard_map/ppermute | solution.py:181
  204.7 23.4 %collective-permute-start.9 = (bf16[2,64,2048]{2,1,0:T(8,128)(2,1)S(1)}, bf16[2,64,2048]{2,1,0:T(8,128)(2,1)S(1)}, u32[]{:S(2)}, u32[]{:S(2)}) collective-permute-start(bf16[2,64,2048]{2,1,0:T(8,128)(2,1)S(1)} %pad_maximum_fusion.3), channel_id=1, source_target_pairs={{0,96},{16,112},{32,0},{48,16},{64,32},{80,48},{96,64},{112,80},{1... | collective-permute-start | bytes 1572872 | tf_op jit(solution)/shard_map/ppermute | solution.py:185
  218.8 35.6 %collective-permute-start.4 = (bf16[2,256,1024]{2,1,0:T(8,128)(2,1)S(1)}, bf16[2,256,1024]{2,1,0:T(8,128)(2,1)S(1)}, u32[]{:S(2)}, u32[]{:S(2)}) collective-permute-start(bf16[2,256,1024]{2,1,0:T(8,128)(2,1)S(1)} %pad_maximum_fusion.1), channel_id=1, source_target_pairs={{0,96},{16,112},{32,0},{48,16},{64,32},{80,48},{96,64},{112,80},{1... | collective-permute-start | bytes 3145736 | tf_op jit(solution)/shard_map/ppermute | solution.py:185
  219.0 35.5 %collective-permute-start.2 = (bf16[2,256,1024]{2,1,0:T(8,128)(2,1)S(1)}, bf16[2,256,1024]{2,1,0:T(8,128)(2,1)S(1)}, u32[]{:S(2)}, u32[]{:S(2)}) collective-permute-start(bf16[2,256,1024]{2,1,0:T(8,128)(2,1)S(1)} %pad_maximum_fusion), channel_id=1, source_target_pairs={{0,32},{16,48},{32,64},{48,80},{64,96},{80,112},{96,0},{112,16},{1... | collective-permute-start | bytes 3145736 | tf_op jit(solution)/shard_map/ppermute | solution.py:184
  222.3 31.0 %collective-permute-start.7 = (bf16[2,64,2048]{2,1,0:T(8,128)(2,1)S(1)}, bf16[2,64,2048]{2,1,0:T(8,128)(2,1)S(1)}, u32[]{:S(2)}, u32[]{:S(2)}) collective-permute-start(bf16[2,64,2048]{2,1,0:T(8,128)(2,1)S(1)} %pad_maximum_fusion.2), channel_id=1, source_target_pairs={{0,32},{16,48},{32,64},{48,80},{64,96},{80,112},{96,0},{112,16},{1... | collective-permute-start | bytes 1572872 | tf_op jit(solution)/shard_map/ppermute | solution.py:184
Sparse Core Ops, SparseCore 0:
  10.5 116.4 all-gather.1
  167.6 86.0 reduce-scatter.1

commit v2 on v1

v2 whole, which is shorter than its diff:
```python
import functools

import jax
import jax.numpy as jnp
from jax import lax
from jax.experimental import pallas as pl
from jax.experimental.pallas import tpu as pltpu
from jax.sharding import PartitionSpec as P

TOP = 8
SRC = 128
CHUNK = 4
PEER = 48
LANES = 128
F32 = jnp.float32
BF16 = jnp.bfloat16

NT = (((1,), (1,)), ((), ()))
TN = (((0,), (0,)), ((), ()))


def dot(a, b, dims=(((1,), (0,)), ((), ()))):
    return lax.dot_general(a, b, dims, preferred_element_type=F32)
VMEM = 58 << 20


def hot(tgt, plane, pair):
    half = 2 * PEER
    places = lax.broadcasted_iota(jnp.int32, (half, 2 * SRC), 0)
    return jnp.concatenate(
        [(places == tgt[plane, e * 2 + pair, :][None, :]).astype(F32).astype(BF16) for e in range(2)], axis=0
    )


def stage_kernel(n, tgt_x, tgt_g, rel, *refs):
    x, g, (wg, wu, wd) = refs[: 2 * n], refs[2 * n : 4 * n], refs[4 * n : 4 * n + 3]
    xs, pa, ab, wp, hp, gs, dap, probs_of, picked = refs[-9:]
    half = 2 * PEER
    slots = CHUNK * PEER
    width, ff = wg.shape[1], wg.shape[2]

    @pl.when(pl.program_id(0) == 0)
    def _():
        for plane in range(n):
            for pair in range(2):
                spots = pl.ds(pair * half, half)
                pick = hot(tgt_x, plane, pair)
                rows = x[plane * 2 + pair]
                got = dot(pick, rows[:, pl.ds(0, width)]).astype(BF16)
                local = rel[plane, pl.ds(pair * 2 * SRC, 2 * SRC), :].astype(F32)
                probs = rows[:, pl.ds(width, LANES)].astype(F32)
                got_g = dot(hot(tgt_g, plane, pair), g[plane * 2 + pair][...]).astype(BF16)
                for e in range(2):
                    part = slice(e * half, (e + 1) * half)
                    xs[e, plane, spots, :] = got[part]
                    picked[e, pl.ds(plane * slots + pair * half, half), :] = got_g[part]
                    for i in range(2):
                        at = e * half + i * PEER
                        gs[e, pair * 2 + i, plane] = got_g[at : at + PEER]
                    mine = jnp.where(local == e, probs, 0.0).astype(BF16)
                    col = jnp.sum(dot(pick[part], mine), axis=1, keepdims=True)
                    probs_of[e, pl.ds(plane * slots + pair * half, half), :] = jnp.broadcast_to(col, (half, LANES))

    e = pl.program_id(0)
    rows = xs[e].reshape(n * slots, width)
    h = dot(rows, wg[0])
    u = dot(rows, wu[0])
    p = probs_of[e][:, :1]
    s = 1.0 / (1.0 + jnp.exp(-h))
    hs = h * s
    a = hs * u
    shape = (n, slots, ff)
    ab[0] = a.astype(BF16).reshape(shape)
    pa[0] = (p * a).astype(BF16).reshape(shape)
    wp[0] = (p * (u * s * (1.0 + h * (1.0 - s)))).reshape(shape)
    hp[0] = (p * hs).reshape(shape)
    back = dot(picked[e], wd[0], NT)
    for plane in range(n):
        for i in range(CHUNK):
            at = plane * slots + i * PEER
            dap[0, i, plane] = back[at : at + PEER]


def fixed(shape, *at):
    return pl.BlockSpec(shape, lambda e: at, pipeline_mode=pl.Buffered(1))


def by_expert(shape, *at):
    return pl.BlockSpec((1, *shape), lambda e: (e, *at))


def stage_pass(n, at, tables, x, g, weights, prior):
    wg, wu, wd = weights
    width, ff = wg.shape[1], wg.shape[2]
    slots = CHUNK * PEER
    by_plane = [(width, BF16), (ff, BF16), (ff, BF16), (ff, F32), (ff, F32)]
    by_line = [(width, BF16), (ff, F32)]
    held = [] if prior is None else list(prior)
    before = 3 + len(x) + len(g) + 3
    return pl.pallas_call(
        functools.partial(stage_kernel, n),
        grid=(2,),
        in_specs=[fixed((n, CHUNK, 2 * SRC), at, 0, 0)] * 2
        + [fixed((n, CHUNK * SRC, LANES), at, 0, 0)]
        + [fixed(v.shape, 0, 0) for v in (*x, *g)]
        + [by_expert(w.shape[1:], 0, 0) for w in weights]
        + [pl.BlockSpec(memory_space=pl.ANY)] * len(held),
        out_specs=[fixed((2, n, slots, width), 0, at, 0, 0)]
        + [by_expert((n, slots, ff), at, 0, 0)] * 4
        + [fixed((2, 4, n, PEER, width), 0, 0, at, 0, 0), by_expert((4, n, PEER, ff), 0, at, 0, 0)],
        out_shape=[jax.ShapeDtypeStruct((2, 4, slots, w), t) for w, t in by_plane]
        + [jax.ShapeDtypeStruct((2, 4, 4, PEER, w), t) for w, t in by_line],
        scratch_shapes=[pltpu.VMEM((2, n * slots, LANES), F32), pltpu.VMEM((2, n * slots, width), BF16)],
        input_output_aliases={before + i: i for i in range(len(held))},
        compiler_params=pltpu.CompilerParams(vmem_limit_bytes=VMEM),
        cost_estimate=pl.CostEstimate(flops=1 << 28, bytes_accessed=1 << 19, transcendentals=0),
        name="stage",
    )(*tables, *x, *g, *weights, *held)


def turn_kernel(wg, wu, out):
    ff = wg.shape[2]
    out[0, pl.ds(0, ff), :] = wg[0].T
    out[0, pl.ds(ff, ff), :] = wu[0].T


def turn_pass(wg, wu):
    width, ff = wg.shape[1], wg.shape[2]
    return pl.pallas_call(
        turn_kernel,
        grid=(2,),
        in_specs=[by_expert((width, ff), 0, 0)] * 2,
        out_specs=by_expert((2 * ff, width), 0, 0),
        out_shape=jax.ShapeDtypeStruct((2, 2 * ff, width), BF16),
        compiler_params=pltpu.CompilerParams(vmem_limit_bytes=VMEM),
        cost_estimate=pl.CostEstimate(flops=1 << 28, bytes_accessed=1 << 19, transcendentals=0),
        name="turn",
    )(wg, wu)


def back_kernel(place, tgt, rel, ab, wp, hp, dap, wt_hbm, dhu, act, wt, dxs, qs, sem):
    half = 2 * PEER
    slots = 2 * CHUNK * PEER
    width = wt.shape[2]
    ff = ab.shape[3]
    step = pl.program_id(0)
    first = step == 0

    @pl.when(first)
    def _():
        for e in range(2):
            pltpu.make_async_copy(wt_hbm.at[e], wt.at[e], sem.at[e]).start()

    for e in range(2):
        back = dap[e].reshape(slots, ff)
        q = jnp.sum(ab[e].reshape(slots, ff).astype(F32) * back, axis=1, keepdims=True)
        dhu[e, :, pl.ds(0, ff)] = (back * wp[e].reshape(slots, ff)).astype(BF16)
        dhu[e, :, pl.ds(ff, ff)] = (back * hp[e].reshape(slots, ff)).astype(BF16)
        wide = jnp.broadcast_to(q, (slots, LANES)).astype(BF16)
        for pair in range(4):
            qs[pair, pl.ds(e * half, half), :] = wide[pair * half : (pair + 1) * half]
    for e in range(2):

        @pl.when(first)
        def _():
            pltpu.make_async_copy(wt_hbm.at[e], wt.at[e], sem.at[e]).wait()

        dx = dot(dhu[e], wt[e]).astype(BF16)
        for pair in range(4):
            dxs[pair, pl.ds(e * half, half), :] = dx[pair * half : (pair + 1) * half]
    for plane in range(2):
        high = place[2 + step * 2 + plane]
        for pair in range(2):
            held = plane * 2 + pair
            pick = hot(tgt, plane, pair)
            rows = dot(pick, dxs[held], TN).astype(BF16)
            local = rel[plane, pl.ds(pair * 2 * SRC, 2 * SRC), :].astype(F32)
            ext = jnp.zeros(local.shape, F32)
            for e in range(2):
                part = slice(e * half, (e + 1) * half)
                ext = ext + jnp.where(local == e, dot(pick[part], qs[held, pl.ds(e * half, half), :], TN), 0.0)
            ext = ext.astype(BF16)
            for i in range(2):
                part = slice(i * SRC, (i + 1) * SRC)
                y = place[6 + pair * 2 + i]
                act[high, 0, y, :, pl.ds(0, width)] = rows[part]
                act[high, 0, y, :, pl.ds(width, LANES)] = ext[part]


def back_pass(place, tgt, rel, ab, wp, hp, dap, wt):
    width, ff = wt.shape[2], ab.shape[3]
    slots = CHUNK * PEER
    by_plane = pl.BlockSpec((2, 2, slots, ff), lambda i, at: (0, i, 0, 0))
    return pl.pallas_call(
        back_kernel,
        grid_spec=pltpu.PrefetchScalarGridSpec(
            num_scalar_prefetch=1,
            grid=(2,),
            in_specs=[
                pl.BlockSpec((2, CHUNK, 2 * SRC), lambda i, at: (i, 0, 0)),
                pl.BlockSpec((2, CHUNK * SRC, LANES), lambda i, at: (i, 0, 0)),
                by_plane,
                by_plane,
                by_plane,
                pl.BlockSpec((2, 2, 4, PEER, ff), lambda i, at: (0, i, 0, 0, 0)),
                pl.BlockSpec(memory_space=pl.ANY),
            ],
            out_specs=[
                pl.BlockSpec((2, 2 * slots, 2 * ff), lambda i, at: (0, i, 0)),
                pl.BlockSpec((2, 1, 4, SRC, width + LANES), lambda i, at: (0, at[i], 0, 0, 0)),
            ],
            scratch_shapes=[
                pltpu.VMEM(wt.shape, BF16),
                pltpu.VMEM((4, 4 * PEER, width), BF16),
                pltpu.VMEM((4, 4 * PEER, LANES), BF16),
                pltpu.SemaphoreType.DMA((2,)),
            ],
        ),
        out_shape=[
            jax.ShapeDtypeStruct((2, 4 * slots, 2 * ff), BF16),
            jax.ShapeDtypeStruct((2, 2, 4, SRC, width + LANES), BF16),
        ],
        compiler_params=pltpu.CompilerParams(vmem_limit_bytes=VMEM),
        cost_estimate=pl.CostEstimate(flops=14 << 30, bytes_accessed=32 << 20, transcendentals=0),
        name="back",
    )(place, tgt, rel, ab, wp, hp, dap, wt)


def place_chunks(where, total, outs, step):
    my_x, my_c = where[0], where[1]
    for ahead in range(4):
        for own in range(2):
            core = my_c if own else 1 - my_c
            piece = lax.rem(my_x + ahead, 4) * 2 + core
            start = pl.multiple_of(piece * step, step)
            outs[own][ahead, 0] = total[pl.ds(start, step), :].astype(BF16)


def down_kernel(where, pa, gs, other, own, total):
    total[...] = dot(pa[0], gs[0], TN)
    place_chunks(where, total, (other, own), total.shape[0] // 8)


def up_kernel(where, xs, dhu, other, own, total):
    total[...] = dot(xs[0], dhu[0], TN)
    place_chunks(where, total, (other, own), total.shape[0] // 8)


def weight_pass(body, where, args, rows, cols, name):
    slots = args[0].shape[1]
    step = rows // 8
    out = jax.ShapeDtypeStruct((4, 2, step, cols), BF16)
    out_spec = pl.BlockSpec((4, 1, step, cols), lambda e: (0, e, 0, 0))
    return pl.pallas_call(
        body,
        grid=(2,),
        in_specs=[pl.BlockSpec(memory_space=pltpu.SMEM)]
        + [pl.BlockSpec((1, slots, a.shape[2]), lambda e: (e, 0, 0)) for a in args],
        out_specs=[out_spec, out_spec],
        out_shape=[out, out],
        scratch_shapes=[pltpu.VMEM((rows, cols), F32)],
        compiler_params=pltpu.CompilerParams(vmem_limit_bytes=VMEM),
        cost_estimate=pl.CostEstimate(flops=4 * slots * rows * cols, bytes_accessed=16 << 20, transcendentals=0),
        name=name,
    )(where, *args)


def along_x(by):
    return [(x * 2 + c, (x + by) % 4 * 2 + c) for x in range(4) for c in range(2)]


def swap_cores(other):
    return lax.ppermute(other, "dp", [(x * 2 + c, x * 2 + 1 - c) for x in range(4) for c in range(2)])


def both(own, got, *at):
    return own[at].astype(F32) + got[at].astype(F32)


def send_far(own, got):
    return (
        lax.ppermute(both(own, got, 2, 0).astype(BF16), "dp", along_x(1)),
        lax.ppermute(both(own, got, 2, 1).astype(BF16), "dp", along_x(-1)),
    )


def send_near(own, got, far):
    ahead = jnp.stack([both(own, got, 1, 0) + far[0].astype(F32), both(own, got, 1, 1)]).astype(BF16)
    back = jnp.stack([both(own, got, 3, 0), both(own, got, 3, 1) + far[1].astype(F32)]).astype(BF16)
    ahead, back = lax.ppermute(ahead, "dp", along_x(1)), lax.ppermute(back, "dp", along_x(-1))
    return both(own, got, 0) + ahead.astype(F32) + back.astype(F32)


def along_y(by):
    return [(z * 4 + y, z * 4 + (y + by) % 4) for z in range(4) for y in range(4)]


def along_z(by):
    return [(z * 4 + y, (z + by) % 4 * 4 + y) for z in range(4) for y in range(4)]


def send(value, route):
    return lax.ppermute(value, "expert", route)


def gather_line(block, ring):
    half = block.shape[0] // 2
    back, ahead = send(block, ring(1)), send(block, ring(-1))
    far = [send(back[:half], ring(1)), send(ahead[half:], ring(-1))]
    return jnp.concatenate([block, *far], axis=0), jnp.concatenate([back, ahead], axis=0)


def tables(ids, first, my_z, my_y):
    mine = first + jnp.arange(2, dtype=jnp.int32)
    ids = ids.reshape(4, 4, SRC, TOP)
    ids = jnp.roll(ids, (-my_z, -my_y), (0, 1))
    ids = jnp.stack([ids[0], ids[2], ids[3], ids[1]])
    ids = jnp.stack([ids[:, 0], ids[:, 2], ids[:, 3], ids[:, 1]], axis=1)
    hit = jnp.any(ids[None] == mine[:, None, None, None, None], axis=4)
    before = jnp.triu(jnp.ones((SRC, SRC), BF16), 1)
    rank = jnp.einsum("ezyr,rs->ezys", hit.astype(BF16), before, preferred_element_type=F32).astype(jnp.int32)
    slot = jnp.where(hit, rank, -2 * PEER)

    def by_pairs(t):
        t = t.reshape(2, 4, 2, 2, SRC) + jnp.arange(2, dtype=jnp.int32)[:, None] * PEER
        return jnp.transpose(t, (1, 0, 2, 3, 4)).reshape(4, CHUNK, 2 * SRC)

    rel = jnp.pad((ids - first).reshape(4, 4 * SRC, TOP), ((0, 0), (0, 0), (0, LANES - TOP)), constant_values=-1)
    return by_pairs(slot), by_pairs(jnp.swapaxes(slot, 1, 2)), rel.astype(BF16)


def on_device(activations, out_grad, gate_probs, expert_ids, w_gate, w_up, w_down):
    my_index = lax.axis_index("expert")
    dp_index = lax.axis_index("dp")
    width = activations.shape[1]
    ff = w_gate.shape[2]
    my_z, my_y = my_index // 4, my_index % 4
    rows = jnp.concatenate([activations, jnp.pad(gate_probs, ((0, 0), (0, LANES - TOP)))], axis=1)
    tgt_x, tgt_g, rel = tables(expert_ids, my_index * 2, my_z, my_y)
    weights = (w_gate, w_up, w_down)
    x_own, g_own = lax.optimization_barrier((gather_line(rows, along_y), gather_line(out_grad, along_z)))
    (x_lo, x_hi), (g_lo, g_hi) = x_own, g_own
    onward = (
        send(x_hi, along_z(1)),
        send(x_lo, along_z(-1)),
        send(g_hi, along_y(1)),
        send(g_lo, along_y(-1)),
    )
    turned = turn_pass(w_gate, w_up)
    made = stage_pass(1, 0, (tgt_x, tgt_g, rel), x_own, g_own, weights, None)
    x_lo, x_hi, g_lo, g_hi, onward, turned, made = lax.optimization_barrier(
        (x_lo, x_hi, g_lo, g_hi, onward, turned, made)
    )
    x_near = send(x_lo, along_z(1)), onward[0], onward[1], send(x_hi, along_z(-1))
    g_near = send(g_lo, along_y(1)), onward[2], onward[3], send(g_hi, along_y(-1))
    x_far = send(onward[1], along_z(-1)), send(onward[0], along_z(1))
    g_far = send(onward[3], along_y(-1)), send(onward[2], along_y(1))
    made = stage_pass(2, 1, (tgt_x, tgt_g, rel), x_near, g_near, weights, made)
    made = stage_pass(1, 1, (tgt_x, tgt_g, rel), x_far, g_far, weights, made)
    xs, pa, ab, wp, hp, gs, dap = made
    away = jnp.array([0, 2, 3, 1], jnp.int32)
    plane_z = (my_z + away) % 4
    place = jnp.concatenate([plane_z[::2] % 2, plane_z // 2, (my_y + away) % 4]).astype(jnp.int32)
    dhu, act = back_pass(place, tgt_x, rel, ab, wp, hp, dap, turned)
    act_sum = lax.psum_scatter(act.reshape(16 * SRC, -1), "expert", scatter_dimension=0, tiled=True)
    where = jnp.stack([dp_index // 2, dp_index % 2]).astype(jnp.int32)
    flat = lambda v: v.reshape(2, 16 * PEER, -1)
    up = weight_pass(up_kernel, where, (flat(xs), dhu), width, 2 * ff, "up_grad")
    down = weight_pass(down_kernel, where, (flat(pa), flat(gs)), ff, width, "down_grad")
    got_up, got_down = swap_cores(up[0]), swap_cores(down[0])
    far_up = send_far(up[1], got_up)
    got_down, far_up = lax.optimization_barrier((got_down, far_up))
    far_down = send_far(down[1], got_down)
    grad_both = send_near(up[1], got_up, far_up)
    grad_down = send_near(down[1], got_down, far_down)
    return (
        act_sum[:, :width],
        act_sum[:, width : width + TOP].astype(F32),
        grad_both[:, :, :ff].astype(BF16),
        grad_both[:, :, ff:].astype(BF16),
        grad_down.astype(BF16),
    )


def solution(mesh):
    placed = (
        P(("dp", "expert"), None),
        P(("dp", "expert"), None),
        P(("dp", "expert"), None),
        P("dp", None),
        P("expert", None, None),
        P("expert", None, None),
        P("expert", None, None),
    )
    return jax.shard_map(
        on_device,
        mesh=mesh,
        in_specs=placed,
        out_specs=(
            P(("dp", "expert"), None),
            P(("dp", "expert"), None),
            P("expert", "dp", None),
            P("expert", "dp", None),
            P("expert", "dp", None),
        ),
        check_vma=False,
    )
```

time: 271 us -> 248 us (0.915); the launches traced: 268 us -> 248 us
  waiting for transfers between devices: 164 us -> 81.4 us
  starting transfers between devices: 9.41 us -> 39.9 us
  Pallas kernels: 60.4 us -> 86.6 us
  local copies, waits for them, and re-layouts: 6.29 us -> 10.4 us
    all_gather x1 -> x0, waiting for transfers between devices: 114 us -> none  [on_device(): whole = lax.all_gather(payload, 'expert', axis=0, tiled=True)]
    ppermute x10 -> x30, waiting for transfers between devices: 49.3 us -> 81.4 us  [the longest x20 34.2 us: send(): return lax.ppermute(value, 'expert', route)]
    ppermute x10 -> x30, starting transfers between devices: 9.33 us -> 39.9 us  [the longest x20 30.9 us: send(): return lax.ppermute(value, 'expert', route)]
    pallas_call x1 -> x5, Pallas kernels: 40.5 us -> 66.7 us  [the longest x3 40.3 us: stage_pass(): pl.pallas_call(functools.partial(stage_kernel, n), grid=(2,), in_specs=[f...]
    convert_element_type x2 -> x1, other arithmetic: 4.28 us -> 0.39 us  [send_far(): both(own, got, 2, 0).astype(BF16)]
  transfers between devices with their start and end apart: 12 -> 31, of which waited for: 8 -> 12; matrix products, arithmetic and copies ran while one was open for 5% -> 8% of each run, Pallas kernels for 7% -> 22%
where the time goes in v2:
time: 248 us
  Pallas kernels  86.6 us (35%)
  waiting for transfers between devices  81.4 us (33%)
  starting transfers between devices  39.9 us (16%)
  other arithmetic  15 us (6%)
  between operations  14.5 us (6%)
  local copies, waits for them, and re-layouts  10.4 us (4%)
    pallas_call x3, Pallas kernels, stage_pass(): pl.pallas_call(functools.partial(stage_kernel, n), grid=(2,), in_specs=[f...  40.3 us
    ppermute x20, waiting for transfers between devices, send(): return lax.ppermute(value, 'expert', route)  34.2 us
    ppermute x20, starting transfers between devices, send(): return lax.ppermute(value, 'expert', route)  30.9 us
    ppermute x2, waiting for transfers between devices, send_near(): lax.ppermute(ahead, 'dp', along_x(1))  29 us
    pallas_call x2, Pallas kernels, weight_pass(): pl.pallas_call(body, grid=(2,), in_specs=[pl.BlockSpec(memory_space=pltpu...  19.9 us
    pallas_call x1, Pallas kernels, back_pass(): pl.pallas_call(back_kernel, grid_spec=pltpu.PrefetchScalarGridSpec(num_sc...  19.6 us
    ppermute x2, waiting for transfers between devices, send_far(): lax.ppermute(both(own, got, 2, 0).astype(BF16), 'dp', along_x(1))  14.9 us
    pallas_call x1, Pallas kernels, turn_pass(): pl.pallas_call(turn_kernel, grid=(2,), in_specs=[by_expert((width, ff), 0...  6.74 us
  transfers between devices with their start and end apart: 31, of which 12 were waited for; matrix products, arithmetic and copies ran while one was open for 8% of the time, Pallas kernels for 22%

profile of v2, /device:TPU:6, one launch (start us, length us, event | category | flops | bytes accessed | tf_op | source)
XLA Modules:
  0.0 247.9 jit_solution(14835583380408575473)
XLA Ops:
  7.2 2.0 collective-permute-start.4
  9.2 2.2 collective-permute-start.6
  12.2 1.9 pad_maximum_fusion.6
  15.7 1.7 collective-permute-start.2
  18.3 5.2 %collective-permute-done.4 = bf16[128,2048]{1,0:T(8,128)(2,1)S(1)} collective-permute-done((bf16[128,2048]{1,0:T(8,128)(2,1)}, bf16[128,2048]{1,0:T(8,128)(2,1)S(1)}, u32[]{:S(2)}, u32[]{:S(2)}) %collective-permute-start.4) | collective-permute-done | bytes 524320 | tf_op jit(solution)/shard_map/ppermute | solution.py:303
  23.6 3.3 %collective-permute-start.7 = (bf16[64,2048]{1,0:T(8,128)(2,1)S(1)}, bf16[64,2048]{1,0:T(8,128)(2,1)S(1)}, u32[]{:S(2)}, u32[]{:S(2)}) collective-permute-start(bf16[64,2048]{1,0:T(8,128)(2,1)S(1)} %slice.185), channel_id=1, source_target_pairs={{0,12},{1,13},{2,14},{3,15},{4,0},{5,1},{6,2},{7,3},{8,4},{9,5},{1... | collective-permute-start | bytes 786440 | tf_op jit(solution)/shard_map/ppermute | solution.py:303
  27.0 2.7 %collective-permute-done = bf16[128,2176]{1,0:T(8,128)(2,1)S(1)} collective-permute-done((bf16[128,2176]{1,0:T(8,128)(2,1)}, bf16[128,2176]{1,0:T(8,128)(2,1)S(1)}, u32[]{:S(2)}, u32[]{:S(2)}) %collective-permute-start) | collective-permute-done | bytes 557088 | tf_op jit(solution)/shard_map/ppermute | solution.py:303
  30.1 3.0 %collective-permute-start.3 = (bf16[64,2176]{1,0:T(8,128)(2,1)S(1)}, bf16[64,2176]{1,0:T(8,128)(2,1)S(1)}, u32[]{:S(2)}, u32[]{:S(2)}) collective-permute-start(bf16[64,2176]{1,0:T(8,128)(2,1)S(1)} %slice.183), channel_id=1, source_target_pairs={{0,3},{1,0},{2,1},{3,2},{4,7},{5,4},{6,5},{7,6},{8,11},{9,8},{10,9... | collective-permute-start | bytes 835592 | tf_op jit(solution)/shard_map/ppermute | solution.py:303
  34.4 3.9 %collective-permute-done.1 = bf16[64,2176]{1,0:T(8,128)(2,1)S(1)} collective-permute-done((bf16[64,2176]{1,0:T(8,128)(2,1)S(1)}, bf16[64,2176]{1,0:T(8,128)(2,1)S(1)}, u32[]{:S(2)}, u32[]{:S(2)}) %collective-permute-start.1) | collective-permute-done | bytes 278560 | tf_op jit(solution)/shard_map/ppermute | solution.py:303
  38.5 3.2 %collective-permute-start.9 = (bf16[256,2176]{1,0:T(8,128)(2,1)S(1)}, bf16[256,2176]{1,0:T(8,128)(2,1)}, u32[]{:S(2)}, u32[]{:S(2)}) collective-permute-start(bf16[256,2176]{1,0:T(8,128)(2,1)S(1)} %pad_maximum_fusion.refs_0_), channel_id=1, source_target_pairs={{0,12},{1,13},{2,14},{3,15},{4,0},{5,1},{6,2},{7,3},{8,4},{9,5},{1... | collective-permute-start | bytes 3342344 | tf_op jit(solution)/shard_map/ppermute | solution.py:303
  42.2 2.8 %collective-permute-start.11 = (bf16[256,2048]{1,0:T(8,128)(2,1)}, bf16[256,2048]{1,0:T(8,128)(2,1)}, u32[]{:S(2)}, u32[]{:S(2)}) collective-permute-start(bf16[256,2048]{1,0:T(8,128)(2,1)} %pad_maximum_fusion.2.refs_2_), channel_id=1, source_target_pairs={{0,3},{1,0},{2,1},{3,2},{4,7},{5,4},{6,5},{7,6},{8,11},{9,8},{10,9... | collective-permute-start | bytes 3145736 | tf_op jit(solution)/shard_map/ppermute | solution.py:303
  47.7 1.9 pad.9.rel
  49.6 6.7 %turn.1.wt_hbm = bf16[2,1024,2048]{2,1,0:T(8,128)(2,1)} custom-call(bf16[2,2048,512]{2,1,0:T(8,128)(2,1)} %refs_4_.3, bf16[2,2048,512]{2,1,0:T(8,128)(2,1)} %refs_5_.3), custom_call_target="tpu_custom_call" | custom-call | flops 268435456 | bytes 524288 | tf_op jit(solution)/shard_map/turn/pallas_call | solution.py:129
  56.4 11.6 %stage.3 = (bf16[2,4,192,2048]{3,2,1,0:T(8,128)(2,1)}, bf16[2,4,192,512]{3,2,1,0:T(8,128)(2,1)}, bf16[2,4,192,512]{3,2,1,0:T(8,128)(2,1)}, f32[2,4,192,512]{3,2,...) custom-call(s32[4,4,256]{2,1,0:T(4,128)} %reshape.197.tgt_x.tgt, ...), custom_call_target="tpu_custom_call" | custom-call | flops 268435456 | bytes 524288 | tf_op jit(solution)/shard_map/stage/pallas_call | solution.py:100
  68.3 3.2 %collective-permute-start.19 = (bf16[256,2048]{1,0:T(8,128)(2,1)S(1)}, bf16[256,2048]{1,0:T(8,128)(2,1)S(1)}, u32[]{:S(2)}, u32[]{:S(2)}) collective-permute-start(bf16[256,2048]{1,0:T(8,128)(2,1)S(1)} %copy-done.4), channel_id=1, source_target_pairs={{0,3},{1,0},{2,1},{3,2},{4,7},{5,4},{6,5},{7,6},{8,11},{9,8},{10,9... | collective-permute-start | bytes 3145736 | tf_op jit(solution)/shard_map/ppermute | solution.py:303
  71.5 3.1 %collective-permute-start.17 = (bf16[256,2176]{1,0:T(8,128)(2,1)}, bf16[256,2176]{1,0:T(8,128)(2,1)}, u32[]{:S(2)}, u32[]{:S(2)}) collective-permute-start(bf16[256,2176]{1,0:T(8,128)(2,1)} %copy-done), channel_id=1, source_target_pairs={{0,12},{1,13},{2,14},{3,15},{4,0},{5,1},{6,2},{7,3},{8,4},{9,5},{1... | collective-permute-start | bytes 3342344 | tf_op jit(solution)/shard_map/ppermute | solution.py:303
  74.7 16.6 %collective-permute-done.18.refs_4_ = bf16[256,2048]{1,0:T(8,128)(2,1)} collective-permute-done((bf16[256,2048]{1,0:T(8,128)(2,1)S(1)}, bf16[256,2048]{1,0:T(8,128)(2,1)}, u32[]{:S(2)}, u32[]{:S(2)}) %collective-permute-start.18) | collective-permute-done | bytes 1048608 | tf_op jit(solution)/shard_map/ppermute | solution.py:303
  91.3 3.3 %collective-permute-start.14 = (bf16[256,2048]{1,0:T(8,128)(2,1)}, bf16[256,2048]{1,0:T(8,128)(2,1)}, u32[]{:S(2)}, u32[]{:S(2)}) collective-permute-start(bf16[256,2048]{1,0:T(8,128)(2,1)} %collective-permute-done.11.refs_6_), channel_id=1, source_target_pairs={{0,3},{1,0},{2,1},{3,2},{4,7},{5,4},{6,5},{7,6},{8,11},{9,8},{10,9... | collective-permute-start | bytes 3145736 | tf_op jit(solution)/shard_map/ppermute | solution.py:303
  95.6 4.4 %collective-permute-done.17.refs_3_ = bf16[256,2176]{1,0:T(8,128)(2,1)} collective-permute-done((bf16[256,2176]{1,0:T(8,128)(2,1)}, bf16[256,2176]{1,0:T(8,128)(2,1)}, u32[]{:S(2)}, u32[]{:S(2)}) %collective-permute-start.17) | collective-permute-done | bytes 1114144 | tf_op jit(solution)/shard_map/ppermute | solution.py:303
  100.0 17.2 %stage.4 = (bf16[2,4,192,2048]{3,2,1,0:T(8,128)(2,1)}, bf16[2,4,192,512]{3,2,1,0:T(8,128)(2,1)}, bf16[2,4,192,512]{3,2,1,0:T(8,128)(2,1)}, f32[2,4,192,512]{3,2,...) custom-call(s32[4,4,256]{2,1,0:T(4,128)} %reshape.197.tgt_x.tgt, ...), custom_call_target="tpu_custom_call", output_to_operand_aliasing={{0}: (14, {}), {1}: (15, {}), {2}: (16, {}), {3}: (17, {}),... | custom-call | flops 268435456 | bytes 524288 | tf_op jit(solution)/shard_map/stage/pallas_call | solution.py:100
  120.0 11.5 %stage.5 = (bf16[2,4,192,2048]{3,2,1,0:T(8,128)(2,1)}, bf16[2,4,192,512]{3,2,1,0:T(8,128)(2,1)}, bf16[2,4,192,512]{3,2,1,0:T(8,128)(2,1)}, f32[2,4,192,512]{3,2,...) custom-call(s32[4,4,256]{2,1,0:T(4,128)} %reshape.197.tgt_x.tgt, ...), custom_call_target="tpu_custom_call", output_to_operand_aliasing={{0}: (10, {}), {1}: (11, {}), {2}: (12, {}), {3}: (13, {}),... | custom-call | flops 268435456 | bytes 524288 | tf_op jit(solution)/shard_map/stage/pallas_call | solution.py:100
  131.5 19.6 %back.1 = (bf16[2,768,1024]{2,1,0:T(8,128)(2,1)}, bf16[2,2,4,128,2176]{4,3,2,1,0:T(8,128)(2,1)}) custom-call(s32[10]{0:T(128)} %pad_add_fusion.4.place, s32[4,4,256]{2,1,0:T(4,128)} %reshape.197.tgt_x.tgt, bf16[4,512,128]{2,1,0:T(8,128)(2,1)} %pad.9.rel, bf16[2,4,192,512]{3,2,1,0:T(8,128)(2,1)} %get-tuple-element.88.ab, ...), custom_call_target="tpu_custom_call" | custom-call | flops 15032385536 | bytes 33554432 | tf_op jit(solution)/shard_map/back/pallas_call | solution.py:194
  151.7 12.1 %up_grad.1 = (bf16[4,2,256,1024]{3,2,1,0:T(8,128)(2,1)}, bf16[4,2,256,1024]{3,2,1,0:T(8,128)(2,1)}) custom-call(s32[2]{0:T(128)} %pad_add_fusion.5.where, bf16[2,768,2048]{2,1,0:T(8,128)(2,1)} %bitcast.83, bf16[2,768,1024]{2,1,0:T(8,128)(2,1)} %get-tuple-element.95.dhu), custom_call_target="tpu_custom_call" | custom-call | flops 6442450944 | bytes 16777216 | tf_op jit(solution)/shard_map/up_grad/pallas_call | solution.py:254
  163.9 7.8 %down_grad.1 = (bf16[4,2,64,2048]{3,2,1,0:T(8,128)(2,1)}, bf16[4,2,64,2048]{3,2,1,0:T(8,128)(2,1)}) custom-call(s32[2]{0:T(128)} %pad_add_fusion.5.where, bf16[2,768,512]{2,1,0:T(8,128)(2,1)} %bitcast.86, bf16[2,768,2048]{2,1,0:T(8,128)(2,1)} %bitcast.84), custom_call_target="tpu_custom_call" | custom-call | flops 3221225472 | bytes 16777216 | tf_op jit(solution)/shard_map/down_grad/pallas_call | solution.py:254
  172.2 2.6 %fusion.9 = (bf16[1,256,1024]{2,1,0:T(8,128)(2,1)S(1)}, bf16[1,256,1024]{2,1,0:T(8,128)(2,1)S(1)}, bf16[256,1024]{1,0:T(8,128)(2,1)S(1)}, bf16[256,1024]{1,0:T(8,128)(2,1)S(1)}) fusion(bf16[4,2,256,1024]{3,2,1,0:T(8,128)(2,1)} %collective-permute-done.20, bf16[4,2,256,1024]{3,2,1,0:T(8,128)(2,1)S(1)} %copy-done.2), kind=kLoop, calls=%fused_computation.25 | loop fusion | flops 4194304 | bytes 6291456 | tf_op jit(solution)/shard_map/add | solution.py:277
  177.0 11.9 %collective-permute-done.22 = bf16[256,1024]{1,0:T(8,128)(2,1)S(1)} collective-permute-done((bf16[256,1024]{1,0:T(8,128)(2,1)S(1)}, bf16[256,1024]{1,0:T(8,128)(2,1)S(1)}, u32[]{:S(2)}, u32[]{:S(2)}) %collective-permute-start.22) | collective-permute-done | bytes 524320 | tf_op jit(solution)/shard_map/ppermute | solution.py:282
  191.1 1.7 collective-permute-start.28
  192.8 1.8 fusion.11
  197.0 3.0 %collective-permute-done.26 = bf16[64,2048]{1,0:T(8,128)(2,1)S(1)} collective-permute-done((bf16[64,2048]{1,0:T(8,128)(2,1)S(1)}, bf16[64,2048]{1,0:T(8,128)(2,1)S(1)}, u32[]{:S(2)}, u32[]{:S(2)}) %collective-permute-start.26) | collective-permute-done | bytes 262176 | tf_op jit(solution)/shard_map/ppermute | solution.py:282
  202.8 29.0 %collective-permute-done.27 = bf16[2,64,2048]{2,1,0:T(8,128)(2,1)S(1)} collective-permute-done((bf16[2,64,2048]{2,1,0:T(8,128)(2,1)S(1)}, bf16[2,64,2048]{2,1,0:T(8,128)(2,1)S(1)}, u32[]{:S(2)}, u32[]{:S(2)}) %collective-permute-start.27) | collective-permute-done | bytes 524320 | tf_op jit(solution)/shard_map/ppermute | solution.py:290
  234.5 2.2 fusion.1
  239.1 1.9 slice.186
  (117 shorter events, 28.2 us)
Async XLA Ops:
  7.2 230.5 %reduce-scatter.4.cloned.1.call-start = ((), (), s32[]{:S(2)}) async-start(), calls=%async_computation.1 | async-start | bytes 9469952
  7.2 16.2 %collective-permute-start.4 = (bf16[128,2048]{1,0:T(8,128)(2,1)}, bf16[128,2048]{1,0:T(8,128)(2,1)S(1)}, u32[]{:S(2)}, u32[]{:S(2)}) collective-permute-start(bf16[128,2048]{1,0:T(8,128)(2,1)} %param.9), channel_id=1, source_target_pairs={{0,4},{1,5},{2,6},{3,7},{4,8},{5,9},{6,10},{7,11},{8,12},{9,13},{1... | collective-permute-start | bytes 1572872 | tf_op jit(solution)/shard_map/ppermute | solution.py:303
  9.2 14.4 %collective-permute-start.6 = (bf16[128,2048]{1,0:T(8,128)(2,1)}, bf16[128,2048]{1,0:T(8,128)(2,1)S(1)}, u32[]{:S(2)}, u32[]{:S(2)}) collective-permute-start(bf16[128,2048]{1,0:T(8,128)(2,1)} %param.9), channel_id=1, source_target_pairs={{0,12},{1,13},{2,14},{3,15},{4,0},{5,1},{6,2},{7,3},{8,4},{9,5},{1... | collective-permute-start | bytes 1572872 | tf_op jit(solution)/shard_map/ppermute | solution.py:303
  14.1 15.6 %collective-permute-start = (bf16[128,2176]{1,0:T(8,128)(2,1)}, bf16[128,2176]{1,0:T(8,128)(2,1)S(1)}, u32[]{:S(2)}, u32[]{:S(2)}) collective-permute-start(bf16[128,2176]{1,0:T(8,128)(2,1)} %pad_maximum_fusion.6), channel_id=1, source_target_pairs={{0,1},{1,2},{2,3},{3,0},{4,5},{5,6},{6,7},{7,4},{8,9},{9,10},{10,1... | collective-permute-start | bytes 1671176 | tf_op jit(solution)/shard_map/ppermute | solution.py:303
  15.7 14.4 %collective-permute-start.2 = (bf16[128,2176]{1,0:T(8,128)(2,1)}, bf16[128,2176]{1,0:T(8,128)(2,1)S(1)}, u32[]{:S(2)}, u32[]{:S(2)}) collective-permute-start(bf16[128,2176]{1,0:T(8,128)(2,1)} %pad_maximum_fusion.6), channel_id=1, source_target_pairs={{0,3},{1,0},{2,1},{3,2},{4,7},{5,4},{6,5},{7,6},{8,11},{9,8},{10,9... | collective-permute-start | bytes 1671176 | tf_op jit(solution)/shard_map/ppermute | solution.py:303
  23.5 9.7 %collective-permute-start.5 = (bf16[64,2048]{1,0:T(8,128)(2,1)S(1)}, bf16[64,2048]{1,0:T(8,128)(2,1)S(1)}, u32[]{:S(2)}, u32[]{:S(2)}) collective-permute-start(bf16[64,2048]{1,0:T(8,128)(2,1)S(1)} %slice.184), channel_id=1, source_target_pairs={{0,4},{1,5},{2,6},{3,7},{4,8},{5,9},{6,10},{7,11},{8,12},{9,13},{1... | collective-permute-start | bytes 786440 | tf_op jit(solution)/shard_map/ppermute | solution.py:303
  23.6 9.6 %collective-permute-start.7 = (bf16[64,2048]{1,0:T(8,128)(2,1)S(1)}, bf16[64,2048]{1,0:T(8,128)(2,1)S(1)}, u32[]{:S(2)}, u32[]{:S(2)}) collective-permute-start(bf16[64,2048]{1,0:T(8,128)(2,1)S(1)} %slice.185), channel_id=1, source_target_pairs={{0,12},{1,13},{2,14},{3,15},{4,0},{5,1},{6,2},{7,3},{8,4},{9,5},{1... | collective-permute-start | bytes 786440 | tf_op jit(solution)/shard_map/ppermute | solution.py:303
  29.7 8.6 %collective-permute-start.1 = (bf16[64,2176]{1,0:T(8,128)(2,1)S(1)}, bf16[64,2176]{1,0:T(8,128)(2,1)S(1)}, u32[]{:S(2)}, u32[]{:S(2)}) collective-permute-start(bf16[64,2176]{1,0:T(8,128)(2,1)S(1)} %slice.182), channel_id=1, source_target_pairs={{0,1},{1,2},{2,3},{3,0},{4,5},{5,6},{6,7},{7,4},{8,9},{9,10},{10,1... | collective-permute-start | bytes 835592 | tf_op jit(solution)/shard_map/ppermute | solution.py:303
  30.1 8.1 %collective-permute-start.3 = (bf16[64,2176]{1,0:T(8,128)(2,1)S(1)}, bf16[64,2176]{1,0:T(8,128)(2,1)S(1)}, u32[]{:S(2)}, u32[]{:S(2)}) collective-permute-start(bf16[64,2176]{1,0:T(8,128)(2,1)S(1)} %slice.183), channel_id=1, source_target_pairs={{0,3},{1,0},{2,1},{3,2},{4,7},{5,4},{6,5},{7,6},{8,11},{9,8},{10,9... | collective-permute-start | bytes 835592 | tf_op jit(solution)/shard_map/ppermute | solution.py:303
  38.4 29.7 %collective-permute-start.8 = (bf16[256,2176]{1,0:T(8,128)(2,1)S(1)}, bf16[256,2176]{1,0:T(8,128)(2,1)}, u32[]{:S(2)}, u32[]{:S(2)}) collective-permute-start(bf16[256,2176]{1,0:T(8,128)(2,1)S(1)} %pad_maximum_fusion.1.refs_1_), channel_id=1, source_target_pairs={{0,4},{1,5},{2,6},{3,7},{4,8},{5,9},{6,10},{7,11},{8,12},{9,13},{1... | collective-permute-start | bytes 3342344 | tf_op jit(solution)/shard_map/ppermute | solution.py:303
  38.5 29.6 %collective-permute-start.9 = (bf16[256,2176]{1,0:T(8,128)(2,1)S(1)}, bf16[256,2176]{1,0:T(8,128)(2,1)}, u32[]{:S(2)}, u32[]{:S(2)}) collective-permute-start(bf16[256,2176]{1,0:T(8,128)(2,1)S(1)} %pad_maximum_fusion.refs_0_), channel_id=1, source_target_pairs={{0,12},{1,13},{2,14},{3,15},{4,0},{5,1},{6,2},{7,3},{8,4},{9,5},{1... | collective-permute-start | bytes 3342344 | tf_op jit(solution)/shard_map/ppermute | solution.py:303
  41.7 26.3 %collective-permute-start.10 = (bf16[256,2048]{1,0:T(8,128)(2,1)S(1)}, bf16[256,2048]{1,0:T(8,128)(2,1)}, u32[]{:S(2)}, u32[]{:S(2)}) collective-permute-start(bf16[256,2048]{1,0:T(8,128)(2,1)S(1)} %pad_maximum_fusion.3.refs_3_), channel_id=1, source_target_pairs={{0,1},{1,2},{2,3},{3,0},{4,5},{5,6},{6,7},{7,4},{8,9},{9,10},{10,1... | collective-permute-start | bytes 3145736 | tf_op jit(solution)/shard_map/ppermute | solution.py:303
  42.2 25.8 %collective-permute-start.11 = (bf16[256,2048]{1,0:T(8,128)(2,1)}, bf16[256,2048]{1,0:T(8,128)(2,1)}, u32[]{:S(2)}, u32[]{:S(2)}) collective-permute-start(bf16[256,2048]{1,0:T(8,128)(2,1)} %pad_maximum_fusion.2.refs_2_), channel_id=1, source_target_pairs={{0,3},{1,0},{2,1},{3,2},{4,7},{5,4},{6,5},{7,6},{8,11},{9,8},{10,9... | collective-permute-start | bytes 3145736 | tf_op jit(solution)/shard_map/ppermute | solution.py:303
  56.4 38.5 %copy-start.13 = (s32[4]{0:T(128)S(1)}, s32[4]{0:T(128)}, u32[]{:S(2)}) copy-start(s32[4]{0:T(128)} %constant.122.clone) | copy-start | bytes 52
  68.1 26.5 %collective-permute-start.16 = (bf16[256,2176]{1,0:T(8,128)(2,1)}, bf16[256,2176]{1,0:T(8,128)(2,1)S(1)}, u32[]{:S(2)}, u32[]{:S(2)}) collective-permute-start(bf16[256,2176]{1,0:T(8,128)(2,1)} %copy-done.1), channel_id=1, source_target_pairs={{0,4},{1,5},{2,6},{3,7},{4,8},{5,9},{6,10},{7,11},{8,12},{9,13},{1... | collective-permute-start | bytes 3342344 | tf_op jit(solution)/shard_map/ppermute | solution.py:303
  68.2 23.1 %collective-permute-start.18 = (bf16[256,2048]{1,0:T(8,128)(2,1)S(1)}, bf16[256,2048]{1,0:T(8,128)(2,1)}, u32[]{:S(2)}, u32[]{:S(2)}) collective-permute-start(bf16[256,2048]{1,0:T(8,128)(2,1)S(1)} %copy-done.5), channel_id=1, source_target_pairs={{0,1},{1,2},{2,3},{3,0},{4,5},{5,6},{6,7},{7,4},{8,9},{9,10},{10,1... | collective-permute-start | bytes 3145736 | tf_op jit(solution)/shard_map/ppermute | solution.py:303
  68.3 23.0 %collective-permute-start.19 = (bf16[256,2048]{1,0:T(8,128)(2,1)S(1)}, bf16[256,2048]{1,0:T(8,128)(2,1)S(1)}, u32[]{:S(2)}, u32[]{:S(2)}) collective-permute-start(bf16[256,2048]{1,0:T(8,128)(2,1)S(1)} %copy-done.4), channel_id=1, source_target_pairs={{0,3},{1,0},{2,1},{3,2},{4,7},{5,4},{6,5},{7,6},{8,11},{9,8},{10,9... | collective-permute-start | bytes 3145736 | tf_op jit(solution)/shard_map/ppermute | solution.py:303
  71.5 28.5 %collective-permute-start.17 = (bf16[256,2176]{1,0:T(8,128)(2,1)}, bf16[256,2176]{1,0:T(8,128)(2,1)}, u32[]{:S(2)}, u32[]{:S(2)}) collective-permute-start(bf16[256,2176]{1,0:T(8,128)(2,1)} %copy-done), channel_id=1, source_target_pairs={{0,12},{1,13},{2,14},{3,15},{4,0},{5,1},{6,2},{7,3},{8,4},{9,5},{1... | collective-permute-start | bytes 3342344 | tf_op jit(solution)/shard_map/ppermute | solution.py:303
  74.6 44.0 %collective-permute-start.12 = (bf16[256,2176]{1,0:T(8,128)(2,1)}, bf16[256,2176]{1,0:T(8,128)(2,1)S(1)}, u32[]{:S(2)}, u32[]{:S(2)}) collective-permute-start(bf16[256,2176]{1,0:T(8,128)(2,1)} %collective-permute-done.9.refs_2_), channel_id=1, source_target_pairs={{0,12},{1,13},{2,14},{3,15},{4,0},{5,1},{6,2},{7,3},{8,4},{9,5},{1... | collective-permute-start | bytes 3342344 | tf_op jit(solution)/shard_map/ppermute | solution.py:303
  91.3 27.4 %collective-permute-start.13 = (bf16[256,2176]{1,0:T(8,128)(2,1)}, bf16[256,2176]{1,0:T(8,128)(2,1)S(1)}, u32[]{:S(2)}, u32[]{:S(2)}) collective-permute-start(bf16[256,2176]{1,0:T(8,128)(2,1)} %collective-permute-done.8.refs_1_), channel_id=1, source_target_pairs={{0,4},{1,5},{2,6},{3,7},{4,8},{5,9},{6,10},{7,11},{8,12},{9,13},{1... | collective-permute-start | bytes 3342344 | tf_op jit(solution)/shard_map/ppermute | solution.py:303
  91.3 25.9 %collective-permute-start.14 = (bf16[256,2048]{1,0:T(8,128)(2,1)}, bf16[256,2048]{1,0:T(8,128)(2,1)}, u32[]{:S(2)}, u32[]{:S(2)}) collective-permute-start(bf16[256,2048]{1,0:T(8,128)(2,1)} %collective-permute-done.11.refs_6_), channel_id=1, source_target_pairs={{0,3},{1,0},{2,1},{3,2},{4,7},{5,4},{6,5},{7,6},{8,11},{9,8},{10,9... | collective-permute-start | bytes 3145736 | tf_op jit(solution)/shard_map/ppermute | solution.py:303
  94.6 22.6 %collective-permute-start.15 = (bf16[256,2048]{1,0:T(8,128)(2,1)}, bf16[256,2048]{1,0:T(8,128)(2,1)}, u32[]{:S(2)}, u32[]{:S(2)}) collective-permute-start(bf16[256,2048]{1,0:T(8,128)(2,1)} %collective-permute-done.10.refs_5_), channel_id=1, source_target_pairs={{0,1},{1,2},{2,3},{3,0},{4,5},{5,6},{6,7},{7,4},{8,9},{9,10},{10,1... | collective-permute-start | bytes 3145736 | tf_op jit(solution)/shard_map/ppermute | solution.py:303
  163.9 8.3 %collective-permute-start.20 = (bf16[4,2,256,1024]{3,2,1,0:T(8,128)(2,1)}, bf16[4,2,256,1024]{3,2,1,0:T(8,128)(2,1)}, u32[]{:S(2)}, u32[]{:S(2)}) collective-permute-start(bf16[4,2,256,1024]{3,2,1,0:T(8,128)(2,1)} %get-tuple-element.97), channel_id=1, source_target_pairs={{0,16},{16,0},{32,48},{48,32},{64,80},{80,64},{96,112},{112,96},{1... | collective-permute-start | bytes 12582920 | tf_op jit(solution)/shard_map/ppermute | solution.py:273
  171.7 5.3 %collective-permute-start.21 = (bf16[4,2,64,2048]{3,2,1,0:T(8,128)(2,1)}, bf16[4,2,64,2048]{3,2,1,0:T(8,128)(2,1)S(1)}, u32[]{:S(2)}, u32[]{:S(2)}) collective-permute-start(bf16[4,2,64,2048]{3,2,1,0:T(8,128)(2,1)} %get-tuple-element.100), channel_id=1, source_target_pairs={{0,16},{16,0},{32,48},{48,32},{64,80},{80,64},{96,112},{112,96},{1... | collective-permute-start | bytes 6291464 | tf_op jit(solution)/shard_map/ppermute | solution.py:273
  174.9 14.0 %collective-permute-start.22 = (bf16[256,1024]{1,0:T(8,128)(2,1)S(1)}, bf16[256,1024]{1,0:T(8,128)(2,1)S(1)}, u32[]{:S(2)}, u32[]{:S(2)}) collective-permute-start(bf16[256,1024]{1,0:T(8,128)(2,1)S(1)} %get-tuple-element.132), channel_id=1, source_target_pairs={{0,32},{16,48},{32,64},{48,80},{64,96},{80,112},{96,0},{112,16},{1... | collective-permute-start | bytes 1572872 | tf_op jit(solution)/shard_map/ppermute | solution.py:282
  175.4 14.9 %collective-permute-start.23 = (bf16[256,1024]{1,0:T(8,128)(2,1)S(1)}, bf16[256,1024]{1,0:T(8,128)(2,1)S(1)}, u32[]{:S(2)}, u32[]{:S(2)}) collective-permute-start(bf16[256,1024]{1,0:T(8,128)(2,1)S(1)} %get-tuple-element.131), channel_id=1, source_target_pairs={{0,96},{16,112},{32,0},{48,16},{64,32},{80,48},{96,64},{112,80},{1... | collective-permute-start | bytes 1572872 | tf_op jit(solution)/shard_map/ppermute | solution.py:283
  190.7 9.3 %collective-permute-start.26 = (bf16[64,2048]{1,0:T(8,128)(2,1)S(1)}, bf16[64,2048]{1,0:T(8,128)(2,1)S(1)}, u32[]{:S(2)}, u32[]{:S(2)}) collective-permute-start(bf16[64,2048]{1,0:T(8,128)(2,1)S(1)} %get-tuple-element.135), channel_id=1, source_target_pairs={{0,32},{16,48},{32,64},{48,80},{64,96},{80,112},{96,0},{112,16},{1... | collective-permute-start | bytes 786440 | tf_op jit(solution)/shard_map/ppermute | solution.py:282
  191.1 9.2 %collective-permute-start.28 = (bf16[64,2048]{1,0:T(8,128)(2,1)S(1)}, bf16[64,2048]{1,0:T(8,128)(2,1)S(1)}, u32[]{:S(2)}, u32[]{:S(2)}) collective-permute-start(bf16[64,2048]{1,0:T(8,128)(2,1)S(1)} %get-tuple-element.136), channel_id=1, source_target_pairs={{0,96},{16,112},{32,0},{48,16},{64,32},{80,48},{96,64},{112,80},{1... | collective-permute-start | bytes 786440 | tf_op jit(solution)/shard_map/ppermute | solution.py:283
  194.8 39.7 %collective-permute-start.24 = (bf16[2,256,1024]{2,1,0:T(8,128)(2,1)S(1)}, bf16[2,256,1024]{2,1,0:T(8,128)(2,1)S(1)}, u32[]{:S(2)}, u32[]{:S(2)}) collective-permute-start(bf16[2,256,1024]{2,1,0:T(8,128)(2,1)S(1)} %pad_maximum_fusion.4), channel_id=1, source_target_pairs={{0,32},{16,48},{32,64},{48,80},{64,96},{80,112},{96,0},{112,16},{1... | collective-permute-start | bytes 3145736 | tf_op jit(solution)/shard_map/ppermute | solution.py:290
  196.4 38.1 %collective-permute-start.25 = (bf16[2,256,1024]{2,1,0:T(8,128)(2,1)S(1)}, bf16[2,256,1024]{2,1,0:T(8,128)(2,1)S(1)}, u32[]{:S(2)}, u32[]{:S(2)}) collective-permute-start(bf16[2,256,1024]{2,1,0:T(8,128)(2,1)S(1)} %pad_maximum_fusion.5), channel_id=1, source_target_pairs={{0,96},{16,112},{32,0},{48,16},{64,32},{80,48},{96,64},{112,80},{1... | collective-permute-start | bytes 3145736 | tf_op jit(solution)/shard_map/ppermute | solution.py:290
  200.6 31.2 %collective-permute-start.27 = (bf16[2,64,2048]{2,1,0:T(8,128)(2,1)S(1)}, bf16[2,64,2048]{2,1,0:T(8,128)(2,1)S(1)}, u32[]{:S(2)}, u32[]{:S(2)}) collective-permute-start(bf16[2,64,2048]{2,1,0:T(8,128)(2,1)S(1)} %pad_maximum_fusion.7), channel_id=1, source_target_pairs={{0,32},{16,48},{32,64},{48,80},{64,96},{80,112},{96,0},{112,16},{1... | collective-permute-start | bytes 1572872 | tf_op jit(solution)/shard_map/ppermute | solution.py:290
  201.6 31.7 %collective-permute-start.29 = (bf16[2,64,2048]{2,1,0:T(8,128)(2,1)S(1)}, bf16[2,64,2048]{2,1,0:T(8,128)(2,1)S(1)}, u32[]{:S(2)}, u32[]{:S(2)}) collective-permute-start(bf16[2,64,2048]{2,1,0:T(8,128)(2,1)S(1)} %pad_maximum_fusion.8), channel_id=1, source_target_pairs={{0,96},{16,112},{32,0},{48,16},{64,32},{80,48},{96,64},{112,80},{1... | collective-permute-start | bytes 1572872 | tf_op jit(solution)/shard_map/ppermute | solution.py:290
  (13 other events, 131.4 us)
Sparse Core Ops, SparseCore 0:
  151.3 85.3 reduce-scatter.3

commit v3 on v2

--- a/solution.py
+++ b/solution.py
@@ -32,49 +32,56 @@
     )
 
 
+def pick_rows(n, tgt_x, tgt_g, rel, x, g, xs, gs, probs_of, picked):
+    half = 2 * PEER
+    slots = CHUNK * PEER
+    width = xs.shape[3]
+    for plane in range(n):
+        for pair in range(2):
+            spots = pl.ds(pair * half, half)
+            pick = hot(tgt_x, plane, pair)
+            rows = x[plane * 2 + pair]
+            got = dot(pick, rows[:, pl.ds(0, width)]).astype(BF16)
+            local = rel[plane, pl.ds(pair * 2 * SRC, 2 * SRC), :].astype(F32)
+            probs = rows[:, pl.ds(width, LANES)].astype(F32)
+            got_g = dot(hot(tgt_g, plane, pair), g[plane * 2 + pair][...]).astype(BF16)
+            for e in range(2):
+                part = slice(e * half, (e + 1) * half)
+                xs[e, plane, spots, :] = got[part]
+                picked[e, pl.ds(plane * slots + pair * half, half), :] = got_g[part]
+                for i in range(2):
+                    at = e * half + i * PEER
+                    gs[e, pair * 2 + i, plane] = got_g[at : at + PEER]
+                mine = jnp.where(local == e, probs, 0.0).astype(BF16)
+                col = jnp.sum(dot(pick[part], mine), axis=1, keepdims=True)
+                probs_of[e, pl.ds(plane * slots + pair * half, half), :] = jnp.broadcast_to(col, (half, LANES))
+
+
+def products(rows, picked, p, wg, wu, wd):
+    h = dot(rows, wg)
+    u = dot(rows, wu)
+    s = 1.0 / (1.0 + jnp.exp(-h))
+    hs = h * s
+    a = hs * u
+    wp = p * (u * s * (1.0 + h * (1.0 - s)))
+    return tuple(v.astype(BF16) for v in (p * a, a, wp, p * hs, dot(picked, wd, NT)))
+
+
 def stage_kernel(n, tgt_x, tgt_g, rel, *refs):
     x, g, (wg, wu, wd) = refs[: 2 * n], refs[2 * n : 4 * n], refs[4 * n : 4 * n + 3]
     xs, pa, ab, wp, hp, gs, dap, probs_of, picked = refs[-9:]
-    half = 2 * PEER
     slots = CHUNK * PEER
     width, ff = wg.shape[1], wg.shape[2]
-
-    @pl.when(pl.program_id(0) == 0)
+    e = pl.program_id(0)
+
+    @pl.when(e == 0)
     def _():
-        for plane in range(n):
-            for pair in range(2):
-                spots = pl.ds(pair * half, half)
-                pick = hot(tgt_x, plane, pair)
-                rows = x[plane * 2 + pair]
-                got = dot(pick, rows[:, pl.ds(0, width)]).astype(BF16)
-                local = rel[plane, pl.ds(pair * 2 * SRC, 2 * SRC), :].astype(F32)
-                probs = rows[:, pl.ds(width, LANES)].astype(F32)
-                got_g = dot(hot(tgt_g, plane, pair), g[plane * 2 + pair][...]).astype(BF16)
-                for e in range(2):
-                    part = slice(e * half, (e + 1) * half)
-                    xs[e, plane, spots, :] = got[part]
-                    picked[e, pl.ds(plane * slots + pair * half, half), :] = got_g[part]
-                    for i in range(2):
-                        at = e * half + i * PEER
-                        gs[e, pair * 2 + i, plane] = got_g[at : at + PEER]
-                    mine = jnp.where(local == e, probs, 0.0).astype(BF16)
-                    col = jnp.sum(dot(pick[part], mine), axis=1, keepdims=True)
-                    probs_of[e, pl.ds(plane * slots + pair * half, half), :] = jnp.broadcast_to(col, (half, LANES))
-
-    e = pl.program_id(0)
+        pick_rows(n, tgt_x, tgt_g, rel, x, g, xs, gs, probs_of, picked)
+
     rows = xs[e].reshape(n * slots, width)
-    h = dot(rows, wg[0])
-    u = dot(rows, wu[0])
-    p = probs_of[e][:, :1]
-    s = 1.0 / (1.0 + jnp.exp(-h))
-    hs = h * s
-    a = hs * u
-    shape = (n, slots, ff)
-    ab[0] = a.astype(BF16).reshape(shape)
-    pa[0] = (p * a).astype(BF16).reshape(shape)
-    wp[0] = (p * (u * s * (1.0 + h * (1.0 - s)))).reshape(shape)
-    hp[0] = (p * hs).reshape(shape)
-    back = dot(picked[e], wd[0], NT)
+    *made, back = products(rows, picked[e], probs_of[e][:, :1], wg[0], wu[0], wd[0])
+    for out, value in zip((pa, ab, wp, hp), made):
+        out[0] = value.reshape(n, slots, ff)
     for plane in range(n):
         for i in range(CHUNK):
             at = plane * slots + i * PEER
@@ -93,8 +100,8 @@
     wg, wu, wd = weights
     width, ff = wg.shape[1], wg.shape[2]
     slots = CHUNK * PEER
-    by_plane = [(width, BF16), (ff, BF16), (ff, BF16), (ff, F32), (ff, F32)]
-    by_line = [(width, BF16), (ff, F32)]
+    by_plane = [width, ff, ff, ff, ff]
+    by_line = [width, ff]
     held = [] if prior is None else list(prior)
     before = 3 + len(x) + len(g) + 3
     return pl.pallas_call(
@@ -108,8 +115,8 @@
         out_specs=[fixed((2, n, slots, width), 0, at, 0, 0)]
         + [by_expert((n, slots, ff), at, 0, 0)] * 4
         + [fixed((2, 4, n, PEER, width), 0, 0, at, 0, 0), by_expert((4, n, PEER, ff), 0, at, 0, 0)],
-        out_shape=[jax.ShapeDtypeStruct((2, 4, slots, w), t) for w, t in by_plane]
-        + [jax.ShapeDtypeStruct((2, 4, 4, PEER, w), t) for w, t in by_line],
+        out_shape=[jax.ShapeDtypeStruct((2, 4, slots, w), BF16) for w in by_plane]
+        + [jax.ShapeDtypeStruct((2, 4, 4, PEER, w), BF16) for w in by_line],
         scratch_shapes=[pltpu.VMEM((2, n * slots, LANES), F32), pltpu.VMEM((2, n * slots, width), BF16)],
         input_output_aliases={before + i: i for i in range(len(held))},
         compiler_params=pltpu.CompilerParams(vmem_limit_bytes=VMEM),
@@ -138,92 +145,133 @@
     )(wg, wu)
 
 
-def back_kernel(place, tgt, rel, ab, wp, hp, dap, wt_hbm, dhu, act, wt, dxs, qs, sem):
+def held_copies(held, kept, wt_hbm, wt, sem):
+    copies = [(wt_hbm.at[e], wt.at[e]) for e in range(2)]
+    for i, (src, dst) in enumerate(zip(held, kept)):
+        for part in (pl.ds(0, 1), pl.ds(2, 2)):
+            at = (slice(None), slice(None), part) if i == 3 else (slice(None), part)
+            copies.append((src.at[at], dst.at[at]))
+    return [pltpu.make_async_copy(src, dst, sem.at[i]) for i, (src, dst) in enumerate(copies)]
+
+
+def tail_kernel(place, tgt_x, tgt_g, rel_x, tgt, rel, x_lo, x_hi, g_lo, g_hi, wg, wu, wd, wt_hbm, *refs):
+    held = refs[3:7]
+    xs, pa, gs, dhu, act, wt, ab, wp, hp, dap, probs_of, picked, dxs, qs, sem = refs[7:]
+    kept = (ab, wp, hp, dap)
     half = 2 * PEER
-    slots = 2 * CHUNK * PEER
-    width = wt.shape[2]
-    ff = ab.shape[3]
+    slots = CHUNK * PEER
+    width, ff = wg.shape[1], wg.shape[2]
     step = pl.program_id(0)
-    first = step == 0
-
-    @pl.when(first)
+
+    @pl.when(step == 0)
     def _():
+        for copy in held_copies(held, kept, wt_hbm, wt, sem):
+            copy.start()
+        pick_rows(1, tgt_x, tgt_g, rel_x, (x_lo, x_hi), (g_lo, g_hi), xs, gs, probs_of, picked)
+
+    @pl.when(step < 2)
+    def _():
+        made = products(xs[step, 0], picked[step], probs_of[step][:, :1], wg[0], wu[0], wd[0])
+        pa[0, 0] = made[0]
+        for out, value in zip((ab, wp, hp), made[1:4]):
+            out[step, 1] = value
+        for i in range(CHUNK):
+            dap[step, i, 1] = made[4][i * PEER : (i + 1) * PEER]
+
+    @pl.when(step == 2)
+    def _():
+        for copy in held_copies(held, kept, wt_hbm, wt, sem):
+            copy.wait()
+
+    @pl.when(step >= 2)
+    def _():
+        k = step - 2
         for e in range(2):
-            pltpu.make_async_copy(wt_hbm.at[e], wt.at[e], sem.at[e]).start()
-
-    for e in range(2):
-        back = dap[e].reshape(slots, ff)
-        q = jnp.sum(ab[e].reshape(slots, ff).astype(F32) * back, axis=1, keepdims=True)
-        dhu[e, :, pl.ds(0, ff)] = (back * wp[e].reshape(slots, ff)).astype(BF16)
-        dhu[e, :, pl.ds(ff, ff)] = (back * hp[e].reshape(slots, ff)).astype(BF16)
-        wide = jnp.broadcast_to(q, (slots, LANES)).astype(BF16)
-        for pair in range(4):
-            qs[pair, pl.ds(e * half, half), :] = wide[pair * half : (pair + 1) * half]
-    for e in range(2):
-
-        @pl.when(first)
-        def _():
-            pltpu.make_async_copy(wt_hbm.at[e], wt.at[e], sem.at[e]).wait()
-
-        dx = dot(dhu[e], wt[e]).astype(BF16)
-        for pair in range(4):
-            dxs[pair, pl.ds(e * half, half), :] = dx[pair * half : (pair + 1) * half]
-    for plane in range(2):
-        high = place[2 + step * 2 + plane]
+            back = dap[e, k].astype(F32).reshape(slots, ff)
+            q = jnp.sum(ab[e, k].astype(F32) * back, axis=1, keepdims=True)
+            dhu[e, :, pl.ds(0, ff)] = (back * wp[e, k].astype(F32)).astype(BF16)
+            dhu[e, :, pl.ds(ff, ff)] = (back * hp[e, k].astype(F32)).astype(BF16)
+            wide = jnp.broadcast_to(q, (slots, LANES)).astype(BF16)
+            for pair in range(2):
+                qs[pair, pl.ds(e * half, half), :] = wide[pair * half : (pair + 1) * half]
+        for e in range(2):
+            dx = dot(dhu[e], wt[e]).astype(BF16)
+            for pair in range(2):
+                dxs[pair, pl.ds(e * half, half), :] = dx[pair * half : (pair + 1) * half]
         for pair in range(2):
-            held = plane * 2 + pair
-            pick = hot(tgt, plane, pair)
-            rows = dot(pick, dxs[held], TN).astype(BF16)
-            local = rel[plane, pl.ds(pair * 2 * SRC, 2 * SRC), :].astype(F32)
+            pick = hot(tgt, 0, pair)
+            rows = dot(pick, dxs[pair], TN).astype(BF16)
+            local = rel[0, pl.ds(pair * 2 * SRC, 2 * SRC), :].astype(F32)
             ext = jnp.zeros(local.shape, F32)
             for e in range(2):
                 part = slice(e * half, (e + 1) * half)
-                ext = ext + jnp.where(local == e, dot(pick[part], qs[held, pl.ds(e * half, half), :], TN), 0.0)
+                ext = ext + jnp.where(local == e, dot(pick[part], qs[pair, pl.ds(e * half, half), :], TN), 0.0)
             ext = ext.astype(BF16)
             for i in range(2):
                 part = slice(i * SRC, (i + 1) * SRC)
-                y = place[6 + pair * 2 + i]
-                act[high, 0, y, :, pl.ds(0, width)] = rows[part]
-                act[high, 0, y, :, pl.ds(width, LANES)] = ext[part]
-
-
-def back_pass(place, tgt, rel, ab, wp, hp, dap, wt):
-    width, ff = wt.shape[2], ab.shape[3]
+                y = place[4 + pair * 2 + i]
+                act[0, y, :, pl.ds(0, width)] = rows[part]
+                act[0, y, :, pl.ds(width, LANES)] = ext[part]
+
+
+def tail_pass(place, tables, x, g, weights, wt, made):
+    tgt_x, tgt_g, rel = tables
+    wg, wu, wd = weights
+    width, ff = wg.shape[1], wg.shape[2]
     slots = CHUNK * PEER
-    by_plane = pl.BlockSpec((2, 2, slots, ff), lambda i, at: (0, i, 0, 0))
+    xs, pa, ab, wp, hp, gs, dap = made
+    once = pl.Buffered(1)
+    kept = lambda shape, *at: pl.BlockSpec(shape, lambda i, p: at, pipeline_mode=once)
+    plane = lambda i: jnp.maximum(i - 2, 0)
+    expert = lambda i: jnp.minimum(i, 1)
+    of_plane = lambda *shape: pl.BlockSpec((1, *shape), lambda i, p: (plane(i), 0, 0))
+    of_expert = lambda w: pl.BlockSpec((1, *w.shape[1:]), lambda i, p: (expert(i), 0, 0))
+    anywhere = pl.BlockSpec(memory_space=pl.ANY)
     return pl.pallas_call(
-        back_kernel,
+        tail_kernel,
         grid_spec=pltpu.PrefetchScalarGridSpec(
             num_scalar_prefetch=1,
-            grid=(2,),
+            grid=(6,),
             in_specs=[
-                pl.BlockSpec((2, CHUNK, 2 * SRC), lambda i, at: (i, 0, 0)),
-                pl.BlockSpec((2, CHUNK * SRC, LANES), lambda i, at: (i, 0, 0)),
-                by_plane,
-                by_plane,
-                by_plane,
-                pl.BlockSpec((2, 2, 4, PEER, ff), lambda i, at: (0, i, 0, 0, 0)),
-                pl.BlockSpec(memory_space=pl.ANY),
-            ],
+                kept((1, CHUNK, 2 * SRC), 1, 0, 0),
+                kept((1, CHUNK, 2 * SRC), 1, 0, 0),
+                kept((1, CHUNK * SRC, LANES), 1, 0, 0),
+                of_plane(CHUNK, 2 * SRC),
+                of_plane(CHUNK * SRC, LANES),
+            ]
+            + [kept(v.shape, 0, 0) for v in (*x, *g)]
+            + [of_expert(w) for w in weights]
+            + [anywhere] * 8,
             out_specs=[
-                pl.BlockSpec((2, 2 * slots, 2 * ff), lambda i, at: (0, i, 0)),
-                pl.BlockSpec((2, 1, 4, SRC, width + LANES), lambda i, at: (0, at[i], 0, 0, 0)),
+                kept((2, 1, slots, width), 0, 1, 0, 0),
+                pl.BlockSpec((1, 1, slots, ff), lambda i, p: (expert(i), 1, 0, 0)),
+                kept((2, 4, 1, PEER, width), 0, 0, 1, 0, 0),
+                pl.BlockSpec((2, slots, 2 * ff), lambda i, p: (0, plane(i), 0)),
+                pl.BlockSpec((1, 4, SRC, width + LANES), lambda i, p: (p[plane(i)], 0, 0, 0)),
             ],
             scratch_shapes=[
                 pltpu.VMEM(wt.shape, BF16),
-                pltpu.VMEM((4, 4 * PEER, width), BF16),
-                pltpu.VMEM((4, 4 * PEER, LANES), BF16),
-                pltpu.SemaphoreType.DMA((2,)),
+                pltpu.VMEM(ab.shape, BF16),
+                pltpu.VMEM(wp.shape, BF16),
+                pltpu.VMEM(hp.shape, BF16),
+                pltpu.VMEM(dap.shape, BF16),
+                pltpu.VMEM((2, slots, LANES), F32),
+                pltpu.VMEM((2, slots, width), BF16),
+                pltpu.VMEM((2, 4 * PEER, width), BF16),
+                pltpu.VMEM((2, 4 * PEER, LANES), BF16),
+                pltpu.SemaphoreType.DMA((10,)),
             ],
         ),
-        out_shape=[
+        out_shape=[jax.ShapeDtypeStruct(v.shape, BF16) for v in (xs, pa, gs)]
+        + [
             jax.ShapeDtypeStruct((2, 4 * slots, 2 * ff), BF16),
-            jax.ShapeDtypeStruct((2, 2, 4, SRC, width + LANES), BF16),
+            jax.ShapeDtypeStruct((4, 4, SRC, width + LANES), BF16),
         ],
+        input_output_aliases={14: 0, 15: 1, 16: 2},
         compiler_params=pltpu.CompilerParams(vmem_limit_bytes=VMEM),
         cost_estimate=pl.CostEstimate(flops=14 << 30, bytes_accessed=32 << 20, transcendentals=0),
-        name="back",
-    )(place, tgt, rel, ab, wp, hp, dap, wt)
+        name="tail",
+    )(place, tgt_x, tgt_g, rel, tgt_x, rel, *x, *g, wg, wu, wd, wt, xs, pa, gs, ab, wp, hp, dap)
 
 
 def place_chunks(where, total, outs, step):
@@ -356,12 +404,9 @@
     x_far = send(onward[1], along_z(-1)), send(onward[0], along_z(1))
     g_far = send(onward[3], along_y(-1)), send(onward[2], along_y(1))
     made = stage_pass(2, 1, (tgt_x, tgt_g, rel), x_near, g_near, weights, made)
-    made = stage_pass(1, 1, (tgt_x, tgt_g, rel), x_far, g_far, weights, made)
-    xs, pa, ab, wp, hp, gs, dap = made
     away = jnp.array([0, 2, 3, 1], jnp.int32)
-    plane_z = (my_z + away) % 4
-    place = jnp.concatenate([plane_z[::2] % 2, plane_z // 2, (my_y + away) % 4]).astype(jnp.int32)
-    dhu, act = back_pass(place, tgt_x, rel, ab, wp, hp, dap, turned)
+    place = jnp.concatenate([(my_z + away) % 4, (my_y + away) % 4]).astype(jnp.int32)
+    xs, pa, gs, dhu, act = tail_pass(place, (tgt_x, tgt_g, rel), x_far, g_far, weights, turned, made)
     act_sum = lax.psum_scatter(act.reshape(16 * SRC, -1), "expert", scatter_dimension=0, tiled=True)
     where = jnp.stack([dp_index // 2, dp_index % 2]).astype(jnp.int32)
     flat = lambda v: v.reshape(2, 16 * PEER, -1)

time: 248 us -> 240 us (0.968)
  Pallas kernels: 86.6 us -> 79.3 us
    pallas_call x3 -> x2, Pallas kernels: 40.3 us -> 28.5 us  [stage_pass(): pl.pallas_call(functools.partial(stage_kernel, n), grid=(2,), in_specs=[f...]
    pallas_call x1, Pallas kernels: 19.6 us -> 24.1 us  [tail_pass(): pl.pallas_call(tail_kernel, grid_spec=pltpu.PrefetchScalarGridSpec(num_sc...]
  transfers between devices with their start and end apart: 31 -> 31, of which waited for: 12 -> 12; matrix products, arithmetic and copies ran while one was open for 8% -> 9% of each run, Pallas kernels for 22% -> 23%
where the time goes in v3:
time: 240 us; the launch traced here: 239 us
  waiting for transfers between devices  80.6 us (34%)
  Pallas kernels  79.3 us (33%)
  starting transfers between devices  39.8 us (17%)
  other arithmetic  14.9 us (6%)
  between operations  14.5 us (6%)
  local copies, waits for them, and re-layouts  10.2 us (4%)
    ppermute x20, waiting for transfers between devices, send(): return lax.ppermute(value, 'expert', route)  33.4 us
    ppermute x20, starting transfers between devices, send(): return lax.ppermute(value, 'expert', route)  30.8 us
    ppermute x2, waiting for transfers between devices, send_near(): lax.ppermute(ahead, 'dp', along_x(1))  29 us
    pallas_call x2, Pallas kernels, stage_pass(): pl.pallas_call(functools.partial(stage_kernel, n), grid=(2,), in_specs=[f...  28.5 us
    pallas_call x1, Pallas kernels, tail_pass(): pl.pallas_call(tail_kernel, grid_spec=pltpu.PrefetchScalarGridSpec(num_sc...  24.1 us
    pallas_call x2, Pallas kernels, weight_pass(): pl.pallas_call(body, grid=(2,), in_specs=[pl.BlockSpec(memory_space=pltpu...  20 us
    ppermute x2, waiting for transfers between devices, send_far(): lax.ppermute(both(own, got, 2, 0).astype(BF16), 'dp', along_x(1))  15 us
    pallas_call x1, Pallas kernels, turn_pass(): pl.pallas_call(turn_kernel, grid=(2,), in_specs=[by_expert((width, ff), 0...  6.78 us
  transfers between devices with their start and end apart: 31, of which 12 were waited for; matrix products, arithmetic and copies ran while one was open for 9% of the time, Pallas kernels for 23%

profile of v3, /device:TPU:6, one launch (start us, length us, event | category | flops | bytes accessed | tf_op | source)
XLA Modules:
  0.0 239.5 jit_solution(17246662124147965845)
XLA Ops:
  7.2 2.0 collective-permute-start.4
  9.2 2.2 collective-permute-start.6
  12.2 1.9 pad_maximum_fusion.6
  14.1 1.6 collective-permute-start
  15.7 1.7 collective-permute-start.2
  18.3 5.2 %collective-permute-done.4 = bf16[128,2048]{1,0:T(8,128)(2,1)S(1)} collective-permute-done((bf16[128,2048]{1,0:T(8,128)(2,1)}, bf16[128,2048]{1,0:T(8,128)(2,1)S(1)}, u32[]{:S(2)}, u32[]{:S(2)}) %collective-permute-start.4) | collective-permute-done | bytes 524320 | tf_op jit(solution)/shard_map/ppermute | solution.py:351
  23.6 3.3 %collective-permute-start.7 = (bf16[64,2048]{1,0:T(8,128)(2,1)S(1)}, bf16[64,2048]{1,0:T(8,128)(2,1)S(1)}, u32[]{:S(2)}, u32[]{:S(2)}) collective-permute-start(bf16[64,2048]{1,0:T(8,128)(2,1)S(1)} %slice.181), channel_id=1, source_target_pairs={{0,12},{1,13},{2,14},{3,15},{4,0},{5,1},{6,2},{7,3},{8,4},{9,5},{1... | collective-permute-start | bytes 786440 | tf_op jit(solution)/shard_map/ppermute | solution.py:351
  27.0 2.7 %collective-permute-done = bf16[128,2176]{1,0:T(8,128)(2,1)S(1)} collective-permute-done((bf16[128,2176]{1,0:T(8,128)(2,1)}, bf16[128,2176]{1,0:T(8,128)(2,1)S(1)}, u32[]{:S(2)}, u32[]{:S(2)}) %collective-permute-start) | collective-permute-done | bytes 557088 | tf_op jit(solution)/shard_map/ppermute | solution.py:351
  30.1 3.0 %collective-permute-start.3 = (bf16[64,2176]{1,0:T(8,128)(2,1)S(1)}, bf16[64,2176]{1,0:T(8,128)(2,1)S(1)}, u32[]{:S(2)}, u32[]{:S(2)}) collective-permute-start(bf16[64,2176]{1,0:T(8,128)(2,1)S(1)} %slice.179), channel_id=1, source_target_pairs={{0,3},{1,0},{2,1},{3,2},{4,7},{5,4},{6,5},{7,6},{8,11},{9,8},{10,9... | collective-permute-start | bytes 835592 | tf_op jit(solution)/shard_map/ppermute | solution.py:351
  34.4 3.8 %collective-permute-done.1 = bf16[64,2176]{1,0:T(8,128)(2,1)S(1)} collective-permute-done((bf16[64,2176]{1,0:T(8,128)(2,1)S(1)}, bf16[64,2176]{1,0:T(8,128)(2,1)S(1)}, u32[]{:S(2)}, u32[]{:S(2)}) %collective-permute-start.1) | collective-permute-done | bytes 278560 | tf_op jit(solution)/shard_map/ppermute | solution.py:351
  38.5 3.2 %collective-permute-start.9 = (bf16[256,2176]{1,0:T(8,128)(2,1)S(1)}, bf16[256,2176]{1,0:T(8,128)(2,1)}, u32[]{:S(2)}, u32[]{:S(2)}) collective-permute-start(bf16[256,2176]{1,0:T(8,128)(2,1)S(1)} %pad_maximum_fusion.refs_0_), channel_id=1, source_target_pairs={{0,12},{1,13},{2,14},{3,15},{4,0},{5,1},{6,2},{7,3},{8,4},{9,5},{1... | collective-permute-start | bytes 3342344 | tf_op jit(solution)/shard_map/ppermute | solution.py:351
  42.2 2.8 %collective-permute-start.11 = (bf16[256,2048]{1,0:T(8,128)(2,1)}, bf16[256,2048]{1,0:T(8,128)(2,1)}, u32[]{:S(2)}, u32[]{:S(2)}) collective-permute-start(bf16[256,2048]{1,0:T(8,128)(2,1)} %pad_maximum_fusion.2.refs_2_), channel_id=1, source_target_pairs={{0,3},{1,0},{2,1},{3,2},{4,7},{5,4},{6,5},{7,6},{8,11},{9,8},{10,9... | collective-permute-start | bytes 3145736 | tf_op jit(solution)/shard_map/ppermute | solution.py:351
  47.7 1.9 pad.9.rel.rel_x
  49.6 6.8 %turn.1.wt_hbm = bf16[2,1024,2048]{2,1,0:T(8,128)(2,1)} custom-call(bf16[2,2048,512]{2,1,0:T(8,128)(2,1)} %wg.3, bf16[2,2048,512]{2,1,0:T(8,128)(2,1)} %wu.3), custom_call_target="tpu_custom_call" | custom-call | flops 268435456 | bytes 524288 | tf_op jit(solution)/shard_map/turn/pallas_call | solution.py:136
  56.4 11.5 %stage.2 = (bf16[2,4,192,2048]{3,2,1,0:T(8,128)(2,1)}, bf16[2,4,192,512]{3,2,1,0:T(8,128)(2,1)}, bf16[2,4,192,512]{3,2,1,0:T(8,128)(2,1)}, bf16[2,4,192,512]{3,2...) custom-call(s32[4,4,256]{2,1,0:T(4,128)} %reshape.197.tgt_x.tgt, ...), custom_call_target="tpu_custom_call" | custom-call | flops 268435456 | bytes 524288 | tf_op jit(solution)/shard_map/stage/pallas_call | solution.py:107
  68.2 3.2 %collective-permute-start.19 = (bf16[256,2048]{1,0:T(8,128)(2,1)S(1)}, bf16[256,2048]{1,0:T(8,128)(2,1)S(1)}, u32[]{:S(2)}, u32[]{:S(2)}) collective-permute-start(bf16[256,2048]{1,0:T(8,128)(2,1)S(1)} %copy-done.5), channel_id=1, source_target_pairs={{0,3},{1,0},{2,1},{3,2},{4,7},{5,4},{6,5},{7,6},{8,11},{9,8},{10,9... | collective-permute-start | bytes 3145736 | tf_op jit(solution)/shard_map/ppermute | solution.py:351
  71.4 3.2 %collective-permute-start.17 = (bf16[256,2176]{1,0:T(8,128)(2,1)S(1)}, bf16[256,2176]{1,0:T(8,128)(2,1)S(1)}, u32[]{:S(2)}, u32[]{:S(2)}) collective-permute-start(bf16[256,2176]{1,0:T(8,128)(2,1)S(1)} %copy-done.1), channel_id=1, source_target_pairs={{0,12},{1,13},{2,14},{3,15},{4,0},{5,1},{6,2},{7,3},{8,4},{9,5},{1... | collective-permute-start | bytes 3342344 | tf_op jit(solution)/shard_map/ppermute | solution.py:351
  74.6 16.7 %collective-permute-done.18.refs_4_ = bf16[256,2048]{1,0:T(8,128)(2,1)S(1)} collective-permute-done((bf16[256,2048]{1,0:T(8,128)(2,1)}, bf16[256,2048]{1,0:T(8,128)(2,1)S(1)}, u32[]{:S(2)}, u32[]{:S(2)}) %collective-permute-start.18) | collective-permute-done | bytes 1048608 | tf_op jit(solution)/shard_map/ppermute | solution.py:351
  91.3 3.2 %collective-permute-start.14 = (bf16[256,2048]{1,0:T(8,128)(2,1)}, bf16[256,2048]{1,0:T(8,128)(2,1)S(1)}, u32[]{:S(2)}, u32[]{:S(2)}) collective-permute-start(bf16[256,2048]{1,0:T(8,128)(2,1)} %collective-permute-done.11.refs_6_), channel_id=1, source_target_pairs={{0,3},{1,0},{2,1},{3,2},{4,7},{5,4},{6,5},{7,6},{8,11},{9,8},{10,9... | collective-permute-start | bytes 3145736 | tf_op jit(solution)/shard_map/ppermute | solution.py:351
  95.4 4.2 %collective-permute-done.17.refs_3_ = bf16[256,2176]{1,0:T(8,128)(2,1)S(1)} collective-permute-done((bf16[256,2176]{1,0:T(8,128)(2,1)S(1)}, bf16[256,2176]{1,0:T(8,128)(2,1)S(1)}, u32[]{:S(2)}, u32[]{:S(2)}) %collective-permute-start.17) | collective-permute-done | bytes 1114144 | tf_op jit(solution)/shard_map/ppermute | solution.py:351
  100.6 17.0 %stage.3 = (bf16[2,4,192,2048]{3,2,1,0:T(8,128)(2,1)}, bf16[2,4,192,512]{3,2,1,0:T(8,128)(2,1)}, bf16[2,4,192,512]{3,2,1,0:T(8,128)(2,1)}, bf16[2,4,192,512]{3,2...) custom-call(s32[4,4,256]{2,1,0:T(4,128)} %reshape.197.tgt_x.tgt, ...), custom_call_target="tpu_custom_call", output_to_operand_aliasing={{0}: (14, {}), {1}: (15, {}), {2}: (16, {}), {3}: (17, {}),... | custom-call | flops 268435456 | bytes 524288 | tf_op jit(solution)/shard_map/stage/pallas_call | solution.py:107
  118.5 24.1 %tail.1 = (bf16[2,4,192,2048]{3,2,1,0:T(8,128)(2,1)}, bf16[2,4,192,512]{3,2,1,0:T(8,128)(2,1)}, bf16[2,4,4,48,2048]{4,3,2,1,0:T(8,128)(2,1)}, bf16[2,768,1024]{2,1,0:T(8,128)(2,1)}, bf16[4,4,128,2176]{3,2,1,0:T(8,128)(2,1)}) custom-call(s32[8]{0:T(128)} %pad_add_fusion.4.place, ...), custom_call_target="tpu_custom_call", output_to_operand_aliasing={{0}: (14, {}), {1}: (15, {}), {2}: (16, {})} | custom-call | flops 15032385536 | bytes 33554432 | tf_op jit(solution)/shard_map/tail/pallas_call | solution.py:230
  143.2 12.2 %up_grad.1 = (bf16[4,2,256,1024]{3,2,1,0:T(8,128)(2,1)}, bf16[4,2,256,1024]{3,2,1,0:T(8,128)(2,1)}) custom-call(s32[2]{0:T(128)} %pad_add_fusion.5.where, bf16[2,768,2048]{2,1,0:T(8,128)(2,1)} %bitcast.84, bf16[2,768,1024]{2,1,0:T(8,128)(2,1)} %get-tuple-element.87.dhu), custom_call_target="tpu_custom_call" | custom-call | flops 6442450944 | bytes 16777216 | tf_op jit(solution)/shard_map/up_grad/pallas_call | solution.py:302
  155.4 7.8 %down_grad.1 = (bf16[4,2,64,2048]{3,2,1,0:T(8,128)(2,1)}, bf16[4,2,64,2048]{3,2,1,0:T(8,128)(2,1)}) custom-call(s32[2]{0:T(128)} %pad_add_fusion.5.where, bf16[2,768,512]{2,1,0:T(8,128)(2,1)} %bitcast.87, bf16[2,768,2048]{2,1,0:T(8,128)(2,1)} %bitcast.85), custom_call_target="tpu_custom_call" | custom-call | flops 3221225472 | bytes 16777216 | tf_op jit(solution)/shard_map/down_grad/pallas_call | solution.py:302
  163.7 2.6 %fusion.9 = (bf16[1,256,1024]{2,1,0:T(8,128)(2,1)S(1)}, bf16[1,256,1024]{2,1,0:T(8,128)(2,1)S(1)}, bf16[256,1024]{1,0:T(8,128)(2,1)S(1)}, bf16[256,1024]{1,0:T(8,128)(2,1)S(1)}) fusion(bf16[4,2,256,1024]{3,2,1,0:T(8,128)(2,1)} %collective-permute-done.20, bf16[4,2,256,1024]{3,2,1,0:T(8,128)(2,1)S(1)} %copy-done.3), kind=kLoop, calls=%fused_computation.25 | loop fusion | flops 4194304 | bytes 6291456 | tf_op jit(solution)/shard_map/add | solution.py:325
  168.5 12.0 %collective-permute-done.22 = bf16[256,1024]{1,0:T(8,128)(2,1)S(1)} collective-permute-done((bf16[256,1024]{1,0:T(8,128)(2,1)S(1)}, bf16[256,1024]{1,0:T(8,128)(2,1)S(1)}, u32[]{:S(2)}, u32[]{:S(2)}) %collective-permute-start.22) | collective-permute-done | bytes 524320 | tf_op jit(solution)/shard_map/ppermute | solution.py:330
  182.6 1.7 collective-permute-start.28
  184.4 1.9 fusion.11
  188.6 3.0 %collective-permute-done.26 = bf16[64,2048]{1,0:T(8,128)(2,1)S(1)} collective-permute-done((bf16[64,2048]{1,0:T(8,128)(2,1)S(1)}, bf16[64,2048]{1,0:T(8,128)(2,1)S(1)}, u32[]{:S(2)}, u32[]{:S(2)}) %collective-permute-start.26) | collective-permute-done | bytes 262176 | tf_op jit(solution)/shard_map/ppermute | solution.py:330
  194.4 29.0 %collective-permute-done.27 = bf16[2,64,2048]{2,1,0:T(8,128)(2,1)S(1)} collective-permute-done((bf16[2,64,2048]{2,1,0:T(8,128)(2,1)S(1)}, bf16[2,64,2048]{2,1,0:T(8,128)(2,1)S(1)}, u32[]{:S(2)}, u32[]{:S(2)}) %collective-permute-start.27) | collective-permute-done | bytes 524320 | tf_op jit(solution)/shard_map/ppermute | solution.py:338
  226.1 2.2 fusion.1
  230.7 1.9 slice.182
  (116 shorter events, 25.7 us)
Async XLA Ops:
  7.2 222.1 %reduce-scatter.4.cloned.1.call-start = ((), (), s32[]{:S(2)}) async-start(), calls=%async_computation.1 | async-start | bytes 9469952
  7.2 16.2 %collective-permute-start.4 = (bf16[128,2048]{1,0:T(8,128)(2,1)}, bf16[128,2048]{1,0:T(8,128)(2,1)S(1)}, u32[]{:S(2)}, u32[]{:S(2)}) collective-permute-start(bf16[128,2048]{1,0:T(8,128)(2,1)} %param.9), channel_id=1, source_target_pairs={{0,4},{1,5},{2,6},{3,7},{4,8},{5,9},{6,10},{7,11},{8,12},{9,13},{1... | collective-permute-start | bytes 1572872 | tf_op jit(solution)/shard_map/ppermute | solution.py:351
  9.2 14.4 %collective-permute-start.6 = (bf16[128,2048]{1,0:T(8,128)(2,1)}, bf16[128,2048]{1,0:T(8,128)(2,1)S(1)}, u32[]{:S(2)}, u32[]{:S(2)}) collective-permute-start(bf16[128,2048]{1,0:T(8,128)(2,1)} %param.9), channel_id=1, source_target_pairs={{0,12},{1,13},{2,14},{3,15},{4,0},{5,1},{6,2},{7,3},{8,4},{9,5},{1... | collective-permute-start | bytes 1572872 | tf_op jit(solution)/shard_map/ppermute | solution.py:351
  14.1 15.6 %collective-permute-start = (bf16[128,2176]{1,0:T(8,128)(2,1)}, bf16[128,2176]{1,0:T(8,128)(2,1)S(1)}, u32[]{:S(2)}, u32[]{:S(2)}) collective-permute-start(bf16[128,2176]{1,0:T(8,128)(2,1)} %pad_maximum_fusion.6), channel_id=1, source_target_pairs={{0,1},{1,2},{2,3},{3,0},{4,5},{5,6},{6,7},{7,4},{8,9},{9,10},{10,1... | collective-permute-start | bytes 1671176 | tf_op jit(solution)/shard_map/ppermute | solution.py:351
  15.7 14.4 %collective-permute-start.2 = (bf16[128,2176]{1,0:T(8,128)(2,1)}, bf16[128,2176]{1,0:T(8,128)(2,1)S(1)}, u32[]{:S(2)}, u32[]{:S(2)}) collective-permute-start(bf16[128,2176]{1,0:T(8,128)(2,1)} %pad_maximum_fusion.6), channel_id=1, source_target_pairs={{0,3},{1,0},{2,1},{3,2},{4,7},{5,4},{6,5},{7,6},{8,11},{9,8},{10,9... | collective-permute-start | bytes 1671176 | tf_op jit(solution)/shard_map/ppermute | solution.py:351
  23.5 9.7 %collective-permute-start.5 = (bf16[64,2048]{1,0:T(8,128)(2,1)S(1)}, bf16[64,2048]{1,0:T(8,128)(2,1)S(1)}, u32[]{:S(2)}, u32[]{:S(2)}) collective-permute-start(bf16[64,2048]{1,0:T(8,128)(2,1)S(1)} %slice.180), channel_id=1, source_target_pairs={{0,4},{1,5},{2,6},{3,7},{4,8},{5,9},{6,10},{7,11},{8,12},{9,13},{1... | collective-permute-start | bytes 786440 | tf_op jit(solution)/shard_map/ppermute | solution.py:351
  23.6 9.6 %collective-permute-start.7 = (bf16[64,2048]{1,0:T(8,128)(2,1)S(1)}, bf16[64,2048]{1,0:T(8,128)(2,1)S(1)}, u32[]{:S(2)}, u32[]{:S(2)}) collective-permute-start(bf16[64,2048]{1,0:T(8,128)(2,1)S(1)} %slice.181), channel_id=1, source_target_pairs={{0,12},{1,13},{2,14},{3,15},{4,0},{5,1},{6,2},{7,3},{8,4},{9,5},{1... | collective-permute-start | bytes 786440 | tf_op jit(solution)/shard_map/ppermute | solution.py:351
  29.7 8.6 %collective-permute-start.1 = (bf16[64,2176]{1,0:T(8,128)(2,1)S(1)}, bf16[64,2176]{1,0:T(8,128)(2,1)S(1)}, u32[]{:S(2)}, u32[]{:S(2)}) collective-permute-start(bf16[64,2176]{1,0:T(8,128)(2,1)S(1)} %slice.178), channel_id=1, source_target_pairs={{0,1},{1,2},{2,3},{3,0},{4,5},{5,6},{6,7},{7,4},{8,9},{9,10},{10,1... | collective-permute-start | bytes 835592 | tf_op jit(solution)/shard_map/ppermute | solution.py:351
  30.1 8.1 %collective-permute-start.3 = (bf16[64,2176]{1,0:T(8,128)(2,1)S(1)}, bf16[64,2176]{1,0:T(8,128)(2,1)S(1)}, u32[]{:S(2)}, u32[]{:S(2)}) collective-permute-start(bf16[64,2176]{1,0:T(8,128)(2,1)S(1)} %slice.179), channel_id=1, source_target_pairs={{0,3},{1,0},{2,1},{3,2},{4,7},{5,4},{6,5},{7,6},{8,11},{9,8},{10,9... | collective-permute-start | bytes 835592 | tf_op jit(solution)/shard_map/ppermute | solution.py:351
  38.4 29.6 %collective-permute-start.8 = (bf16[256,2176]{1,0:T(8,128)(2,1)S(1)}, bf16[256,2176]{1,0:T(8,128)(2,1)}, u32[]{:S(2)}, u32[]{:S(2)}) collective-permute-start(bf16[256,2176]{1,0:T(8,128)(2,1)S(1)} %pad_maximum_fusion.1.refs_1_), channel_id=1, source_target_pairs={{0,4},{1,5},{2,6},{3,7},{4,8},{5,9},{6,10},{7,11},{8,12},{9,13},{1... | collective-permute-start | bytes 3342344 | tf_op jit(solution)/shard_map/ppermute | solution.py:351
  38.5 29.5 %collective-permute-start.9 = (bf16[256,2176]{1,0:T(8,128)(2,1)S(1)}, bf16[256,2176]{1,0:T(8,128)(2,1)}, u32[]{:S(2)}, u32[]{:S(2)}) collective-permute-start(bf16[256,2176]{1,0:T(8,128)(2,1)S(1)} %pad_maximum_fusion.refs_0_), channel_id=1, source_target_pairs={{0,12},{1,13},{2,14},{3,15},{4,0},{5,1},{6,2},{7,3},{8,4},{9,5},{1... | collective-permute-start | bytes 3342344 | tf_op jit(solution)/shard_map/ppermute | solution.py:351
  41.7 26.2 %collective-permute-start.10 = (bf16[256,2048]{1,0:T(8,128)(2,1)S(1)}, bf16[256,2048]{1,0:T(8,128)(2,1)}, u32[]{:S(2)}, u32[]{:S(2)}) collective-permute-start(bf16[256,2048]{1,0:T(8,128)(2,1)S(1)} %pad_maximum_fusion.3.refs_3_), channel_id=1, source_target_pairs={{0,1},{1,2},{2,3},{3,0},{4,5},{5,6},{6,7},{7,4},{8,9},{9,10},{10,1... | collective-permute-start | bytes 3145736 | tf_op jit(solution)/shard_map/ppermute | solution.py:351
  42.2 25.7 %collective-permute-start.11 = (bf16[256,2048]{1,0:T(8,128)(2,1)}, bf16[256,2048]{1,0:T(8,128)(2,1)}, u32[]{:S(2)}, u32[]{:S(2)}) collective-permute-start(bf16[256,2048]{1,0:T(8,128)(2,1)} %pad_maximum_fusion.2.refs_2_), channel_id=1, source_target_pairs={{0,3},{1,0},{2,1},{3,2},{4,7},{5,4},{6,5},{7,6},{8,11},{9,8},{10,9... | collective-permute-start | bytes 3145736 | tf_op jit(solution)/shard_map/ppermute | solution.py:351
  56.4 38.3 %copy-start.13 = (s32[4]{0:T(128)S(1)}, s32[4]{0:T(128)}, u32[]{:S(2)}) copy-start(s32[4]{0:T(128)} %constant.105.clone) | copy-start | bytes 52
  68.0 26.5 %collective-permute-start.16 = (bf16[256,2176]{1,0:T(8,128)(2,1)}, bf16[256,2176]{1,0:T(8,128)(2,1)S(1)}, u32[]{:S(2)}, u32[]{:S(2)}) collective-permute-start(bf16[256,2176]{1,0:T(8,128)(2,1)} %copy-done.2), channel_id=1, source_target_pairs={{0,4},{1,5},{2,6},{3,7},{4,8},{5,9},{6,10},{7,11},{8,12},{9,13},{1... | collective-permute-start | bytes 3342344 | tf_op jit(solution)/shard_map/ppermute | solution.py:351
  68.1 23.2 %collective-permute-start.18 = (bf16[256,2048]{1,0:T(8,128)(2,1)}, bf16[256,2048]{1,0:T(8,128)(2,1)S(1)}, u32[]{:S(2)}, u32[]{:S(2)}) collective-permute-start(bf16[256,2048]{1,0:T(8,128)(2,1)} %pad_maximum_fusion.2.refs_2_), channel_id=1, source_target_pairs={{0,1},{1,2},{2,3},{3,0},{4,5},{5,6},{6,7},{7,4},{8,9},{9,10},{10,1... | collective-permute-start | bytes 3145736 | tf_op jit(solution)/shard_map/ppermute | solution.py:351
  68.2 23.1 %collective-permute-start.19 = (bf16[256,2048]{1,0:T(8,128)(2,1)S(1)}, bf16[256,2048]{1,0:T(8,128)(2,1)S(1)}, u32[]{:S(2)}, u32[]{:S(2)}) collective-permute-start(bf16[256,2048]{1,0:T(8,128)(2,1)S(1)} %copy-done.5), channel_id=1, source_target_pairs={{0,3},{1,0},{2,1},{3,2},{4,7},{5,4},{6,5},{7,6},{8,11},{9,8},{10,9... | collective-permute-start | bytes 3145736 | tf_op jit(solution)/shard_map/ppermute | solution.py:351
  71.4 28.2 %collective-permute-start.17 = (bf16[256,2176]{1,0:T(8,128)(2,1)S(1)}, bf16[256,2176]{1,0:T(8,128)(2,1)S(1)}, u32[]{:S(2)}, u32[]{:S(2)}) collective-permute-start(bf16[256,2176]{1,0:T(8,128)(2,1)S(1)} %copy-done.1), channel_id=1, source_target_pairs={{0,12},{1,13},{2,14},{3,15},{4,0},{5,1},{6,2},{7,3},{8,4},{9,5},{1... | collective-permute-start | bytes 3342344 | tf_op jit(solution)/shard_map/ppermute | solution.py:351
  74.5 43.8 %collective-permute-start.12 = (bf16[256,2176]{1,0:T(8,128)(2,1)}, bf16[256,2176]{1,0:T(8,128)(2,1)}, u32[]{:S(2)}, u32[]{:S(2)}) collective-permute-start(bf16[256,2176]{1,0:T(8,128)(2,1)} %collective-permute-done.9.refs_2_), channel_id=1, source_target_pairs={{0,12},{1,13},{2,14},{3,15},{4,0},{5,1},{6,2},{7,3},{8,4},{9,5},{1... | collective-permute-start | bytes 3342344 | tf_op jit(solution)/shard_map/ppermute | solution.py:351
  91.3 27.0 %collective-permute-start.13 = (bf16[256,2176]{1,0:T(8,128)(2,1)}, bf16[256,2176]{1,0:T(8,128)(2,1)}, u32[]{:S(2)}, u32[]{:S(2)}) collective-permute-start(bf16[256,2176]{1,0:T(8,128)(2,1)} %collective-permute-done.8.refs_1_), channel_id=1, source_target_pairs={{0,4},{1,5},{2,6},{3,7},{4,8},{5,9},{6,10},{7,11},{8,12},{9,13},{1... | collective-permute-start | bytes 3342344 | tf_op jit(solution)/shard_map/ppermute | solution.py:351
  91.3 26.2 %collective-permute-start.14 = (bf16[256,2048]{1,0:T(8,128)(2,1)}, bf16[256,2048]{1,0:T(8,128)(2,1)S(1)}, u32[]{:S(2)}, u32[]{:S(2)}) collective-permute-start(bf16[256,2048]{1,0:T(8,128)(2,1)} %collective-permute-done.11.refs_6_), channel_id=1, source_target_pairs={{0,3},{1,0},{2,1},{3,2},{4,7},{5,4},{6,5},{7,6},{8,11},{9,8},{10,9... | collective-permute-start | bytes 3145736 | tf_op jit(solution)/shard_map/ppermute | solution.py:351
  94.5 23.1 %collective-permute-start.15 = (bf16[256,2048]{1,0:T(8,128)(2,1)}, bf16[256,2048]{1,0:T(8,128)(2,1)}, u32[]{:S(2)}, u32[]{:S(2)}) collective-permute-start(bf16[256,2048]{1,0:T(8,128)(2,1)} %collective-permute-done.10.refs_5_), channel_id=1, source_target_pairs={{0,1},{1,2},{2,3},{3,0},{4,5},{5,6},{6,7},{7,4},{8,9},{9,10},{10,1... | collective-permute-start | bytes 3145736 | tf_op jit(solution)/shard_map/ppermute | solution.py:351
  155.4 8.3 %collective-permute-start.20 = (bf16[4,2,256,1024]{3,2,1,0:T(8,128)(2,1)}, bf16[4,2,256,1024]{3,2,1,0:T(8,128)(2,1)}, u32[]{:S(2)}, u32[]{:S(2)}) collective-permute-start(bf16[4,2,256,1024]{3,2,1,0:T(8,128)(2,1)} %get-tuple-element.89), channel_id=1, source_target_pairs={{0,16},{16,0},{32,48},{48,32},{64,80},{80,64},{96,112},{112,96},{1... | collective-permute-start | bytes 12582920 | tf_op jit(solution)/shard_map/ppermute | solution.py:321
  163.2 5.3 %collective-permute-start.21 = (bf16[4,2,64,2048]{3,2,1,0:T(8,128)(2,1)}, bf16[4,2,64,2048]{3,2,1,0:T(8,128)(2,1)S(1)}, u32[]{:S(2)}, u32[]{:S(2)}) collective-permute-start(bf16[4,2,64,2048]{3,2,1,0:T(8,128)(2,1)} %get-tuple-element.92), channel_id=1, source_target_pairs={{0,16},{16,0},{32,48},{48,32},{64,80},{80,64},{96,112},{112,96},{1... | collective-permute-start | bytes 6291464 | tf_op jit(solution)/shard_map/ppermute | solution.py:321
  166.4 14.1 %collective-permute-start.22 = (bf16[256,1024]{1,0:T(8,128)(2,1)S(1)}, bf16[256,1024]{1,0:T(8,128)(2,1)S(1)}, u32[]{:S(2)}, u32[]{:S(2)}) collective-permute-start(bf16[256,1024]{1,0:T(8,128)(2,1)S(1)} %get-tuple-element.122), channel_id=1, source_target_pairs={{0,32},{16,48},{32,64},{48,80},{64,96},{80,112},{96,0},{112,16},{1... | collective-permute-start | bytes 1572872 | tf_op jit(solution)/shard_map/ppermute | solution.py:330
  166.9 15.0 %collective-permute-start.23 = (bf16[256,1024]{1,0:T(8,128)(2,1)S(1)}, bf16[256,1024]{1,0:T(8,128)(2,1)S(1)}, u32[]{:S(2)}, u32[]{:S(2)}) collective-permute-start(bf16[256,1024]{1,0:T(8,128)(2,1)S(1)} %get-tuple-element.121), channel_id=1, source_target_pairs={{0,96},{16,112},{32,0},{48,16},{64,32},{80,48},{96,64},{112,80},{1... | collective-permute-start | bytes 1572872 | tf_op jit(solution)/shard_map/ppermute | solution.py:331
  182.3 9.3 %collective-permute-start.26 = (bf16[64,2048]{1,0:T(8,128)(2,1)S(1)}, bf16[64,2048]{1,0:T(8,128)(2,1)S(1)}, u32[]{:S(2)}, u32[]{:S(2)}) collective-permute-start(bf16[64,2048]{1,0:T(8,128)(2,1)S(1)} %get-tuple-element.125), channel_id=1, source_target_pairs={{0,32},{16,48},{32,64},{48,80},{64,96},{80,112},{96,0},{112,16},{1... | collective-permute-start | bytes 786440 | tf_op jit(solution)/shard_map/ppermute | solution.py:330
  182.6 9.3 %collective-permute-start.28 = (bf16[64,2048]{1,0:T(8,128)(2,1)S(1)}, bf16[64,2048]{1,0:T(8,128)(2,1)S(1)}, u32[]{:S(2)}, u32[]{:S(2)}) collective-permute-start(bf16[64,2048]{1,0:T(8,128)(2,1)S(1)} %get-tuple-element.126), channel_id=1, source_target_pairs={{0,96},{16,112},{32,0},{48,16},{64,32},{80,48},{96,64},{112,80},{1... | collective-permute-start | bytes 786440 | tf_op jit(solution)/shard_map/ppermute | solution.py:331
  186.3 39.7 %collective-permute-start.24 = (bf16[2,256,1024]{2,1,0:T(8,128)(2,1)S(1)}, bf16[2,256,1024]{2,1,0:T(8,128)(2,1)S(1)}, u32[]{:S(2)}, u32[]{:S(2)}) collective-permute-start(bf16[2,256,1024]{2,1,0:T(8,128)(2,1)S(1)} %pad_maximum_fusion.4), channel_id=1, source_target_pairs={{0,32},{16,48},{32,64},{48,80},{64,96},{80,112},{96,0},{112,16},{1... | collective-permute-start | bytes 3145736 | tf_op jit(solution)/shard_map/ppermute | solution.py:338
  188.0 38.1 %collective-permute-start.25 = (bf16[2,256,1024]{2,1,0:T(8,128)(2,1)S(1)}, bf16[2,256,1024]{2,1,0:T(8,128)(2,1)S(1)}, u32[]{:S(2)}, u32[]{:S(2)}) collective-permute-start(bf16[2,256,1024]{2,1,0:T(8,128)(2,1)S(1)} %pad_maximum_fusion.5), channel_id=1, source_target_pairs={{0,96},{16,112},{32,0},{48,16},{64,32},{80,48},{96,64},{112,80},{1... | collective-permute-start | bytes 3145736 | tf_op jit(solution)/shard_map/ppermute | solution.py:338
  192.2 31.2 %collective-permute-start.27 = (bf16[2,64,2048]{2,1,0:T(8,128)(2,1)S(1)}, bf16[2,64,2048]{2,1,0:T(8,128)(2,1)S(1)}, u32[]{:S(2)}, u32[]{:S(2)}) collective-permute-start(bf16[2,64,2048]{2,1,0:T(8,128)(2,1)S(1)} %pad_maximum_fusion.7), channel_id=1, source_target_pairs={{0,32},{16,48},{32,64},{48,80},{64,96},{80,112},{96,0},{112,16},{1... | collective-permute-start | bytes 1572872 | tf_op jit(solution)/shard_map/ppermute | solution.py:338
  193.2 31.8 %collective-permute-start.29 = (bf16[2,64,2048]{2,1,0:T(8,128)(2,1)S(1)}, bf16[2,64,2048]{2,1,0:T(8,128)(2,1)S(1)}, u32[]{:S(2)}, u32[]{:S(2)}) collective-permute-start(bf16[2,64,2048]{2,1,0:T(8,128)(2,1)S(1)} %pad_maximum_fusion.8), channel_id=1, source_target_pairs={{0,96},{16,112},{32,0},{48,16},{64,32},{80,48},{96,64},{112,80},{1... | collective-permute-start | bytes 1572872 | tf_op jit(solution)/shard_map/ppermute | solution.py:338
  (14 other events, 124.0 us)
Sparse Core Ops, SparseCore 0:
  142.7 86.0 reduce-scatter.3

commit v4 on v3

--- a/solution.py
+++ b/solution.py
@@ -145,6 +145,10 @@
     )(wg, wu)
 
 
+def weight_copies(e, given, kept, sem):
+    return [pltpu.make_async_copy(g.at[e], k.at[e], sem.at[e, i]) for i, (g, k) in enumerate(zip(given, kept))]
+
+
 def held_copies(held, kept, wt_hbm, wt, sem):
     copies = [(wt_hbm.at[e], wt.at[e]) for e in range(2)]
     for i, (src, dst) in enumerate(zip(held, kept)):
@@ -154,10 +158,10 @@
     return [pltpu.make_async_copy(src, dst, sem.at[i]) for i, (src, dst) in enumerate(copies)]
 
 
-def tail_kernel(place, tgt_x, tgt_g, rel_x, tgt, rel, x_lo, x_hi, g_lo, g_hi, wg, wu, wd, wt_hbm, *refs):
-    held = refs[3:7]
-    xs, pa, gs, dhu, act, wt, ab, wp, hp, dap, probs_of, picked, dxs, qs, sem = refs[7:]
-    kept = (ab, wp, hp, dap)
+def tail_kernel(place, tgt_x, tgt_g, rel_x, tgt, rel, x_lo, x_hi, g_lo, g_hi, *refs):
+    given, wt_hbm, held = refs[:3], refs[3], refs[7:11]
+    xs, pa, gs, dhu, act, wg, wu, wd, wt, ab, wp, hp, dap, probs_of, picked, dxs, qs, weight_sem, sem = refs[11:]
+    own, kept = (wg, wu, wd), (ab, wp, hp, dap)
     half = 2 * PEER
     slots = CHUNK * PEER
     width, ff = wg.shape[1], wg.shape[2]
@@ -165,13 +169,23 @@
 
     @pl.when(step == 0)
     def _():
+        for e in range(2):
+            for copy in weight_copies(e, given, own, weight_sem):
+                copy.start()
         for copy in held_copies(held, kept, wt_hbm, wt, sem):
             copy.start()
         pick_rows(1, tgt_x, tgt_g, rel_x, (x_lo, x_hi), (g_lo, g_hi), xs, gs, probs_of, picked)
 
+    for e in range(2):
+
+        @pl.when(step == e)
+        def _():
+            for copy in weight_copies(e, given, own, weight_sem):
+                copy.wait()
+
     @pl.when(step < 2)
     def _():
-        made = products(xs[step, 0], picked[step], probs_of[step][:, :1], wg[0], wu[0], wd[0])
+        made = products(xs[step, 0], picked[step], probs_of[step][:, :1], wg[step], wu[step], wd[step])
         pa[0, 0] = made[0]
         for out, value in zip((ab, wp, hp), made[1:4]):
             out[step, 1] = value
@@ -225,7 +239,6 @@
     plane = lambda i: jnp.maximum(i - 2, 0)
     expert = lambda i: jnp.minimum(i, 1)
     of_plane = lambda *shape: pl.BlockSpec((1, *shape), lambda i, p: (plane(i), 0, 0))
-    of_expert = lambda w: pl.BlockSpec((1, *w.shape[1:]), lambda i, p: (expert(i), 0, 0))
     anywhere = pl.BlockSpec(memory_space=pl.ANY)
     return pl.pallas_call(
         tail_kernel,
@@ -240,8 +253,7 @@
                 of_plane(CHUNK * SRC, LANES),
             ]
             + [kept(v.shape, 0, 0) for v in (*x, *g)]
-            + [of_expert(w) for w in weights]
-            + [anywhere] * 8,
+            + [anywhere] * 11,
             out_specs=[
                 kept((2, 1, slots, width), 0, 1, 0, 0),
                 pl.BlockSpec((1, 1, slots, ff), lambda i, p: (expert(i), 1, 0, 0)),
@@ -249,7 +261,8 @@
                 pl.BlockSpec((2, slots, 2 * ff), lambda i, p: (0, plane(i), 0)),
                 pl.BlockSpec((1, 4, SRC, width + LANES), lambda i, p: (p[plane(i)], 0, 0, 0)),
             ],
-            scratch_shapes=[
+            scratch_shapes=[pltpu.VMEM(w.shape, BF16) for w in weights]
+            + [
                 pltpu.VMEM(wt.shape, BF16),
                 pltpu.VMEM(ab.shape, BF16),
                 pltpu.VMEM(wp.shape, BF16),
@@ -259,6 +272,7 @@
                 pltpu.VMEM((2, slots, width), BF16),
                 pltpu.VMEM((2, 4 * PEER, width), BF16),
                 pltpu.VMEM((2, 4 * PEER, LANES), BF16),
+                pltpu.SemaphoreType.DMA((2, 3)),
                 pltpu.SemaphoreType.DMA((10,)),
             ],
         ),
@@ -339,6 +353,22 @@
     return both(own, got, 0) + ahead.astype(F32) + back.astype(F32)
 
 
+def split_kernel(both, rows, probs):
+    width = rows.shape[1]
+    rows[...] = both[:, pl.ds(0, width)]
+    probs[...] = both[:, pl.ds(width, LANES)].astype(F32)[:, : probs.shape[1]]
+
+
+def split_pass(both, width):
+    count = both.shape[0]
+    return pl.pallas_call(
+        split_kernel,
+        out_shape=[jax.ShapeDtypeStruct((count, width), BF16), jax.ShapeDtypeStruct((count, TOP), F32)],
+        cost_estimate=pl.CostEstimate(flops=0, bytes_accessed=1 << 20, transcendentals=0),
+        name="split",
+    )(both)
+
+
 def along_y(by):
     return [(z * 4 + y, z * 4 + (y + by) % 4) for z in range(4) for y in range(4)]
 
@@ -352,10 +382,8 @@
 
 
 def gather_line(block, ring):
-    half = block.shape[0] // 2
-    back, ahead = send(block, ring(1)), send(block, ring(-1))
-    far = [send(back[:half], ring(1)), send(ahead[half:], ring(-1))]
-    return jnp.concatenate([block, *far], axis=0), jnp.concatenate([back, ahead], axis=0)
+    back, ahead, far = send(block, ring(1)), send(block, ring(-1)), send(block, ring(2))
+    return jnp.concatenate([block, far], axis=0), jnp.concatenate([back, ahead], axis=0)
 
 
 def tables(ids, first, my_z, my_y):
@@ -418,9 +446,10 @@
     far_down = send_far(down[1], got_down)
     grad_both = send_near(up[1], got_up, far_up)
     grad_down = send_near(down[1], got_down, far_down)
+    grad_act, grad_prob = split_pass(act_sum, width)
     return (
-        act_sum[:, :width],
-        act_sum[:, width : width + TOP].astype(F32),
+        grad_act,
+        grad_prob,
         grad_both[:, :, :ff].astype(BF16),
         grad_both[:, :, ff:].astype(BF16),
         grad_down.astype(BF16),

time: 240 us -> 250 us (1.042)
  Pallas kernels: 79.3 us -> 83.5 us
  waiting for transfers between devices: 80.6 us -> 83.7 us
  other arithmetic: 14.9 us -> 17.6 us
    concatenate x2, other arithmetic: 0.18 us -> 3.27 us  [gather_line(): jnp.concatenate([back, ahead], axis=0)]
    ppermute x20 -> x18, waiting for transfers between devices: 33.4 us -> 36.4 us  [send(): return lax.ppermute(value, 'expert', route)]
    slice x6 -> x0, local copies, waits for them, and re-layouts: 2.72 us -> none  [the longest x1 1.88 us: on_device(): act_sum[:, :width]]
    ppermute x20 -> x18, starting transfers between devices: 30.8 us -> 31.3 us  [send(): return lax.ppermute(value, 'expert', route)]
  transfers between devices with their start and end apart: 31 -> 29, of which waited for: 12 -> 13; matrix products, arithmetic and copies ran while one was open for 9% -> 9% of each run, Pallas kernels for 23% -> 22%
where the time goes in v4:
time: 250 us; the launch traced here: 249 us
  waiting for transfers between devices  83.7 us (33%)
  Pallas kernels  83.5 us (33%)
  starting transfers between devices  40.4 us (16%)
  other arithmetic  17.6 us (7%)
  between operations  14.4 us (6%)
  local copies, waits for them, and re-layouts  9.57 us (4%)
    ppermute x18, waiting for transfers between devices, send(): return lax.ppermute(value, 'expert', route)  36.4 us
    ppermute x18, starting transfers between devices, send(): return lax.ppermute(value, 'expert', route)  31.3 us
    ppermute x2, waiting for transfers between devices, send_near(): lax.ppermute(ahead, 'dp', along_x(1))  29 us
    pallas_call x2, Pallas kernels, stage_pass(): pl.pallas_call(functools.partial(stage_kernel, n), grid=(2,), in_specs=[f...  28.4 us
    pallas_call x1, Pallas kernels, tail_pass(): pl.pallas_call(tail_kernel, grid_spec=pltpu.PrefetchScalarGridSpec(num_sc...  26.4 us
    pallas_call x2, Pallas kernels, weight_pass(): pl.pallas_call(body, grid=(2,), in_specs=[pl.BlockSpec(memory_space=pltpu...  20 us
    ppermute x2, waiting for transfers between devices, send_far(): lax.ppermute(both(own, got, 2, 0).astype(BF16), 'dp', along_x(1))  15 us
    pallas_call x1, Pallas kernels, turn_pass(): pl.pallas_call(turn_kernel, grid=(2,), in_specs=[by_expert((width, ff), 0...  6.78 us
  transfers between devices with their start and end apart: 29, of which 13 were waited for; matrix products, arithmetic and copies ran while one was open for 9% of the time, Pallas kernels for 22%

profile of v4, /device:TPU:6, one launch (start us, length us, event | category | flops | bytes accessed | tf_op | source)
XLA Modules:
  0.0 249.2 jit_solution(16370182274141090997)
XLA Ops:
  7.2 4.0 %collective-permute-start.3 = (bf16[128,2048]{1,0:T(8,128)(2,1)}, bf16[128,2048]{1,0:T(8,128)(2,1)S(1)}, u32[]{:S(2)}, u32[]{:S(2)}) collective-permute-start(bf16[128,2048]{1,0:T(8,128)(2,1)} %param.9), channel_id=1, source_target_pairs={{0,8},{1,9},{2,10},{3,11},{4,12},{5,13},{6,14},{7,15},{8,0},{9,1},... | collective-permute-start | bytes 1572872 | tf_op jit(solution)/shard_map/ppermute | solution.py:381
  13.1 1.6 collective-permute-start.1
  14.7 2.9 %collective-permute-start = (bf16[128,2176]{1,0:T(8,128)(2,1)S(1)}, bf16[128,2176]{1,0:T(8,128)(2,1)}, u32[]{:S(2)}, u32[]{:S(2)}) collective-permute-start(bf16[128,2176]{1,0:T(8,128)(2,1)S(1)} %pad_maximum_fusion.6), channel_id=1, source_target_pairs={{0,2},{1,3},{2,0},{3,1},{4,6},{5,7},{6,4},{7,5},{8,10},{9,11},{10,... | collective-permute-start | bytes 1671176 | tf_op jit(solution)/shard_map/ppermute | solution.py:381
  18.6 2.2 collective-permute-start.5
  21.8 2.4 collective-permute-done.3
  24.2 3.0 %collective-permute-start.2 = (bf16[128,2176]{1,0:T(8,128)(2,1)S(1)}, bf16[128,2176]{1,0:T(8,128)(2,1)S(1)}, u32[]{:S(2)}, u32[]{:S(2)}) collective-permute-start(bf16[128,2176]{1,0:T(8,128)(2,1)S(1)} %pad_maximum_fusion.6), channel_id=1, source_target_pairs={{0,3},{1,0},{2,1},{3,2},{4,7},{5,4},{6,5},{7,6},{8,11},{9,8},{10,9... | collective-permute-start | bytes 1671176 | tf_op jit(solution)/shard_map/ppermute | solution.py:381
  28.3 6.2 %collective-permute-done.4 = bf16[128,2048]{1,0:T(8,128)(2,1)S(1)} collective-permute-done((bf16[128,2048]{1,0:T(8,128)(2,1)}, bf16[128,2048]{1,0:T(8,128)(2,1)S(1)}, u32[]{:S(2)}, u32[]{:S(2)}) %collective-permute-start.4) | collective-permute-done | bytes 524320 | tf_op jit(solution)/shard_map/ppermute | solution.py:381
  35.4 2.1 pad_maximum_fusion.3.refs_3_
  37.6 4.2 %collective-permute-done = bf16[128,2176]{1,0:T(8,128)(2,1)} collective-permute-done((bf16[128,2176]{1,0:T(8,128)(2,1)S(1)}, bf16[128,2176]{1,0:T(8,128)(2,1)}, u32[]{:S(2)}, u32[]{:S(2)}) %collective-permute-start) | collective-permute-done | bytes 557088 | tf_op jit(solution)/shard_map/ppermute | solution.py:381
  46.0 2.2 collective-permute-start.7
  48.3 3.2 %collective-permute-start.9 = (bf16[256,2048]{1,0:T(8,128)(2,1)S(1)}, bf16[256,2048]{1,0:T(8,128)(2,1)}, u32[]{:S(2)}, u32[]{:S(2)}) collective-permute-start(bf16[256,2048]{1,0:T(8,128)(2,1)S(1)} %pad_maximum_fusion.2.refs_2_), channel_id=1, source_target_pairs={{0,3},{1,0},{2,1},{3,2},{4,7},{5,4},{6,5},{7,6},{8,11},{9,8},{10,9... | collective-permute-start | bytes 3145736 | tf_op jit(solution)/shard_map/ppermute | solution.py:381
  54.2 1.9 pad.9.rel.rel_x
  56.1 6.8 %turn.1.refs_3_ = bf16[2,1024,2048]{2,1,0:T(8,128)(2,1)} custom-call(bf16[2,2048,512]{2,1,0:T(8,128)(2,1)} %refs_0_.1, bf16[2,2048,512]{2,1,0:T(8,128)(2,1)} %refs_1_.1), custom_call_target="tpu_custom_call" | custom-call | flops 268435456 | bytes 524288 | tf_op jit(solution)/shard_map/turn/pallas_call | solution.py:136
  63.0 11.5 %stage.2 = (bf16[2,4,192,2048]{3,2,1,0:T(8,128)(2,1)}, bf16[2,4,192,512]{3,2,1,0:T(8,128)(2,1)}, bf16[2,4,192,512]{3,2,1,0:T(8,128)(2,1)}, bf16[2,4,192,512]{3,2...) custom-call(s32[4,4,256]{2,1,0:T(4,128)} %reshape.197.tgt_x.tgt, ...), custom_call_target="tpu_custom_call" | custom-call | flops 268435456 | bytes 524288 | tf_op jit(solution)/shard_map/stage/pallas_call | solution.py:107
  74.7 3.2 %collective-permute-start.17 = (bf16[256,2048]{1,0:T(8,128)(2,1)}, bf16[256,2048]{1,0:T(8,128)(2,1)S(1)}, u32[]{:S(2)}, u32[]{:S(2)}) collective-permute-start(bf16[256,2048]{1,0:T(8,128)(2,1)} %pad_maximum_fusion.3.refs_3_), channel_id=1, source_target_pairs={{0,3},{1,0},{2,1},{3,2},{4,7},{5,4},{6,5},{7,6},{8,11},{9,8},{10,9... | collective-permute-start | bytes 3145736 | tf_op jit(solution)/shard_map/ppermute | solution.py:381
  77.9 3.1 %collective-permute-start.15 = (bf16[256,2176]{1,0:T(8,128)(2,1)}, bf16[256,2176]{1,0:T(8,128)(2,1)S(1)}, u32[]{:S(2)}, u32[]{:S(2)}) collective-permute-start(bf16[256,2176]{1,0:T(8,128)(2,1)} %copy-done), channel_id=1, source_target_pairs={{0,12},{1,13},{2,14},{3,15},{4,0},{5,1},{6,2},{7,3},{8,4},{9,5},{1... | collective-permute-start | bytes 3342344 | tf_op jit(solution)/shard_map/ppermute | solution.py:381
  81.1 17.4 %collective-permute-done.16.refs_4_ = bf16[256,2048]{1,0:T(8,128)(2,1)S(1)} collective-permute-done((bf16[256,2048]{1,0:T(8,128)(2,1)S(1)}, bf16[256,2048]{1,0:T(8,128)(2,1)S(1)}, u32[]{:S(2)}, u32[]{:S(2)}) %collective-permute-start.16) | collective-permute-done | bytes 1048608 | tf_op jit(solution)/shard_map/ppermute | solution.py:381
  98.5 3.1 %collective-permute-start.12 = (bf16[256,2048]{1,0:T(8,128)(2,1)}, bf16[256,2048]{1,0:T(8,128)(2,1)S(1)}, u32[]{:S(2)}, u32[]{:S(2)}) collective-permute-start(bf16[256,2048]{1,0:T(8,128)(2,1)} %collective-permute-done.9.refs_6_), channel_id=1, source_target_pairs={{0,3},{1,0},{2,1},{3,2},{4,7},{5,4},{6,5},{7,6},{8,11},{9,8},{10,9... | collective-permute-start | bytes 3145736 | tf_op jit(solution)/shard_map/ppermute | solution.py:381
  102.5 3.8 %collective-permute-done.15.refs_3_ = bf16[256,2176]{1,0:T(8,128)(2,1)S(1)} collective-permute-done((bf16[256,2176]{1,0:T(8,128)(2,1)}, bf16[256,2176]{1,0:T(8,128)(2,1)S(1)}, u32[]{:S(2)}, u32[]{:S(2)}) %collective-permute-start.15) | collective-permute-done | bytes 1114144 | tf_op jit(solution)/shard_map/ppermute | solution.py:381
  107.4 17.0 %stage.3 = (bf16[2,4,192,2048]{3,2,1,0:T(8,128)(2,1)}, bf16[2,4,192,512]{3,2,1,0:T(8,128)(2,1)}, bf16[2,4,192,512]{3,2,1,0:T(8,128)(2,1)}, bf16[2,4,192,512]{3,2...) custom-call(s32[4,4,256]{2,1,0:T(4,128)} %reshape.197.tgt_x.tgt, ...), custom_call_target="tpu_custom_call", output_to_operand_aliasing={{0}: (14, {}), {1}: (15, {}), {2}: (16, {}), {3}: (17, {}),... | custom-call | flops 268435456 | bytes 524288 | tf_op jit(solution)/shard_map/stage/pallas_call | solution.py:107
  125.9 26.4 %tail.1 = (bf16[2,4,192,2048]{3,2,1,0:T(8,128)(2,1)}, bf16[2,4,192,512]{3,2,1,0:T(8,128)(2,1)}, bf16[2,4,4,48,2048]{4,3,2,1,0:T(8,128)(2,1)}, bf16[2,768,1024]{2,1,0:T(8,128)(2,1)}, bf16[4,4,128,2176]{3,2,1,0:T(8,128)(2,1)}) custom-call(s32[8]{0:T(128)} %pad_add_fusion.4.place, ...), custom_call_target="tpu_custom_call", output_to_operand_aliasing={{0}: (14, {}), {1}: (15, {}), {2}: (16, {})} | custom-call | flops 15032385536 | bytes 33554432 | tf_op jit(solution)/shard_map/tail/pallas_call | solution.py:243
  153.0 12.2 %up_grad.1 = (bf16[4,2,256,1024]{3,2,1,0:T(8,128)(2,1)}, bf16[4,2,256,1024]{3,2,1,0:T(8,128)(2,1)}) custom-call(s32[2]{0:T(128)} %pad_add_fusion.5.where, bf16[2,768,2048]{2,1,0:T(8,128)(2,1)} %bitcast.83, bf16[2,768,1024]{2,1,0:T(8,128)(2,1)} %get-tuple-element.91.dhu), custom_call_target="tpu_custom_call" | custom-call | flops 6442450944 | bytes 16777216 | tf_op jit(solution)/shard_map/up_grad/pallas_call | solution.py:316
  165.2 7.8 %down_grad.1 = (bf16[4,2,64,2048]{3,2,1,0:T(8,128)(2,1)}, bf16[4,2,64,2048]{3,2,1,0:T(8,128)(2,1)}) custom-call(s32[2]{0:T(128)} %pad_add_fusion.5.where, bf16[2,768,512]{2,1,0:T(8,128)(2,1)} %bitcast.86, bf16[2,768,2048]{2,1,0:T(8,128)(2,1)} %bitcast.84), custom_call_target="tpu_custom_call" | custom-call | flops 3221225472 | bytes 16777216 | tf_op jit(solution)/shard_map/down_grad/pallas_call | solution.py:316
  173.5 2.6 %fusion.9 = (bf16[1,256,1024]{2,1,0:T(8,128)(2,1)S(1)}, bf16[1,256,1024]{2,1,0:T(8,128)(2,1)S(1)}, bf16[256,1024]{1,0:T(8,128)(2,1)S(1)}, bf16[256,1024]{1,0:T(8,128)(2,1)S(1)}) fusion(bf16[4,2,256,1024]{3,2,1,0:T(8,128)(2,1)} %collective-permute-done.18, bf16[4,2,256,1024]{3,2,1,0:T(8,128)(2,1)S(1)} %copy-done.3), kind=kLoop, calls=%fused_computation.25 | loop fusion | flops 4194304 | bytes 6291456 | tf_op jit(solution)/shard_map/add | solution.py:339
  176.7 1.6 collective-permute-start.21
  178.2 12.0 %collective-permute-done.20 = bf16[256,1024]{1,0:T(8,128)(2,1)S(1)} collective-permute-done((bf16[256,1024]{1,0:T(8,128)(2,1)S(1)}, bf16[256,1024]{1,0:T(8,128)(2,1)S(1)}, u32[]{:S(2)}, u32[]{:S(2)}) %collective-permute-start.20) | collective-permute-done | bytes 524320 | tf_op jit(solution)/shard_map/ppermute | solution.py:344
  192.3 1.7 collective-permute-start.26
  194.1 1.8 fusion.11
  198.3 3.0 %collective-permute-done.24 = bf16[64,2048]{1,0:T(8,128)(2,1)S(1)} collective-permute-done((bf16[64,2048]{1,0:T(8,128)(2,1)S(1)}, bf16[64,2048]{1,0:T(8,128)(2,1)S(1)}, u32[]{:S(2)}, u32[]{:S(2)}) %collective-permute-start.24) | collective-permute-done | bytes 262176 | tf_op jit(solution)/shard_map/ppermute | solution.py:344
  204.1 29.0 %collective-permute-done.25 = bf16[2,64,2048]{2,1,0:T(8,128)(2,1)S(1)} collective-permute-done((bf16[2,64,2048]{2,1,0:T(8,128)(2,1)S(1)}, bf16[2,64,2048]{2,1,0:T(8,128)(2,1)S(1)}, u32[]{:S(2)}, u32[]{:S(2)}) %collective-permute-start.25) | collective-permute-done | bytes 524320 | tf_op jit(solution)/shard_map/ppermute | solution.py:352
  235.8 2.2 fusion.1
  239.0 1.9 split.1
  (108 shorter events, 30.6 us)
Async XLA Ops:
  7.2 231.8 %reduce-scatter.2.cloned.1.call-start = ((), (), s32[]{:S(2)}) async-start(), calls=%async_computation.1 | async-start | bytes 9469952 | tf_op jit(solution)/shard_map/reduce_scatter | solution.py:438
  7.2 17.0 %collective-permute-start.3 = (bf16[128,2048]{1,0:T(8,128)(2,1)}, bf16[128,2048]{1,0:T(8,128)(2,1)S(1)}, u32[]{:S(2)}, u32[]{:S(2)}) collective-permute-start(bf16[128,2048]{1,0:T(8,128)(2,1)} %param.9), channel_id=1, source_target_pairs={{0,8},{1,9},{2,10},{3,11},{4,12},{5,13},{6,14},{7,15},{8,0},{9,1},... | collective-permute-start | bytes 1572872 | tf_op jit(solution)/shard_map/ppermute | solution.py:381
  13.1 29.8 %collective-permute-start.1 = (bf16[128,2176]{1,0:T(8,128)(2,1)S(1)}, bf16[128,2176]{1,0:T(8,128)(2,1)S(1)}, u32[]{:S(2)}, u32[]{:S(2)}) collective-permute-start(bf16[128,2176]{1,0:T(8,128)(2,1)S(1)} %pad_maximum_fusion.6), channel_id=1, source_target_pairs={{0,1},{1,2},{2,3},{3,0},{4,5},{5,6},{6,7},{7,4},{8,9},{9,10},{10,1... | collective-permute-start | bytes 1671176 | tf_op jit(solution)/shard_map/ppermute | solution.py:381
  14.7 27.0 %collective-permute-start = (bf16[128,2176]{1,0:T(8,128)(2,1)S(1)}, bf16[128,2176]{1,0:T(8,128)(2,1)}, u32[]{:S(2)}, u32[]{:S(2)}) collective-permute-start(bf16[128,2176]{1,0:T(8,128)(2,1)S(1)} %pad_maximum_fusion.6), channel_id=1, source_target_pairs={{0,2},{1,3},{2,0},{3,1},{4,6},{5,7},{6,4},{7,5},{8,10},{9,11},{10,... | collective-permute-start | bytes 1671176 | tf_op jit(solution)/shard_map/ppermute | solution.py:381
  17.6 16.9 %collective-permute-start.4 = (bf16[128,2048]{1,0:T(8,128)(2,1)}, bf16[128,2048]{1,0:T(8,128)(2,1)S(1)}, u32[]{:S(2)}, u32[]{:S(2)}) collective-permute-start(bf16[128,2048]{1,0:T(8,128)(2,1)} %param.9), channel_id=1, source_target_pairs={{0,4},{1,5},{2,6},{3,7},{4,8},{5,9},{6,10},{7,11},{8,12},{9,13},{1... | collective-permute-start | bytes 1572872 | tf_op jit(solution)/shard_map/ppermute | solution.py:381
  18.6 16.8 %collective-permute-start.5 = (bf16[128,2048]{1,0:T(8,128)(2,1)}, bf16[128,2048]{1,0:T(8,128)(2,1)}, u32[]{:S(2)}, u32[]{:S(2)}) collective-permute-start(bf16[128,2048]{1,0:T(8,128)(2,1)} %param.9), channel_id=1, source_target_pairs={{0,12},{1,13},{2,14},{3,15},{4,0},{5,1},{6,2},{7,3},{8,4},{9,5},{1... | collective-permute-start | bytes 1572872 | tf_op jit(solution)/shard_map/ppermute | solution.py:381
  21.8 20.0 %copy-start.7 = (bf16[128,2048]{1,0:T(8,128)(2,1)S(1)}, bf16[128,2048]{1,0:T(8,128)(2,1)}, u32[]{:S(2)}) copy-start(bf16[128,2048]{1,0:T(8,128)(2,1)} %param.8) | copy-start | bytes 1572868
  24.2 19.6 %collective-permute-start.2 = (bf16[128,2176]{1,0:T(8,128)(2,1)S(1)}, bf16[128,2176]{1,0:T(8,128)(2,1)S(1)}, u32[]{:S(2)}, u32[]{:S(2)}) collective-permute-start(bf16[128,2176]{1,0:T(8,128)(2,1)S(1)} %pad_maximum_fusion.6), channel_id=1, source_target_pairs={{0,3},{1,0},{2,1},{3,2},{4,7},{5,4},{6,5},{7,6},{8,11},{9,8},{10,9... | collective-permute-start | bytes 1671176 | tf_op jit(solution)/shard_map/ppermute | solution.py:381
  28.3 20.0 %copy-start.4 = (bf16[256,2048]{1,0:T(8,128)(2,1)}, bf16[256,2048]{1,0:T(8,128)(2,1)S(1)}, u32[]{:S(2)}) copy-start(bf16[256,2048]{1,0:T(8,128)(2,1)S(1)} %pad_maximum_fusion.2.refs_2_) | copy-start | bytes 3145732
  44.9 29.6 %collective-permute-start.6 = (bf16[256,2176]{1,0:T(8,128)(2,1)S(1)}, bf16[256,2176]{1,0:T(8,128)(2,1)}, u32[]{:S(2)}, u32[]{:S(2)}) collective-permute-start(bf16[256,2176]{1,0:T(8,128)(2,1)S(1)} %pad_maximum_fusion.1.refs_1_), channel_id=1, source_target_pairs={{0,4},{1,5},{2,6},{3,7},{4,8},{5,9},{6,10},{7,11},{8,12},{9,13},{1... | collective-permute-start | bytes 3342344 | tf_op jit(solution)/shard_map/ppermute | solution.py:381
  46.0 28.5 %collective-permute-start.7 = (bf16[256,2176]{1,0:T(8,128)(2,1)S(1)}, bf16[256,2176]{1,0:T(8,128)(2,1)}, u32[]{:S(2)}, u32[]{:S(2)}) collective-permute-start(bf16[256,2176]{1,0:T(8,128)(2,1)S(1)} %pad_maximum_fusion.refs_0_), channel_id=1, source_target_pairs={{0,12},{1,13},{2,14},{3,15},{4,0},{5,1},{6,2},{7,3},{8,4},{9,5},{1... | collective-permute-start | bytes 3342344 | tf_op jit(solution)/shard_map/ppermute | solution.py:381
  48.2 26.2 %collective-permute-start.8 = (bf16[256,2048]{1,0:T(8,128)(2,1)}, bf16[256,2048]{1,0:T(8,128)(2,1)}, u32[]{:S(2)}, u32[]{:S(2)}) collective-permute-start(bf16[256,2048]{1,0:T(8,128)(2,1)} %pad_maximum_fusion.3.refs_3_), channel_id=1, source_target_pairs={{0,1},{1,2},{2,3},{3,0},{4,5},{5,6},{6,7},{7,4},{8,9},{9,10},{10,1... | collective-permute-start | bytes 3145736 | tf_op jit(solution)/shard_map/ppermute | solution.py:381
  48.3 26.1 %collective-permute-start.9 = (bf16[256,2048]{1,0:T(8,128)(2,1)S(1)}, bf16[256,2048]{1,0:T(8,128)(2,1)}, u32[]{:S(2)}, u32[]{:S(2)}) collective-permute-start(bf16[256,2048]{1,0:T(8,128)(2,1)S(1)} %pad_maximum_fusion.2.refs_2_), channel_id=1, source_target_pairs={{0,3},{1,0},{2,1},{3,2},{4,7},{5,4},{6,5},{7,6},{8,11},{9,8},{10,9... | collective-permute-start | bytes 3145736 | tf_op jit(solution)/shard_map/ppermute | solution.py:381
  62.9 39.0 %copy-start.13 = (s32[4]{0:T(128)S(1)}, s32[4]{0:T(128)}, u32[]{:S(2)}) copy-start(s32[4]{0:T(128)} %constant.105.clone) | copy-start | bytes 52
  74.5 27.2 %collective-permute-start.14 = (bf16[256,2176]{1,0:T(8,128)(2,1)S(1)}, bf16[256,2176]{1,0:T(8,128)(2,1)S(1)}, u32[]{:S(2)}, u32[]{:S(2)}) collective-permute-start(bf16[256,2176]{1,0:T(8,128)(2,1)S(1)} %copy-done.2), channel_id=1, source_target_pairs={{0,4},{1,5},{2,6},{3,7},{4,8},{5,9},{6,10},{7,11},{8,12},{9,13},{1... | collective-permute-start | bytes 3342344 | tf_op jit(solution)/shard_map/ppermute | solution.py:381
  74.6 23.9 %collective-permute-start.16 = (bf16[256,2048]{1,0:T(8,128)(2,1)S(1)}, bf16[256,2048]{1,0:T(8,128)(2,1)S(1)}, u32[]{:S(2)}, u32[]{:S(2)}) collective-permute-start(bf16[256,2048]{1,0:T(8,128)(2,1)S(1)} %copy-done.5), channel_id=1, source_target_pairs={{0,1},{1,2},{2,3},{3,0},{4,5},{5,6},{6,7},{7,4},{8,9},{9,10},{10,1... | collective-permute-start | bytes 3145736 | tf_op jit(solution)/shard_map/ppermute | solution.py:381
  74.7 23.8 %collective-permute-start.17 = (bf16[256,2048]{1,0:T(8,128)(2,1)}, bf16[256,2048]{1,0:T(8,128)(2,1)S(1)}, u32[]{:S(2)}, u32[]{:S(2)}) collective-permute-start(bf16[256,2048]{1,0:T(8,128)(2,1)} %pad_maximum_fusion.3.refs_3_), channel_id=1, source_target_pairs={{0,3},{1,0},{2,1},{3,2},{4,7},{5,4},{6,5},{7,6},{8,11},{9,8},{10,9... | collective-permute-start | bytes 3145736 | tf_op jit(solution)/shard_map/ppermute | solution.py:381
  77.9 28.5 %collective-permute-start.15 = (bf16[256,2176]{1,0:T(8,128)(2,1)}, bf16[256,2176]{1,0:T(8,128)(2,1)S(1)}, u32[]{:S(2)}, u32[]{:S(2)}) collective-permute-start(bf16[256,2176]{1,0:T(8,128)(2,1)} %copy-done), channel_id=1, source_target_pairs={{0,12},{1,13},{2,14},{3,15},{4,0},{5,1},{6,2},{7,3},{8,4},{9,5},{1... | collective-permute-start | bytes 3342344 | tf_op jit(solution)/shard_map/ppermute | solution.py:381
  81.0 44.9 %collective-permute-start.10 = (bf16[256,2176]{1,0:T(8,128)(2,1)}, bf16[256,2176]{1,0:T(8,128)(2,1)}, u32[]{:S(2)}, u32[]{:S(2)}) collective-permute-start(bf16[256,2176]{1,0:T(8,128)(2,1)} %collective-permute-done.7.refs_2_), channel_id=1, source_target_pairs={{0,12},{1,13},{2,14},{3,15},{4,0},{5,1},{6,2},{7,3},{8,4},{9,5},{1... | collective-permute-start | bytes 3342344 | tf_op jit(solution)/shard_map/ppermute | solution.py:381
  98.5 27.4 %collective-permute-start.11 = (bf16[256,2176]{1,0:T(8,128)(2,1)}, bf16[256,2176]{1,0:T(8,128)(2,1)}, u32[]{:S(2)}, u32[]{:S(2)}) collective-permute-start(bf16[256,2176]{1,0:T(8,128)(2,1)} %collective-permute-done.6.refs_1_), channel_id=1, source_target_pairs={{0,4},{1,5},{2,6},{3,7},{4,8},{5,9},{6,10},{7,11},{8,12},{9,13},{1... | collective-permute-start | bytes 3342344 | tf_op jit(solution)/shard_map/ppermute | solution.py:381
  98.5 25.9 %collective-permute-start.12 = (bf16[256,2048]{1,0:T(8,128)(2,1)}, bf16[256,2048]{1,0:T(8,128)(2,1)S(1)}, u32[]{:S(2)}, u32[]{:S(2)}) collective-permute-start(bf16[256,2048]{1,0:T(8,128)(2,1)} %collective-permute-done.9.refs_6_), channel_id=1, source_target_pairs={{0,3},{1,0},{2,1},{3,2},{4,7},{5,4},{6,5},{7,6},{8,11},{9,8},{10,9... | collective-permute-start | bytes 3145736 | tf_op jit(solution)/shard_map/ppermute | solution.py:381
  101.7 22.8 %collective-permute-start.13 = (bf16[256,2048]{1,0:T(8,128)(2,1)}, bf16[256,2048]{1,0:T(8,128)(2,1)S(1)}, u32[]{:S(2)}, u32[]{:S(2)}) collective-permute-start(bf16[256,2048]{1,0:T(8,128)(2,1)} %collective-permute-done.8.refs_5_), channel_id=1, source_target_pairs={{0,1},{1,2},{2,3},{3,0},{4,5},{5,6},{6,7},{7,4},{8,9},{9,10},{10,1... | collective-permute-start | bytes 3145736 | tf_op jit(solution)/shard_map/ppermute | solution.py:381
  165.1 8.3 %collective-permute-start.18 = (bf16[4,2,256,1024]{3,2,1,0:T(8,128)(2,1)}, bf16[4,2,256,1024]{3,2,1,0:T(8,128)(2,1)}, u32[]{:S(2)}, u32[]{:S(2)}) collective-permute-start(bf16[4,2,256,1024]{3,2,1,0:T(8,128)(2,1)} %get-tuple-element.93), channel_id=1, source_target_pairs={{0,16},{16,0},{32,48},{48,32},{64,80},{80,64},{96,112},{112,96},{1... | collective-permute-start | bytes 12582920 | tf_op jit(solution)/shard_map/ppermute | solution.py:335
  172.9 5.3 %collective-permute-start.19 = (bf16[4,2,64,2048]{3,2,1,0:T(8,128)(2,1)}, bf16[4,2,64,2048]{3,2,1,0:T(8,128)(2,1)S(1)}, u32[]{:S(2)}, u32[]{:S(2)}) collective-permute-start(bf16[4,2,64,2048]{3,2,1,0:T(8,128)(2,1)} %get-tuple-element.96), channel_id=1, source_target_pairs={{0,16},{16,0},{32,48},{48,32},{64,80},{80,64},{96,112},{112,96},{1... | collective-permute-start | bytes 6291464 | tf_op jit(solution)/shard_map/ppermute | solution.py:335
  176.1 14.1 %collective-permute-start.20 = (bf16[256,1024]{1,0:T(8,128)(2,1)S(1)}, bf16[256,1024]{1,0:T(8,128)(2,1)S(1)}, u32[]{:S(2)}, u32[]{:S(2)}) collective-permute-start(bf16[256,1024]{1,0:T(8,128)(2,1)S(1)} %get-tuple-element.126), channel_id=1, source_target_pairs={{0,32},{16,48},{32,64},{48,80},{64,96},{80,112},{96,0},{112,16},{1... | collective-permute-start | bytes 1572872 | tf_op jit(solution)/shard_map/ppermute | solution.py:344
  176.7 14.9 %collective-permute-start.21 = (bf16[256,1024]{1,0:T(8,128)(2,1)S(1)}, bf16[256,1024]{1,0:T(8,128)(2,1)S(1)}, u32[]{:S(2)}, u32[]{:S(2)}) collective-permute-start(bf16[256,1024]{1,0:T(8,128)(2,1)S(1)} %get-tuple-element.125), channel_id=1, source_target_pairs={{0,96},{16,112},{32,0},{48,16},{64,32},{80,48},{96,64},{112,80},{1... | collective-permute-start | bytes 1572872 | tf_op jit(solution)/shard_map/ppermute | solution.py:345
  192.0 9.3 %collective-permute-start.24 = (bf16[64,2048]{1,0:T(8,128)(2,1)S(1)}, bf16[64,2048]{1,0:T(8,128)(2,1)S(1)}, u32[]{:S(2)}, u32[]{:S(2)}) collective-permute-start(bf16[64,2048]{1,0:T(8,128)(2,1)S(1)} %get-tuple-element.129), channel_id=1, source_target_pairs={{0,32},{16,48},{32,64},{48,80},{64,96},{80,112},{96,0},{112,16},{1... | collective-permute-start | bytes 786440 | tf_op jit(solution)/shard_map/ppermute | solution.py:344
  192.3 9.3 %collective-permute-start.26 = (bf16[64,2048]{1,0:T(8,128)(2,1)S(1)}, bf16[64,2048]{1,0:T(8,128)(2,1)S(1)}, u32[]{:S(2)}, u32[]{:S(2)}) collective-permute-start(bf16[64,2048]{1,0:T(8,128)(2,1)S(1)} %get-tuple-element.130), channel_id=1, source_target_pairs={{0,96},{16,112},{32,0},{48,16},{64,32},{80,48},{96,64},{112,80},{1... | collective-permute-start | bytes 786440 | tf_op jit(solution)/shard_map/ppermute | solution.py:345
  196.0 39.7 %collective-permute-start.22 = (bf16[2,256,1024]{2,1,0:T(8,128)(2,1)S(1)}, bf16[2,256,1024]{2,1,0:T(8,128)(2,1)S(1)}, u32[]{:S(2)}, u32[]{:S(2)}) collective-permute-start(bf16[2,256,1024]{2,1,0:T(8,128)(2,1)S(1)} %pad_maximum_fusion.4), channel_id=1, source_target_pairs={{0,32},{16,48},{32,64},{48,80},{64,96},{80,112},{96,0},{112,16},{1... | collective-permute-start | bytes 3145736 | tf_op jit(solution)/shard_map/ppermute | solution.py:352
  197.7 38.1 %collective-permute-start.23 = (bf16[2,256,1024]{2,1,0:T(8,128)(2,1)S(1)}, bf16[2,256,1024]{2,1,0:T(8,128)(2,1)S(1)}, u32[]{:S(2)}, u32[]{:S(2)}) collective-permute-start(bf16[2,256,1024]{2,1,0:T(8,128)(2,1)S(1)} %pad_maximum_fusion.5), channel_id=1, source_target_pairs={{0,96},{16,112},{32,0},{48,16},{64,32},{80,48},{96,64},{112,80},{1... | collective-permute-start | bytes 3145736 | tf_op jit(solution)/shard_map/ppermute | solution.py:352
  201.9 31.2 %collective-permute-start.25 = (bf16[2,64,2048]{2,1,0:T(8,128)(2,1)S(1)}, bf16[2,64,2048]{2,1,0:T(8,128)(2,1)S(1)}, u32[]{:S(2)}, u32[]{:S(2)}) collective-permute-start(bf16[2,64,2048]{2,1,0:T(8,128)(2,1)S(1)} %pad_maximum_fusion.7), channel_id=1, source_target_pairs={{0,32},{16,48},{32,64},{48,80},{64,96},{80,112},{96,0},{112,16},{1... | collective-permute-start | bytes 1572872 | tf_op jit(solution)/shard_map/ppermute | solution.py:352
  202.6 32.0 %collective-permute-start.27 = (bf16[2,64,2048]{2,1,0:T(8,128)(2,1)S(1)}, bf16[2,64,2048]{2,1,0:T(8,128)(2,1)S(1)}, u32[]{:S(2)}, u32[]{:S(2)}) collective-permute-start(bf16[2,64,2048]{2,1,0:T(8,128)(2,1)S(1)} %pad_maximum_fusion.8), channel_id=1, source_target_pairs={{0,96},{16,112},{32,0},{48,16},{64,32},{80,48},{96,64},{112,80},{1... | collective-permute-start | bytes 1572872 | tf_op jit(solution)/shard_map/ppermute | solution.py:352
  (13 other events, 101.7 us)
Sparse Core Ops, SparseCore 0:
  152.5 85.4 reduce-scatter.1

commit v5 on v3

--- a/solution.py
+++ b/solution.py
@@ -145,8 +145,12 @@
     )(wg, wu)
 
 
-def held_copies(held, kept, wt_hbm, wt, sem):
-    copies = [(wt_hbm.at[e], wt.at[e]) for e in range(2)]
+def expert_copies(e, given, kept, sem):
+    return [pltpu.make_async_copy(g.at[e], k.at[e], sem.at[e, i]) for i, (g, k) in enumerate(zip(given, kept))]
+
+
+def held_copies(held, kept, sem):
+    copies = []
     for i, (src, dst) in enumerate(zip(held, kept)):
         for part in (pl.ds(0, 1), pl.ds(2, 2)):
             at = (slice(None), slice(None), part) if i == 3 else (slice(None), part)
@@ -154,10 +158,10 @@
     return [pltpu.make_async_copy(src, dst, sem.at[i]) for i, (src, dst) in enumerate(copies)]
 
 
-def tail_kernel(place, tgt_x, tgt_g, rel_x, tgt, rel, x_lo, x_hi, g_lo, g_hi, wg, wu, wd, wt_hbm, *refs):
-    held = refs[3:7]
-    xs, pa, gs, dhu, act, wt, ab, wp, hp, dap, probs_of, picked, dxs, qs, sem = refs[7:]
-    kept = (ab, wp, hp, dap)
+def tail_kernel(place, tgt_x, tgt_g, rel_x, tgt, rel, x_lo, x_hi, g_lo, g_hi, *refs):
+    given, wt_hbm, held = refs[:3], refs[3:4], refs[7:11]
+    xs, pa, gs, dhu, act, wg, wu, wd, wt, ab, wp, hp, dap, probs_of, picked, dxs, qs, in_sem, out_sem, sem = refs[11:]
+    own, kept = (wg, wu, wd), (ab, wp, hp, dap)
     half = 2 * PEER
     slots = CHUNK * PEER
     width, ff = wg.shape[1], wg.shape[2]
@@ -165,13 +169,25 @@
 
     @pl.when(step == 0)
     def _():
-        for copy in held_copies(held, kept, wt_hbm, wt, sem):
+        for copy in expert_copies(0, given, own, in_sem):
             copy.start()
         pick_rows(1, tgt_x, tgt_g, rel_x, (x_lo, x_hi), (g_lo, g_hi), xs, gs, probs_of, picked)
+        for copy in expert_copies(0, given, own, in_sem):
+            copy.wait()
+        for copy in expert_copies(1, given, own, in_sem) + held_copies(held, kept, sem):
+            copy.start()
+
+    @pl.when(step == 1)
+    def _():
+        for copy in expert_copies(1, given, own, in_sem):
+            copy.wait()
+        for e in range(2):
+            for copy in expert_copies(e, wt_hbm, (wt,), out_sem):
+                copy.start()
 
     @pl.when(step < 2)
     def _():
-        made = products(xs[step, 0], picked[step], probs_of[step][:, :1], wg[0], wu[0], wd[0])
+        made = products(xs[step, 0], picked[step], probs_of[step][:, :1], wg[step], wu[step], wd[step])
         pa[0, 0] = made[0]
         for out, value in zip((ab, wp, hp), made[1:4]):
             out[step, 1] = value
@@ -180,7 +196,7 @@
 
     @pl.when(step == 2)
     def _():
-        for copy in held_copies(held, kept, wt_hbm, wt, sem):
+        for copy in held_copies(held, kept, sem):
             copy.wait()
 
     @pl.when(step >= 2)
@@ -195,6 +211,12 @@
             for pair in range(2):
                 qs[pair, pl.ds(e * half, half), :] = wide[pair * half : (pair + 1) * half]
         for e in range(2):
+
+            @pl.when(k == 0)
+            def _():
+                for copy in expert_copies(e, wt_hbm, (wt,), out_sem):
+                    copy.wait()
+
             dx = dot(dhu[e], wt[e]).astype(BF16)
             for pair in range(2):
                 dxs[pair, pl.ds(e * half, half), :] = dx[pair * half : (pair + 1) * half]
@@ -225,7 +247,6 @@
     plane = lambda i: jnp.maximum(i - 2, 0)
     expert = lambda i: jnp.minimum(i, 1)
     of_plane = lambda *shape: pl.BlockSpec((1, *shape), lambda i, p: (plane(i), 0, 0))
-    of_expert = lambda w: pl.BlockSpec((1, *w.shape[1:]), lambda i, p: (expert(i), 0, 0))
     anywhere = pl.BlockSpec(memory_space=pl.ANY)
     return pl.pallas_call(
         tail_kernel,
@@ -240,8 +261,7 @@
                 of_plane(CHUNK * SRC, LANES),
             ]
             + [kept(v.shape, 0, 0) for v in (*x, *g)]
-            + [of_expert(w) for w in weights]
-            + [anywhere] * 8,
+            + [anywhere] * 11,
             out_specs=[
                 kept((2, 1, slots, width), 0, 1, 0, 0),
                 pl.BlockSpec((1, 1, slots, ff), lambda i, p: (expert(i), 1, 0, 0)),
@@ -249,7 +269,8 @@
                 pl.BlockSpec((2, slots, 2 * ff), lambda i, p: (0, plane(i), 0)),
                 pl.BlockSpec((1, 4, SRC, width + LANES), lambda i, p: (p[plane(i)], 0, 0, 0)),
             ],
-            scratch_shapes=[
+            scratch_shapes=[pltpu.VMEM(w.shape, BF16) for w in weights]
+            + [
                 pltpu.VMEM(wt.shape, BF16),
                 pltpu.VMEM(ab.shape, BF16),
                 pltpu.VMEM(wp.shape, BF16),
@@ -259,7 +280,9 @@
                 pltpu.VMEM((2, slots, width), BF16),
                 pltpu.VMEM((2, 4 * PEER, width), BF16),
                 pltpu.VMEM((2, 4 * PEER, LANES), BF16),
-                pltpu.SemaphoreType.DMA((10,)),
+                pltpu.SemaphoreType.DMA((2, 3)),
+                pltpu.SemaphoreType.DMA((2, 1)),
+                pltpu.SemaphoreType.DMA((8,)),
             ],
         ),
         out_shape=[jax.ShapeDtypeStruct(v.shape, BF16) for v in (xs, pa, gs)]

time: 240 us -> 243 us (1.012)
  Pallas kernels: 79.3 us -> 82.6 us
    pallas_call x1, Pallas kernels: 24.1 us -> 27.4 us  [tail_pass(): pl.pallas_call(tail_kernel, grid_spec=pltpu.PrefetchScalarGridSpec(num_sc...]
  transfers between devices with their start and end apart: 31 -> 31, of which waited for: 12 -> 12; matrix products, arithmetic and copies ran while one was open for 9% -> 8% of each run, Pallas kernels for 23% -> 23%
where the time goes in v5:
time: 243 us
  Pallas kernels  82.6 us (34%)
  waiting for transfers between devices  80.6 us (33%)
  starting transfers between devices  39.8 us (16%)
  other arithmetic  14.9 us (6%)
  between operations  14.5 us (6%)
  local copies, waits for them, and re-layouts  10.2 us (4%)
    ppermute x20, waiting for transfers between devices, send(): return lax.ppermute(value, 'expert', route)  33.4 us
    ppermute x20, starting transfers between devices, send(): return lax.ppermute(value, 'expert', route)  30.8 us
    ppermute x2, waiting for transfers between devices, send_near(): lax.ppermute(ahead, 'dp', along_x(1))  29 us
    pallas_call x2, Pallas kernels, stage_pass(): pl.pallas_call(functools.partial(stage_kernel, n), grid=(2,), in_specs=[f...  28.5 us
    pallas_call x1, Pallas kernels, tail_pass(): pl.pallas_call(tail_kernel, grid_spec=pltpu.PrefetchScalarGridSpec(num_sc...  27.4 us
    pallas_call x2, Pallas kernels, weight_pass(): pl.pallas_call(body, grid=(2,), in_specs=[pl.BlockSpec(memory_space=pltpu...  20 us
    ppermute x2, waiting for transfers between devices, send_far(): lax.ppermute(both(own, got, 2, 0).astype(BF16), 'dp', along_x(1))  15 us
    pallas_call x1, Pallas kernels, turn_pass(): pl.pallas_call(turn_kernel, grid=(2,), in_specs=[by_expert((width, ff), 0...  6.78 us
  transfers between devices with their start and end apart: 31, of which 12 were waited for; matrix products, arithmetic and copies ran while one was open for 8% of the time, Pallas kernels for 23%

profile of v5, /device:TPU:6, one launch (start us, length us, event | category | flops | bytes accessed | tf_op | source)
XLA Modules:
  0.0 242.8 jit_solution(15566484239020463519)
XLA Ops:
  7.2 2.0 collective-permute-start.4
  9.2 2.2 collective-permute-start.6
  12.2 1.9 pad_maximum_fusion.6
  14.1 1.6 collective-permute-start
  15.7 1.7 collective-permute-start.2
  18.3 5.2 %collective-permute-done.4 = bf16[128,2048]{1,0:T(8,128)(2,1)S(1)} collective-permute-done((bf16[128,2048]{1,0:T(8,128)(2,1)}, bf16[128,2048]{1,0:T(8,128)(2,1)S(1)}, u32[]{:S(2)}, u32[]{:S(2)}) %collective-permute-start.4) | collective-permute-done | bytes 524320 | tf_op jit(solution)/shard_map/ppermute | solution.py:374
  23.6 3.3 %collective-permute-start.7 = (bf16[64,2048]{1,0:T(8,128)(2,1)S(1)}, bf16[64,2048]{1,0:T(8,128)(2,1)S(1)}, u32[]{:S(2)}, u32[]{:S(2)}) collective-permute-start(bf16[64,2048]{1,0:T(8,128)(2,1)S(1)} %slice.181), channel_id=1, source_target_pairs={{0,12},{1,13},{2,14},{3,15},{4,0},{5,1},{6,2},{7,3},{8,4},{9,5},{1... | collective-permute-start | bytes 786440 | tf_op jit(solution)/shard_map/ppermute | solution.py:374
  27.0 2.7 %collective-permute-done = bf16[128,2176]{1,0:T(8,128)(2,1)S(1)} collective-permute-done((bf16[128,2176]{1,0:T(8,128)(2,1)}, bf16[128,2176]{1,0:T(8,128)(2,1)S(1)}, u32[]{:S(2)}, u32[]{:S(2)}) %collective-permute-start) | collective-permute-done | bytes 557088 | tf_op jit(solution)/shard_map/ppermute | solution.py:374
  30.1 3.0 %collective-permute-start.3 = (bf16[64,2176]{1,0:T(8,128)(2,1)S(1)}, bf16[64,2176]{1,0:T(8,128)(2,1)S(1)}, u32[]{:S(2)}, u32[]{:S(2)}) collective-permute-start(bf16[64,2176]{1,0:T(8,128)(2,1)S(1)} %slice.179), channel_id=1, source_target_pairs={{0,3},{1,0},{2,1},{3,2},{4,7},{5,4},{6,5},{7,6},{8,11},{9,8},{10,9... | collective-permute-start | bytes 835592 | tf_op jit(solution)/shard_map/ppermute | solution.py:374
  34.4 3.8 %collective-permute-done.1 = bf16[64,2176]{1,0:T(8,128)(2,1)S(1)} collective-permute-done((bf16[64,2176]{1,0:T(8,128)(2,1)S(1)}, bf16[64,2176]{1,0:T(8,128)(2,1)S(1)}, u32[]{:S(2)}, u32[]{:S(2)}) %collective-permute-start.1) | collective-permute-done | bytes 278560 | tf_op jit(solution)/shard_map/ppermute | solution.py:374
  38.5 3.2 %collective-permute-start.9 = (bf16[256,2176]{1,0:T(8,128)(2,1)S(1)}, bf16[256,2176]{1,0:T(8,128)(2,1)}, u32[]{:S(2)}, u32[]{:S(2)}) collective-permute-start(bf16[256,2176]{1,0:T(8,128)(2,1)S(1)} %pad_maximum_fusion.refs_0_), channel_id=1, source_target_pairs={{0,12},{1,13},{2,14},{3,15},{4,0},{5,1},{6,2},{7,3},{8,4},{9,5},{1... | collective-permute-start | bytes 3342344 | tf_op jit(solution)/shard_map/ppermute | solution.py:374
  42.2 2.8 %collective-permute-start.11 = (bf16[256,2048]{1,0:T(8,128)(2,1)}, bf16[256,2048]{1,0:T(8,128)(2,1)}, u32[]{:S(2)}, u32[]{:S(2)}) collective-permute-start(bf16[256,2048]{1,0:T(8,128)(2,1)} %pad_maximum_fusion.2.refs_2_), channel_id=1, source_target_pairs={{0,3},{1,0},{2,1},{3,2},{4,7},{5,4},{6,5},{7,6},{8,11},{9,8},{10,9... | collective-permute-start | bytes 3145736 | tf_op jit(solution)/shard_map/ppermute | solution.py:374
  47.7 1.9 pad.9.rel.rel_x
  49.6 6.8 %turn.1.refs_3_ = bf16[2,1024,2048]{2,1,0:T(8,128)(2,1)} custom-call(bf16[2,2048,512]{2,1,0:T(8,128)(2,1)} %refs_0_.1, bf16[2,2048,512]{2,1,0:T(8,128)(2,1)} %refs_1_.1), custom_call_target="tpu_custom_call" | custom-call | flops 268435456 | bytes 524288 | tf_op jit(solution)/shard_map/turn/pallas_call | solution.py:136
  56.4 11.5 %stage.2 = (bf16[2,4,192,2048]{3,2,1,0:T(8,128)(2,1)}, bf16[2,4,192,512]{3,2,1,0:T(8,128)(2,1)}, bf16[2,4,192,512]{3,2,1,0:T(8,128)(2,1)}, bf16[2,4,192,512]{3,2...) custom-call(s32[4,4,256]{2,1,0:T(4,128)} %reshape.197.tgt_x.tgt, ...), custom_call_target="tpu_custom_call" | custom-call | flops 268435456 | bytes 524288 | tf_op jit(solution)/shard_map/stage/pallas_call | solution.py:107
  68.2 3.2 %collective-permute-start.19 = (bf16[256,2048]{1,0:T(8,128)(2,1)S(1)}, bf16[256,2048]{1,0:T(8,128)(2,1)S(1)}, u32[]{:S(2)}, u32[]{:S(2)}) collective-permute-start(bf16[256,2048]{1,0:T(8,128)(2,1)S(1)} %copy-done.5), channel_id=1, source_target_pairs={{0,3},{1,0},{2,1},{3,2},{4,7},{5,4},{6,5},{7,6},{8,11},{9,8},{10,9... | collective-permute-start | bytes 3145736 | tf_op jit(solution)/shard_map/ppermute | solution.py:374
  71.4 3.2 %collective-permute-start.17 = (bf16[256,2176]{1,0:T(8,128)(2,1)S(1)}, bf16[256,2176]{1,0:T(8,128)(2,1)S(1)}, u32[]{:S(2)}, u32[]{:S(2)}) collective-permute-start(bf16[256,2176]{1,0:T(8,128)(2,1)S(1)} %copy-done.1), channel_id=1, source_target_pairs={{0,12},{1,13},{2,14},{3,15},{4,0},{5,1},{6,2},{7,3},{8,4},{9,5},{1... | collective-permute-start | bytes 3342344 | tf_op jit(solution)/shard_map/ppermute | solution.py:374
  74.6 16.7 %collective-permute-done.18.refs_4_ = bf16[256,2048]{1,0:T(8,128)(2,1)S(1)} collective-permute-done((bf16[256,2048]{1,0:T(8,128)(2,1)}, bf16[256,2048]{1,0:T(8,128)(2,1)S(1)}, u32[]{:S(2)}, u32[]{:S(2)}) %collective-permute-start.18) | collective-permute-done | bytes 1048608 | tf_op jit(solution)/shard_map/ppermute | solution.py:374
  91.3 3.2 %collective-permute-start.14 = (bf16[256,2048]{1,0:T(8,128)(2,1)}, bf16[256,2048]{1,0:T(8,128)(2,1)S(1)}, u32[]{:S(2)}, u32[]{:S(2)}) collective-permute-start(bf16[256,2048]{1,0:T(8,128)(2,1)} %collective-permute-done.11.refs_6_), channel_id=1, source_target_pairs={{0,3},{1,0},{2,1},{3,2},{4,7},{5,4},{6,5},{7,6},{8,11},{9,8},{10,9... | collective-permute-start | bytes 3145736 | tf_op jit(solution)/shard_map/ppermute | solution.py:374
  95.4 4.2 %collective-permute-done.17.refs_3_ = bf16[256,2176]{1,0:T(8,128)(2,1)S(1)} collective-permute-done((bf16[256,2176]{1,0:T(8,128)(2,1)S(1)}, bf16[256,2176]{1,0:T(8,128)(2,1)S(1)}, u32[]{:S(2)}, u32[]{:S(2)}) %collective-permute-start.17) | collective-permute-done | bytes 1114144 | tf_op jit(solution)/shard_map/ppermute | solution.py:374
  100.6 17.0 %stage.3 = (bf16[2,4,192,2048]{3,2,1,0:T(8,128)(2,1)}, bf16[2,4,192,512]{3,2,1,0:T(8,128)(2,1)}, bf16[2,4,192,512]{3,2,1,0:T(8,128)(2,1)}, bf16[2,4,192,512]{3,2...) custom-call(s32[4,4,256]{2,1,0:T(4,128)} %reshape.197.tgt_x.tgt, ...), custom_call_target="tpu_custom_call", output_to_operand_aliasing={{0}: (14, {}), {1}: (15, {}), {2}: (16, {}), {3}: (17, {}),... | custom-call | flops 268435456 | bytes 524288 | tf_op jit(solution)/shard_map/stage/pallas_call | solution.py:107
  118.5 27.4 %tail.1 = (bf16[2,4,192,2048]{3,2,1,0:T(8,128)(2,1)}, bf16[2,4,192,512]{3,2,1,0:T(8,128)(2,1)}, bf16[2,4,4,48,2048]{4,3,2,1,0:T(8,128)(2,1)}, bf16[2,768,1024]{2,1,0:T(8,128)(2,1)}, bf16[4,4,128,2176]{3,2,1,0:T(8,128)(2,1)}) custom-call(s32[8]{0:T(128)} %pad_add_fusion.4.place, ...), custom_call_target="tpu_custom_call", output_to_operand_aliasing={{0}: (14, {}), {1}: (15, {}), {2}: (16, {})} | custom-call | flops 15032385536 | bytes 33554432 | tf_op jit(solution)/shard_map/tail/pallas_call | solution.py:251
  146.6 12.2 %up_grad.1 = (bf16[4,2,256,1024]{3,2,1,0:T(8,128)(2,1)}, bf16[4,2,256,1024]{3,2,1,0:T(8,128)(2,1)}) custom-call(s32[2]{0:T(128)} %pad_add_fusion.5.where, bf16[2,768,2048]{2,1,0:T(8,128)(2,1)} %bitcast.84, bf16[2,768,1024]{2,1,0:T(8,128)(2,1)} %get-tuple-element.87.dhu), custom_call_target="tpu_custom_call" | custom-call | flops 6442450944 | bytes 16777216 | tf_op jit(solution)/shard_map/up_grad/pallas_call | solution.py:325
  158.7 7.8 %down_grad.1 = (bf16[4,2,64,2048]{3,2,1,0:T(8,128)(2,1)}, bf16[4,2,64,2048]{3,2,1,0:T(8,128)(2,1)}) custom-call(s32[2]{0:T(128)} %pad_add_fusion.5.where, bf16[2,768,512]{2,1,0:T(8,128)(2,1)} %bitcast.87, bf16[2,768,2048]{2,1,0:T(8,128)(2,1)} %bitcast.85), custom_call_target="tpu_custom_call" | custom-call | flops 3221225472 | bytes 16777216 | tf_op jit(solution)/shard_map/down_grad/pallas_call | solution.py:325
  167.1 2.6 %fusion.9 = (bf16[1,256,1024]{2,1,0:T(8,128)(2,1)S(1)}, bf16[1,256,1024]{2,1,0:T(8,128)(2,1)S(1)}, bf16[256,1024]{1,0:T(8,128)(2,1)S(1)}, bf16[256,1024]{1,0:T(8,128)(2,1)S(1)}) fusion(bf16[4,2,256,1024]{3,2,1,0:T(8,128)(2,1)} %collective-permute-done.20, bf16[4,2,256,1024]{3,2,1,0:T(8,128)(2,1)S(1)} %copy-done.3), kind=kLoop, calls=%fused_computation.25 | loop fusion | flops 4194304 | bytes 6291456 | tf_op jit(solution)/shard_map/add | solution.py:348
  171.8 12.0 %collective-permute-done.22 = bf16[256,1024]{1,0:T(8,128)(2,1)S(1)} collective-permute-done((bf16[256,1024]{1,0:T(8,128)(2,1)S(1)}, bf16[256,1024]{1,0:T(8,128)(2,1)S(1)}, u32[]{:S(2)}, u32[]{:S(2)}) %collective-permute-start.22) | collective-permute-done | bytes 524320 | tf_op jit(solution)/shard_map/ppermute | solution.py:353
  186.0 1.7 collective-permute-start.28
  187.7 1.9 fusion.11
  191.9 3.0 %collective-permute-done.26 = bf16[64,2048]{1,0:T(8,128)(2,1)S(1)} collective-permute-done((bf16[64,2048]{1,0:T(8,128)(2,1)S(1)}, bf16[64,2048]{1,0:T(8,128)(2,1)S(1)}, u32[]{:S(2)}, u32[]{:S(2)}) %collective-permute-start.26) | collective-permute-done | bytes 262176 | tf_op jit(solution)/shard_map/ppermute | solution.py:353
  197.8 29.0 %collective-permute-done.27 = bf16[2,64,2048]{2,1,0:T(8,128)(2,1)S(1)} collective-permute-done((bf16[2,64,2048]{2,1,0:T(8,128)(2,1)S(1)}, bf16[2,64,2048]{2,1,0:T(8,128)(2,1)S(1)}, u32[]{:S(2)}, u32[]{:S(2)}) %collective-permute-start.27) | collective-permute-done | bytes 524320 | tf_op jit(solution)/shard_map/ppermute | solution.py:361
  229.4 2.2 fusion.1
  234.1 1.9 slice.182
  (116 shorter events, 25.7 us)
Async XLA Ops:
  7.2 225.5 %reduce-scatter.4.cloned.1.call-start = ((), (), s32[]{:S(2)}) async-start(), calls=%async_computation.1 | async-start | bytes 9469952
  7.2 16.2 %collective-permute-start.4 = (bf16[128,2048]{1,0:T(8,128)(2,1)}, bf16[128,2048]{1,0:T(8,128)(2,1)S(1)}, u32[]{:S(2)}, u32[]{:S(2)}) collective-permute-start(bf16[128,2048]{1,0:T(8,128)(2,1)} %param.9), channel_id=1, source_target_pairs={{0,4},{1,5},{2,6},{3,7},{4,8},{5,9},{6,10},{7,11},{8,12},{9,13},{1... | collective-permute-start | bytes 1572872 | tf_op jit(solution)/shard_map/ppermute | solution.py:374
  9.2 14.4 %collective-permute-start.6 = (bf16[128,2048]{1,0:T(8,128)(2,1)}, bf16[128,2048]{1,0:T(8,128)(2,1)S(1)}, u32[]{:S(2)}, u32[]{:S(2)}) collective-permute-start(bf16[128,2048]{1,0:T(8,128)(2,1)} %param.9), channel_id=1, source_target_pairs={{0,12},{1,13},{2,14},{3,15},{4,0},{5,1},{6,2},{7,3},{8,4},{9,5},{1... | collective-permute-start | bytes 1572872 | tf_op jit(solution)/shard_map/ppermute | solution.py:374
  14.1 15.6 %collective-permute-start = (bf16[128,2176]{1,0:T(8,128)(2,1)}, bf16[128,2176]{1,0:T(8,128)(2,1)S(1)}, u32[]{:S(2)}, u32[]{:S(2)}) collective-permute-start(bf16[128,2176]{1,0:T(8,128)(2,1)} %pad_maximum_fusion.6), channel_id=1, source_target_pairs={{0,1},{1,2},{2,3},{3,0},{4,5},{5,6},{6,7},{7,4},{8,9},{9,10},{10,1... | collective-permute-start | bytes 1671176 | tf_op jit(solution)/shard_map/ppermute | solution.py:374
  15.7 14.4 %collective-permute-start.2 = (bf16[128,2176]{1,0:T(8,128)(2,1)}, bf16[128,2176]{1,0:T(8,128)(2,1)S(1)}, u32[]{:S(2)}, u32[]{:S(2)}) collective-permute-start(bf16[128,2176]{1,0:T(8,128)(2,1)} %pad_maximum_fusion.6), channel_id=1, source_target_pairs={{0,3},{1,0},{2,1},{3,2},{4,7},{5,4},{6,5},{7,6},{8,11},{9,8},{10,9... | collective-permute-start | bytes 1671176 | tf_op jit(solution)/shard_map/ppermute | solution.py:374
  23.5 9.7 %collective-permute-start.5 = (bf16[64,2048]{1,0:T(8,128)(2,1)S(1)}, bf16[64,2048]{1,0:T(8,128)(2,1)S(1)}, u32[]{:S(2)}, u32[]{:S(2)}) collective-permute-start(bf16[64,2048]{1,0:T(8,128)(2,1)S(1)} %slice.180), channel_id=1, source_target_pairs={{0,4},{1,5},{2,6},{3,7},{4,8},{5,9},{6,10},{7,11},{8,12},{9,13},{1... | collective-permute-start | bytes 786440 | tf_op jit(solution)/shard_map/ppermute | solution.py:374
  23.6 9.6 %collective-permute-start.7 = (bf16[64,2048]{1,0:T(8,128)(2,1)S(1)}, bf16[64,2048]{1,0:T(8,128)(2,1)S(1)}, u32[]{:S(2)}, u32[]{:S(2)}) collective-permute-start(bf16[64,2048]{1,0:T(8,128)(2,1)S(1)} %slice.181), channel_id=1, source_target_pairs={{0,12},{1,13},{2,14},{3,15},{4,0},{5,1},{6,2},{7,3},{8,4},{9,5},{1... | collective-permute-start | bytes 786440 | tf_op jit(solution)/shard_map/ppermute | solution.py:374
  29.7 8.6 %collective-permute-start.1 = (bf16[64,2176]{1,0:T(8,128)(2,1)S(1)}, bf16[64,2176]{1,0:T(8,128)(2,1)S(1)}, u32[]{:S(2)}, u32[]{:S(2)}) collective-permute-start(bf16[64,2176]{1,0:T(8,128)(2,1)S(1)} %slice.178), channel_id=1, source_target_pairs={{0,1},{1,2},{2,3},{3,0},{4,5},{5,6},{6,7},{7,4},{8,9},{9,10},{10,1... | collective-permute-start | bytes 835592 | tf_op jit(solution)/shard_map/ppermute | solution.py:374
  30.1 8.1 %collective-permute-start.3 = (bf16[64,2176]{1,0:T(8,128)(2,1)S(1)}, bf16[64,2176]{1,0:T(8,128)(2,1)S(1)}, u32[]{:S(2)}, u32[]{:S(2)}) collective-permute-start(bf16[64,2176]{1,0:T(8,128)(2,1)S(1)} %slice.179), channel_id=1, source_target_pairs={{0,3},{1,0},{2,1},{3,2},{4,7},{5,4},{6,5},{7,6},{8,11},{9,8},{10,9... | collective-permute-start | bytes 835592 | tf_op jit(solution)/shard_map/ppermute | solution.py:374
  38.4 29.6 %collective-permute-start.8 = (bf16[256,2176]{1,0:T(8,128)(2,1)S(1)}, bf16[256,2176]{1,0:T(8,128)(2,1)}, u32[]{:S(2)}, u32[]{:S(2)}) collective-permute-start(bf16[256,2176]{1,0:T(8,128)(2,1)S(1)} %pad_maximum_fusion.1.refs_1_), channel_id=1, source_target_pairs={{0,4},{1,5},{2,6},{3,7},{4,8},{5,9},{6,10},{7,11},{8,12},{9,13},{1... | collective-permute-start | bytes 3342344 | tf_op jit(solution)/shard_map/ppermute | solution.py:374
  38.5 29.5 %collective-permute-start.9 = (bf16[256,2176]{1,0:T(8,128)(2,1)S(1)}, bf16[256,2176]{1,0:T(8,128)(2,1)}, u32[]{:S(2)}, u32[]{:S(2)}) collective-permute-start(bf16[256,2176]{1,0:T(8,128)(2,1)S(1)} %pad_maximum_fusion.refs_0_), channel_id=1, source_target_pairs={{0,12},{1,13},{2,14},{3,15},{4,0},{5,1},{6,2},{7,3},{8,4},{9,5},{1... | collective-permute-start | bytes 3342344 | tf_op jit(solution)/shard_map/ppermute | solution.py:374
  41.7 26.2 %collective-permute-start.10 = (bf16[256,2048]{1,0:T(8,128)(2,1)S(1)}, bf16[256,2048]{1,0:T(8,128)(2,1)}, u32[]{:S(2)}, u32[]{:S(2)}) collective-permute-start(bf16[256,2048]{1,0:T(8,128)(2,1)S(1)} %pad_maximum_fusion.3.refs_3_), channel_id=1, source_target_pairs={{0,1},{1,2},{2,3},{3,0},{4,5},{5,6},{6,7},{7,4},{8,9},{9,10},{10,1... | collective-permute-start | bytes 3145736 | tf_op jit(solution)/shard_map/ppermute | solution.py:374
  42.2 25.7 %collective-permute-start.11 = (bf16[256,2048]{1,0:T(8,128)(2,1)}, bf16[256,2048]{1,0:T(8,128)(2,1)}, u32[]{:S(2)}, u32[]{:S(2)}) collective-permute-start(bf16[256,2048]{1,0:T(8,128)(2,1)} %pad_maximum_fusion.2.refs_2_), channel_id=1, source_target_pairs={{0,3},{1,0},{2,1},{3,2},{4,7},{5,4},{6,5},{7,6},{8,11},{9,8},{10,9... | collective-permute-start | bytes 3145736 | tf_op jit(solution)/shard_map/ppermute | solution.py:374
  56.4 38.3 %copy-start.13 = (s32[4]{0:T(128)S(1)}, s32[4]{0:T(128)}, u32[]{:S(2)}) copy-start(s32[4]{0:T(128)} %constant.105.clone) | copy-start | bytes 52
  68.0 26.5 %collective-permute-start.16 = (bf16[256,2176]{1,0:T(8,128)(2,1)}, bf16[256,2176]{1,0:T(8,128)(2,1)S(1)}, u32[]{:S(2)}, u32[]{:S(2)}) collective-permute-start(bf16[256,2176]{1,0:T(8,128)(2,1)} %copy-done.2), channel_id=1, source_target_pairs={{0,4},{1,5},{2,6},{3,7},{4,8},{5,9},{6,10},{7,11},{8,12},{9,13},{1... | collective-permute-start | bytes 3342344 | tf_op jit(solution)/shard_map/ppermute | solution.py:374
  68.1 23.2 %collective-permute-start.18 = (bf16[256,2048]{1,0:T(8,128)(2,1)}, bf16[256,2048]{1,0:T(8,128)(2,1)S(1)}, u32[]{:S(2)}, u32[]{:S(2)}) collective-permute-start(bf16[256,2048]{1,0:T(8,128)(2,1)} %pad_maximum_fusion.2.refs_2_), channel_id=1, source_target_pairs={{0,1},{1,2},{2,3},{3,0},{4,5},{5,6},{6,7},{7,4},{8,9},{9,10},{10,1... | collective-permute-start | bytes 3145736 | tf_op jit(solution)/shard_map/ppermute | solution.py:374
  68.2 23.1 %collective-permute-start.19 = (bf16[256,2048]{1,0:T(8,128)(2,1)S(1)}, bf16[256,2048]{1,0:T(8,128)(2,1)S(1)}, u32[]{:S(2)}, u32[]{:S(2)}) collective-permute-start(bf16[256,2048]{1,0:T(8,128)(2,1)S(1)} %copy-done.5), channel_id=1, source_target_pairs={{0,3},{1,0},{2,1},{3,2},{4,7},{5,4},{6,5},{7,6},{8,11},{9,8},{10,9... | collective-permute-start | bytes 3145736 | tf_op jit(solution)/shard_map/ppermute | solution.py:374
  71.4 28.2 %collective-permute-start.17 = (bf16[256,2176]{1,0:T(8,128)(2,1)S(1)}, bf16[256,2176]{1,0:T(8,128)(2,1)S(1)}, u32[]{:S(2)}, u32[]{:S(2)}) collective-permute-start(bf16[256,2176]{1,0:T(8,128)(2,1)S(1)} %copy-done.1), channel_id=1, source_target_pairs={{0,12},{1,13},{2,14},{3,15},{4,0},{5,1},{6,2},{7,3},{8,4},{9,5},{1... | collective-permute-start | bytes 3342344 | tf_op jit(solution)/shard_map/ppermute | solution.py:374
  74.5 43.8 %collective-permute-start.12 = (bf16[256,2176]{1,0:T(8,128)(2,1)}, bf16[256,2176]{1,0:T(8,128)(2,1)}, u32[]{:S(2)}, u32[]{:S(2)}) collective-permute-start(bf16[256,2176]{1,0:T(8,128)(2,1)} %collective-permute-done.9.refs_2_), channel_id=1, source_target_pairs={{0,12},{1,13},{2,14},{3,15},{4,0},{5,1},{6,2},{7,3},{8,4},{9,5},{1... | collective-permute-start | bytes 3342344 | tf_op jit(solution)/shard_map/ppermute | solution.py:374
  91.3 27.0 %collective-permute-start.13 = (bf16[256,2176]{1,0:T(8,128)(2,1)}, bf16[256,2176]{1,0:T(8,128)(2,1)}, u32[]{:S(2)}, u32[]{:S(2)}) collective-permute-start(bf16[256,2176]{1,0:T(8,128)(2,1)} %collective-permute-done.8.refs_1_), channel_id=1, source_target_pairs={{0,4},{1,5},{2,6},{3,7},{4,8},{5,9},{6,10},{7,11},{8,12},{9,13},{1... | collective-permute-start | bytes 3342344 | tf_op jit(solution)/shard_map/ppermute | solution.py:374
  91.3 26.2 %collective-permute-start.14 = (bf16[256,2048]{1,0:T(8,128)(2,1)}, bf16[256,2048]{1,0:T(8,128)(2,1)S(1)}, u32[]{:S(2)}, u32[]{:S(2)}) collective-permute-start(bf16[256,2048]{1,0:T(8,128)(2,1)} %collective-permute-done.11.refs_6_), channel_id=1, source_target_pairs={{0,3},{1,0},{2,1},{3,2},{4,7},{5,4},{6,5},{7,6},{8,11},{9,8},{10,9... | collective-permute-start | bytes 3145736 | tf_op jit(solution)/shard_map/ppermute | solution.py:374
  94.5 23.1 %collective-permute-start.15 = (bf16[256,2048]{1,0:T(8,128)(2,1)}, bf16[256,2048]{1,0:T(8,128)(2,1)}, u32[]{:S(2)}, u32[]{:S(2)}) collective-permute-start(bf16[256,2048]{1,0:T(8,128)(2,1)} %collective-permute-done.10.refs_5_), channel_id=1, source_target_pairs={{0,1},{1,2},{2,3},{3,0},{4,5},{5,6},{6,7},{7,4},{8,9},{9,10},{10,1... | collective-permute-start | bytes 3145736 | tf_op jit(solution)/shard_map/ppermute | solution.py:374
  158.7 8.3 %collective-permute-start.20 = (bf16[4,2,256,1024]{3,2,1,0:T(8,128)(2,1)}, bf16[4,2,256,1024]{3,2,1,0:T(8,128)(2,1)}, u32[]{:S(2)}, u32[]{:S(2)}) collective-permute-start(bf16[4,2,256,1024]{3,2,1,0:T(8,128)(2,1)} %get-tuple-element.89), channel_id=1, source_target_pairs={{0,16},{16,0},{32,48},{48,32},{64,80},{80,64},{96,112},{112,96},{1... | collective-permute-start | bytes 12582920 | tf_op jit(solution)/shard_map/ppermute | solution.py:344
  166.5 5.3 %collective-permute-start.21 = (bf16[4,2,64,2048]{3,2,1,0:T(8,128)(2,1)}, bf16[4,2,64,2048]{3,2,1,0:T(8,128)(2,1)S(1)}, u32[]{:S(2)}, u32[]{:S(2)}) collective-permute-start(bf16[4,2,64,2048]{3,2,1,0:T(8,128)(2,1)} %get-tuple-element.92), channel_id=1, source_target_pairs={{0,16},{16,0},{32,48},{48,32},{64,80},{80,64},{96,112},{112,96},{1... | collective-permute-start | bytes 6291464 | tf_op jit(solution)/shard_map/ppermute | solution.py:344
  169.7 14.1 %collective-permute-start.22 = (bf16[256,1024]{1,0:T(8,128)(2,1)S(1)}, bf16[256,1024]{1,0:T(8,128)(2,1)S(1)}, u32[]{:S(2)}, u32[]{:S(2)}) collective-permute-start(bf16[256,1024]{1,0:T(8,128)(2,1)S(1)} %get-tuple-element.122), channel_id=1, source_target_pairs={{0,32},{16,48},{32,64},{48,80},{64,96},{80,112},{96,0},{112,16},{1... | collective-permute-start | bytes 1572872 | tf_op jit(solution)/shard_map/ppermute | solution.py:353
  170.3 14.9 %collective-permute-start.23 = (bf16[256,1024]{1,0:T(8,128)(2,1)S(1)}, bf16[256,1024]{1,0:T(8,128)(2,1)S(1)}, u32[]{:S(2)}, u32[]{:S(2)}) collective-permute-start(bf16[256,1024]{1,0:T(8,128)(2,1)S(1)} %get-tuple-element.121), channel_id=1, source_target_pairs={{0,96},{16,112},{32,0},{48,16},{64,32},{80,48},{96,64},{112,80},{1... | collective-permute-start | bytes 1572872 | tf_op jit(solution)/shard_map/ppermute | solution.py:354
  185.6 9.3 %collective-permute-start.26 = (bf16[64,2048]{1,0:T(8,128)(2,1)S(1)}, bf16[64,2048]{1,0:T(8,128)(2,1)S(1)}, u32[]{:S(2)}, u32[]{:S(2)}) collective-permute-start(bf16[64,2048]{1,0:T(8,128)(2,1)S(1)} %get-tuple-element.125), channel_id=1, source_target_pairs={{0,32},{16,48},{32,64},{48,80},{64,96},{80,112},{96,0},{112,16},{1... | collective-permute-start | bytes 786440 | tf_op jit(solution)/shard_map/ppermute | solution.py:353
  186.0 9.3 %collective-permute-start.28 = (bf16[64,2048]{1,0:T(8,128)(2,1)S(1)}, bf16[64,2048]{1,0:T(8,128)(2,1)S(1)}, u32[]{:S(2)}, u32[]{:S(2)}) collective-permute-start(bf16[64,2048]{1,0:T(8,128)(2,1)S(1)} %get-tuple-element.126), channel_id=1, source_target_pairs={{0,96},{16,112},{32,0},{48,16},{64,32},{80,48},{96,64},{112,80},{1... | collective-permute-start | bytes 786440 | tf_op jit(solution)/shard_map/ppermute | solution.py:354
  189.7 39.7 %collective-permute-start.24 = (bf16[2,256,1024]{2,1,0:T(8,128)(2,1)S(1)}, bf16[2,256,1024]{2,1,0:T(8,128)(2,1)S(1)}, u32[]{:S(2)}, u32[]{:S(2)}) collective-permute-start(bf16[2,256,1024]{2,1,0:T(8,128)(2,1)S(1)} %pad_maximum_fusion.4), channel_id=1, source_target_pairs={{0,32},{16,48},{32,64},{48,80},{64,96},{80,112},{96,0},{112,16},{1... | collective-permute-start | bytes 3145736 | tf_op jit(solution)/shard_map/ppermute | solution.py:361
  191.3 38.1 %collective-permute-start.25 = (bf16[2,256,1024]{2,1,0:T(8,128)(2,1)S(1)}, bf16[2,256,1024]{2,1,0:T(8,128)(2,1)S(1)}, u32[]{:S(2)}, u32[]{:S(2)}) collective-permute-start(bf16[2,256,1024]{2,1,0:T(8,128)(2,1)S(1)} %pad_maximum_fusion.5), channel_id=1, source_target_pairs={{0,96},{16,112},{32,0},{48,16},{64,32},{80,48},{96,64},{112,80},{1... | collective-permute-start | bytes 3145736 | tf_op jit(solution)/shard_map/ppermute | solution.py:361
  195.5 31.2 %collective-permute-start.27 = (bf16[2,64,2048]{2,1,0:T(8,128)(2,1)S(1)}, bf16[2,64,2048]{2,1,0:T(8,128)(2,1)S(1)}, u32[]{:S(2)}, u32[]{:S(2)}) collective-permute-start(bf16[2,64,2048]{2,1,0:T(8,128)(2,1)S(1)} %pad_maximum_fusion.7), channel_id=1, source_target_pairs={{0,32},{16,48},{32,64},{48,80},{64,96},{80,112},{96,0},{112,16},{1... | collective-permute-start | bytes 1572872 | tf_op jit(solution)/shard_map/ppermute | solution.py:361
  196.5 31.8 %collective-permute-start.29 = (bf16[2,64,2048]{2,1,0:T(8,128)(2,1)S(1)}, bf16[2,64,2048]{2,1,0:T(8,128)(2,1)S(1)}, u32[]{:S(2)}, u32[]{:S(2)}) collective-permute-start(bf16[2,64,2048]{2,1,0:T(8,128)(2,1)S(1)} %pad_maximum_fusion.8), channel_id=1, source_target_pairs={{0,96},{16,112},{32,0},{48,16},{64,32},{80,48},{96,64},{112,80},{1... | collective-permute-start | bytes 1572872 | tf_op jit(solution)/shard_map/ppermute | solution.py:361
  (14 other events, 124.0 us)
Sparse Core Ops, SparseCore 0:
  146.1 85.5 reduce-scatter.3

commit v6 on v3

--- a/solution.py
+++ b/solution.py
@@ -165,9 +165,14 @@
 
     @pl.when(step == 0)
     def _():
-        for copy in held_copies(held, kept, wt_hbm, wt, sem):
+        for copy in held_copies(held, kept, wt_hbm, wt, sem)[2:]:
             copy.start()
         pick_rows(1, tgt_x, tgt_g, rel_x, (x_lo, x_hi), (g_lo, g_hi), xs, gs, probs_of, picked)
+
+    @pl.when(step == 1)
+    def _():
+        for copy in held_copies(held, kept, wt_hbm, wt, sem)[:2]:
+            copy.start()
 
     @pl.when(step < 2)
     def _():

time: 240 us -> 241 us (level)
  no operation moved by 1% of the time
where the time goes in v6:
time: 241 us
  waiting for transfers between devices  80.6 us (33%)
  Pallas kernels  80.6 us (33%)
  starting transfers between devices  39.8 us (17%)
  other arithmetic  14.9 us (6%)
  between operations  14.5 us (6%)
  local copies, waits for them, and re-layouts  10.2 us (4%)
    ppermute x20, waiting for transfers between devices, send(): return lax.ppermute(value, 'expert', route)  33.4 us
    ppermute x20, starting transfers between devices, send(): return lax.ppermute(value, 'expert', route)  30.8 us
    ppermute x2, waiting for transfers between devices, send_near(): lax.ppermute(ahead, 'dp', along_x(1))  29 us
    pallas_call x2, Pallas kernels, stage_pass(): pl.pallas_call(functools.partial(stage_kernel, n), grid=(2,), in_specs=[f...  28.5 us
    pallas_call x1, Pallas kernels, tail_pass(): pl.pallas_call(tail_kernel, grid_spec=pltpu.PrefetchScalarGridSpec(num_sc...  25.4 us
    pallas_call x2, Pallas kernels, weight_pass(): pl.pallas_call(body, grid=(2,), in_specs=[pl.BlockSpec(memory_space=pltpu...  20 us
    ppermute x2, waiting for transfers between devices, send_far(): lax.ppermute(both(own, got, 2, 0).astype(BF16), 'dp', along_x(1))  15 us
    pallas_call x1, Pallas kernels, turn_pass(): pl.pallas_call(turn_kernel, grid=(2,), in_specs=[by_expert((width, ff), 0...  6.78 us
  transfers between devices with their start and end apart: 31, of which 12 were waited for; matrix products, arithmetic and copies ran while one was open for 9% of the time, Pallas kernels for 23%

profile of v6, /device:TPU:6, one launch (start us, length us, event | category | flops | bytes accessed | tf_op | source)
XLA Modules:
  0.0 240.8 jit_solution(2127917806544809803)
XLA Ops:
  7.2 2.0 collective-permute-start.4
  9.2 2.2 collective-permute-start.6
  12.2 1.9 pad_maximum_fusion.6
  14.1 1.6 collective-permute-start
  15.7 1.7 collective-permute-start.2
  18.3 5.2 %collective-permute-done.4 = bf16[128,2048]{1,0:T(8,128)(2,1)S(1)} collective-permute-done((bf16[128,2048]{1,0:T(8,128)(2,1)}, bf16[128,2048]{1,0:T(8,128)(2,1)S(1)}, u32[]{:S(2)}, u32[]{:S(2)}) %collective-permute-start.4) | collective-permute-done | bytes 524320 | tf_op jit(solution)/shard_map/ppermute | solution.py:356
  23.6 3.3 %collective-permute-start.7 = (bf16[64,2048]{1,0:T(8,128)(2,1)S(1)}, bf16[64,2048]{1,0:T(8,128)(2,1)S(1)}, u32[]{:S(2)}, u32[]{:S(2)}) collective-permute-start(bf16[64,2048]{1,0:T(8,128)(2,1)S(1)} %slice.181), channel_id=1, source_target_pairs={{0,12},{1,13},{2,14},{3,15},{4,0},{5,1},{6,2},{7,3},{8,4},{9,5},{1... | collective-permute-start | bytes 786440 | tf_op jit(solution)/shard_map/ppermute | solution.py:356
  27.0 2.7 %collective-permute-done = bf16[128,2176]{1,0:T(8,128)(2,1)S(1)} collective-permute-done((bf16[128,2176]{1,0:T(8,128)(2,1)}, bf16[128,2176]{1,0:T(8,128)(2,1)S(1)}, u32[]{:S(2)}, u32[]{:S(2)}) %collective-permute-start) | collective-permute-done | bytes 557088 | tf_op jit(solution)/shard_map/ppermute | solution.py:356
  30.1 3.0 %collective-permute-start.3 = (bf16[64,2176]{1,0:T(8,128)(2,1)S(1)}, bf16[64,2176]{1,0:T(8,128)(2,1)S(1)}, u32[]{:S(2)}, u32[]{:S(2)}) collective-permute-start(bf16[64,2176]{1,0:T(8,128)(2,1)S(1)} %slice.179), channel_id=1, source_target_pairs={{0,3},{1,0},{2,1},{3,2},{4,7},{5,4},{6,5},{7,6},{8,11},{9,8},{10,9... | collective-permute-start | bytes 835592 | tf_op jit(solution)/shard_map/ppermute | solution.py:356
  34.4 3.8 %collective-permute-done.1 = bf16[64,2176]{1,0:T(8,128)(2,1)S(1)} collective-permute-done((bf16[64,2176]{1,0:T(8,128)(2,1)S(1)}, bf16[64,2176]{1,0:T(8,128)(2,1)S(1)}, u32[]{:S(2)}, u32[]{:S(2)}) %collective-permute-start.1) | collective-permute-done | bytes 278560 | tf_op jit(solution)/shard_map/ppermute | solution.py:356
  38.5 3.2 %collective-permute-start.9 = (bf16[256,2176]{1,0:T(8,128)(2,1)S(1)}, bf16[256,2176]{1,0:T(8,128)(2,1)}, u32[]{:S(2)}, u32[]{:S(2)}) collective-permute-start(bf16[256,2176]{1,0:T(8,128)(2,1)S(1)} %pad_maximum_fusion.refs_0_), channel_id=1, source_target_pairs={{0,12},{1,13},{2,14},{3,15},{4,0},{5,1},{6,2},{7,3},{8,4},{9,5},{1... | collective-permute-start | bytes 3342344 | tf_op jit(solution)/shard_map/ppermute | solution.py:356
  42.2 2.8 %collective-permute-start.11 = (bf16[256,2048]{1,0:T(8,128)(2,1)}, bf16[256,2048]{1,0:T(8,128)(2,1)}, u32[]{:S(2)}, u32[]{:S(2)}) collective-permute-start(bf16[256,2048]{1,0:T(8,128)(2,1)} %pad_maximum_fusion.2.refs_2_), channel_id=1, source_target_pairs={{0,3},{1,0},{2,1},{3,2},{4,7},{5,4},{6,5},{7,6},{8,11},{9,8},{10,9... | collective-permute-start | bytes 3145736 | tf_op jit(solution)/shard_map/ppermute | solution.py:356
  47.7 1.9 pad.9.rel.rel_x
  49.6 6.8 %turn.1.wt_hbm = bf16[2,1024,2048]{2,1,0:T(8,128)(2,1)} custom-call(bf16[2,2048,512]{2,1,0:T(8,128)(2,1)} %wg.3, bf16[2,2048,512]{2,1,0:T(8,128)(2,1)} %wu.3), custom_call_target="tpu_custom_call" | custom-call | flops 268435456 | bytes 524288 | tf_op jit(solution)/shard_map/turn/pallas_call | solution.py:136
  56.4 11.5 %stage.2 = (bf16[2,4,192,2048]{3,2,1,0:T(8,128)(2,1)}, bf16[2,4,192,512]{3,2,1,0:T(8,128)(2,1)}, bf16[2,4,192,512]{3,2,1,0:T(8,128)(2,1)}, bf16[2,4,192,512]{3,2...) custom-call(s32[4,4,256]{2,1,0:T(4,128)} %reshape.197.tgt_x.tgt, ...), custom_call_target="tpu_custom_call" | custom-call | flops 268435456 | bytes 524288 | tf_op jit(solution)/shard_map/stage/pallas_call | solution.py:107
  68.2 3.2 %collective-permute-start.19 = (bf16[256,2048]{1,0:T(8,128)(2,1)S(1)}, bf16[256,2048]{1,0:T(8,128)(2,1)S(1)}, u32[]{:S(2)}, u32[]{:S(2)}) collective-permute-start(bf16[256,2048]{1,0:T(8,128)(2,1)S(1)} %copy-done.5), channel_id=1, source_target_pairs={{0,3},{1,0},{2,1},{3,2},{4,7},{5,4},{6,5},{7,6},{8,11},{9,8},{10,9... | collective-permute-start | bytes 3145736 | tf_op jit(solution)/shard_map/ppermute | solution.py:356
  71.4 3.2 %collective-permute-start.17 = (bf16[256,2176]{1,0:T(8,128)(2,1)S(1)}, bf16[256,2176]{1,0:T(8,128)(2,1)S(1)}, u32[]{:S(2)}, u32[]{:S(2)}) collective-permute-start(bf16[256,2176]{1,0:T(8,128)(2,1)S(1)} %copy-done.1), channel_id=1, source_target_pairs={{0,12},{1,13},{2,14},{3,15},{4,0},{5,1},{6,2},{7,3},{8,4},{9,5},{1... | collective-permute-start | bytes 3342344 | tf_op jit(solution)/shard_map/ppermute | solution.py:356
  74.6 16.7 %collective-permute-done.18.refs_4_ = bf16[256,2048]{1,0:T(8,128)(2,1)S(1)} collective-permute-done((bf16[256,2048]{1,0:T(8,128)(2,1)}, bf16[256,2048]{1,0:T(8,128)(2,1)S(1)}, u32[]{:S(2)}, u32[]{:S(2)}) %collective-permute-start.18) | collective-permute-done | bytes 1048608 | tf_op jit(solution)/shard_map/ppermute | solution.py:356
  91.3 3.2 %collective-permute-start.14 = (bf16[256,2048]{1,0:T(8,128)(2,1)}, bf16[256,2048]{1,0:T(8,128)(2,1)S(1)}, u32[]{:S(2)}, u32[]{:S(2)}) collective-permute-start(bf16[256,2048]{1,0:T(8,128)(2,1)} %collective-permute-done.11.refs_6_), channel_id=1, source_target_pairs={{0,3},{1,0},{2,1},{3,2},{4,7},{5,4},{6,5},{7,6},{8,11},{9,8},{10,9... | collective-permute-start | bytes 3145736 | tf_op jit(solution)/shard_map/ppermute | solution.py:356
  95.4 4.2 %collective-permute-done.17.refs_3_ = bf16[256,2176]{1,0:T(8,128)(2,1)S(1)} collective-permute-done((bf16[256,2176]{1,0:T(8,128)(2,1)S(1)}, bf16[256,2176]{1,0:T(8,128)(2,1)S(1)}, u32[]{:S(2)}, u32[]{:S(2)}) %collective-permute-start.17) | collective-permute-done | bytes 1114144 | tf_op jit(solution)/shard_map/ppermute | solution.py:356
  100.6 17.0 %stage.3 = (bf16[2,4,192,2048]{3,2,1,0:T(8,128)(2,1)}, bf16[2,4,192,512]{3,2,1,0:T(8,128)(2,1)}, bf16[2,4,192,512]{3,2,1,0:T(8,128)(2,1)}, bf16[2,4,192,512]{3,2...) custom-call(s32[4,4,256]{2,1,0:T(4,128)} %reshape.197.tgt_x.tgt, ...), custom_call_target="tpu_custom_call", output_to_operand_aliasing={{0}: (14, {}), {1}: (15, {}), {2}: (16, {}), {3}: (17, {}),... | custom-call | flops 268435456 | bytes 524288 | tf_op jit(solution)/shard_map/stage/pallas_call | solution.py:107
  118.5 25.4 %tail.1 = (bf16[2,4,192,2048]{3,2,1,0:T(8,128)(2,1)}, bf16[2,4,192,512]{3,2,1,0:T(8,128)(2,1)}, bf16[2,4,4,48,2048]{4,3,2,1,0:T(8,128)(2,1)}, bf16[2,768,1024]{2,1,0:T(8,128)(2,1)}, bf16[4,4,128,2176]{3,2,1,0:T(8,128)(2,1)}) custom-call(s32[8]{0:T(128)} %pad_add_fusion.4.place, ...), custom_call_target="tpu_custom_call", output_to_operand_aliasing={{0}: (14, {}), {1}: (15, {}), {2}: (16, {})} | custom-call | flops 15032385536 | bytes 33554432 | tf_op jit(solution)/shard_map/tail/pallas_call | solution.py:235
  144.5 12.2 %up_grad.1 = (bf16[4,2,256,1024]{3,2,1,0:T(8,128)(2,1)}, bf16[4,2,256,1024]{3,2,1,0:T(8,128)(2,1)}) custom-call(s32[2]{0:T(128)} %pad_add_fusion.5.where, bf16[2,768,2048]{2,1,0:T(8,128)(2,1)} %bitcast.84, bf16[2,768,1024]{2,1,0:T(8,128)(2,1)} %get-tuple-element.87.dhu), custom_call_target="tpu_custom_call" | custom-call | flops 6442450944 | bytes 16777216 | tf_op jit(solution)/shard_map/up_grad/pallas_call | solution.py:307
  156.7 7.8 %down_grad.1 = (bf16[4,2,64,2048]{3,2,1,0:T(8,128)(2,1)}, bf16[4,2,64,2048]{3,2,1,0:T(8,128)(2,1)}) custom-call(s32[2]{0:T(128)} %pad_add_fusion.5.where, bf16[2,768,512]{2,1,0:T(8,128)(2,1)} %bitcast.87, bf16[2,768,2048]{2,1,0:T(8,128)(2,1)} %bitcast.85), custom_call_target="tpu_custom_call" | custom-call | flops 3221225472 | bytes 16777216 | tf_op jit(solution)/shard_map/down_grad/pallas_call | solution.py:307
  165.0 2.6 %fusion.9 = (bf16[1,256,1024]{2,1,0:T(8,128)(2,1)S(1)}, bf16[1,256,1024]{2,1,0:T(8,128)(2,1)S(1)}, bf16[256,1024]{1,0:T(8,128)(2,1)S(1)}, bf16[256,1024]{1,0:T(8,128)(2,1)S(1)}) fusion(bf16[4,2,256,1024]{3,2,1,0:T(8,128)(2,1)} %collective-permute-done.20, bf16[4,2,256,1024]{3,2,1,0:T(8,128)(2,1)S(1)} %copy-done.3), kind=kLoop, calls=%fused_computation.25 | loop fusion | flops 4194304 | bytes 6291456 | tf_op jit(solution)/shard_map/add | solution.py:330
  169.8 12.0 %collective-permute-done.22 = bf16[256,1024]{1,0:T(8,128)(2,1)S(1)} collective-permute-done((bf16[256,1024]{1,0:T(8,128)(2,1)S(1)}, bf16[256,1024]{1,0:T(8,128)(2,1)S(1)}, u32[]{:S(2)}, u32[]{:S(2)}) %collective-permute-start.22) | collective-permute-done | bytes 524320 | tf_op jit(solution)/shard_map/ppermute | solution.py:335
  183.9 1.7 collective-permute-start.28
  185.7 1.8 fusion.11
  189.9 3.0 %collective-permute-done.26 = bf16[64,2048]{1,0:T(8,128)(2,1)S(1)} collective-permute-done((bf16[64,2048]{1,0:T(8,128)(2,1)S(1)}, bf16[64,2048]{1,0:T(8,128)(2,1)S(1)}, u32[]{:S(2)}, u32[]{:S(2)}) %collective-permute-start.26) | collective-permute-done | bytes 262176 | tf_op jit(solution)/shard_map/ppermute | solution.py:335
  195.7 29.0 %collective-permute-done.27 = bf16[2,64,2048]{2,1,0:T(8,128)(2,1)S(1)} collective-permute-done((bf16[2,64,2048]{2,1,0:T(8,128)(2,1)S(1)}, bf16[2,64,2048]{2,1,0:T(8,128)(2,1)S(1)}, u32[]{:S(2)}, u32[]{:S(2)}) %collective-permute-start.27) | collective-permute-done | bytes 524320 | tf_op jit(solution)/shard_map/ppermute | solution.py:343
  227.4 2.2 fusion.1
  232.0 1.9 slice.182
  (116 shorter events, 25.8 us)
Async XLA Ops:
  7.2 223.4 %reduce-scatter.4.cloned.1.call-start = ((), (), s32[]{:S(2)}) async-start(), calls=%async_computation.1 | async-start | bytes 9469952
  7.2 16.2 %collective-permute-start.4 = (bf16[128,2048]{1,0:T(8,128)(2,1)}, bf16[128,2048]{1,0:T(8,128)(2,1)S(1)}, u32[]{:S(2)}, u32[]{:S(2)}) collective-permute-start(bf16[128,2048]{1,0:T(8,128)(2,1)} %param.9), channel_id=1, source_target_pairs={{0,4},{1,5},{2,6},{3,7},{4,8},{5,9},{6,10},{7,11},{8,12},{9,13},{1... | collective-permute-start | bytes 1572872 | tf_op jit(solution)/shard_map/ppermute | solution.py:356
  9.2 14.4 %collective-permute-start.6 = (bf16[128,2048]{1,0:T(8,128)(2,1)}, bf16[128,2048]{1,0:T(8,128)(2,1)S(1)}, u32[]{:S(2)}, u32[]{:S(2)}) collective-permute-start(bf16[128,2048]{1,0:T(8,128)(2,1)} %param.9), channel_id=1, source_target_pairs={{0,12},{1,13},{2,14},{3,15},{4,0},{5,1},{6,2},{7,3},{8,4},{9,5},{1... | collective-permute-start | bytes 1572872 | tf_op jit(solution)/shard_map/ppermute | solution.py:356
  14.1 15.6 %collective-permute-start = (bf16[128,2176]{1,0:T(8,128)(2,1)}, bf16[128,2176]{1,0:T(8,128)(2,1)S(1)}, u32[]{:S(2)}, u32[]{:S(2)}) collective-permute-start(bf16[128,2176]{1,0:T(8,128)(2,1)} %pad_maximum_fusion.6), channel_id=1, source_target_pairs={{0,1},{1,2},{2,3},{3,0},{4,5},{5,6},{6,7},{7,4},{8,9},{9,10},{10,1... | collective-permute-start | bytes 1671176 | tf_op jit(solution)/shard_map/ppermute | solution.py:356
  15.7 14.4 %collective-permute-start.2 = (bf16[128,2176]{1,0:T(8,128)(2,1)}, bf16[128,2176]{1,0:T(8,128)(2,1)S(1)}, u32[]{:S(2)}, u32[]{:S(2)}) collective-permute-start(bf16[128,2176]{1,0:T(8,128)(2,1)} %pad_maximum_fusion.6), channel_id=1, source_target_pairs={{0,3},{1,0},{2,1},{3,2},{4,7},{5,4},{6,5},{7,6},{8,11},{9,8},{10,9... | collective-permute-start | bytes 1671176 | tf_op jit(solution)/shard_map/ppermute | solution.py:356
  23.5 9.7 %collective-permute-start.5 = (bf16[64,2048]{1,0:T(8,128)(2,1)S(1)}, bf16[64,2048]{1,0:T(8,128)(2,1)S(1)}, u32[]{:S(2)}, u32[]{:S(2)}) collective-permute-start(bf16[64,2048]{1,0:T(8,128)(2,1)S(1)} %slice.180), channel_id=1, source_target_pairs={{0,4},{1,5},{2,6},{3,7},{4,8},{5,9},{6,10},{7,11},{8,12},{9,13},{1... | collective-permute-start | bytes 786440 | tf_op jit(solution)/shard_map/ppermute | solution.py:356
  23.6 9.6 %collective-permute-start.7 = (bf16[64,2048]{1,0:T(8,128)(2,1)S(1)}, bf16[64,2048]{1,0:T(8,128)(2,1)S(1)}, u32[]{:S(2)}, u32[]{:S(2)}) collective-permute-start(bf16[64,2048]{1,0:T(8,128)(2,1)S(1)} %slice.181), channel_id=1, source_target_pairs={{0,12},{1,13},{2,14},{3,15},{4,0},{5,1},{6,2},{7,3},{8,4},{9,5},{1... | collective-permute-start | bytes 786440 | tf_op jit(solution)/shard_map/ppermute | solution.py:356
  29.7 8.6 %collective-permute-start.1 = (bf16[64,2176]{1,0:T(8,128)(2,1)S(1)}, bf16[64,2176]{1,0:T(8,128)(2,1)S(1)}, u32[]{:S(2)}, u32[]{:S(2)}) collective-permute-start(bf16[64,2176]{1,0:T(8,128)(2,1)S(1)} %slice.178), channel_id=1, source_target_pairs={{0,1},{1,2},{2,3},{3,0},{4,5},{5,6},{6,7},{7,4},{8,9},{9,10},{10,1... | collective-permute-start | bytes 835592 | tf_op jit(solution)/shard_map/ppermute | solution.py:356
  30.1 8.1 %collective-permute-start.3 = (bf16[64,2176]{1,0:T(8,128)(2,1)S(1)}, bf16[64,2176]{1,0:T(8,128)(2,1)S(1)}, u32[]{:S(2)}, u32[]{:S(2)}) collective-permute-start(bf16[64,2176]{1,0:T(8,128)(2,1)S(1)} %slice.179), channel_id=1, source_target_pairs={{0,3},{1,0},{2,1},{3,2},{4,7},{5,4},{6,5},{7,6},{8,11},{9,8},{10,9... | collective-permute-start | bytes 835592 | tf_op jit(solution)/shard_map/ppermute | solution.py:356
  38.4 29.6 %collective-permute-start.8 = (bf16[256,2176]{1,0:T(8,128)(2,1)S(1)}, bf16[256,2176]{1,0:T(8,128)(2,1)}, u32[]{:S(2)}, u32[]{:S(2)}) collective-permute-start(bf16[256,2176]{1,0:T(8,128)(2,1)S(1)} %pad_maximum_fusion.1.refs_1_), channel_id=1, source_target_pairs={{0,4},{1,5},{2,6},{3,7},{4,8},{5,9},{6,10},{7,11},{8,12},{9,13},{1... | collective-permute-start | bytes 3342344 | tf_op jit(solution)/shard_map/ppermute | solution.py:356
  38.5 29.5 %collective-permute-start.9 = (bf16[256,2176]{1,0:T(8,128)(2,1)S(1)}, bf16[256,2176]{1,0:T(8,128)(2,1)}, u32[]{:S(2)}, u32[]{:S(2)}) collective-permute-start(bf16[256,2176]{1,0:T(8,128)(2,1)S(1)} %pad_maximum_fusion.refs_0_), channel_id=1, source_target_pairs={{0,12},{1,13},{2,14},{3,15},{4,0},{5,1},{6,2},{7,3},{8,4},{9,5},{1... | collective-permute-start | bytes 3342344 | tf_op jit(solution)/shard_map/ppermute | solution.py:356
  41.7 26.2 %collective-permute-start.10 = (bf16[256,2048]{1,0:T(8,128)(2,1)S(1)}, bf16[256,2048]{1,0:T(8,128)(2,1)}, u32[]{:S(2)}, u32[]{:S(2)}) collective-permute-start(bf16[256,2048]{1,0:T(8,128)(2,1)S(1)} %pad_maximum_fusion.3.refs_3_), channel_id=1, source_target_pairs={{0,1},{1,2},{2,3},{3,0},{4,5},{5,6},{6,7},{7,4},{8,9},{9,10},{10,1... | collective-permute-start | bytes 3145736 | tf_op jit(solution)/shard_map/ppermute | solution.py:356
  42.2 25.7 %collective-permute-start.11 = (bf16[256,2048]{1,0:T(8,128)(2,1)}, bf16[256,2048]{1,0:T(8,128)(2,1)}, u32[]{:S(2)}, u32[]{:S(2)}) collective-permute-start(bf16[256,2048]{1,0:T(8,128)(2,1)} %pad_maximum_fusion.2.refs_2_), channel_id=1, source_target_pairs={{0,3},{1,0},{2,1},{3,2},{4,7},{5,4},{6,5},{7,6},{8,11},{9,8},{10,9... | collective-permute-start | bytes 3145736 | tf_op jit(solution)/shard_map/ppermute | solution.py:356
  56.4 38.3 %copy-start.13 = (s32[4]{0:T(128)S(1)}, s32[4]{0:T(128)}, u32[]{:S(2)}) copy-start(s32[4]{0:T(128)} %constant.105.clone) | copy-start | bytes 52
  68.0 26.5 %collective-permute-start.16 = (bf16[256,2176]{1,0:T(8,128)(2,1)}, bf16[256,2176]{1,0:T(8,128)(2,1)S(1)}, u32[]{:S(2)}, u32[]{:S(2)}) collective-permute-start(bf16[256,2176]{1,0:T(8,128)(2,1)} %copy-done.2), channel_id=1, source_target_pairs={{0,4},{1,5},{2,6},{3,7},{4,8},{5,9},{6,10},{7,11},{8,12},{9,13},{1... | collective-permute-start | bytes 3342344 | tf_op jit(solution)/shard_map/ppermute | solution.py:356
  68.1 23.2 %collective-permute-start.18 = (bf16[256,2048]{1,0:T(8,128)(2,1)}, bf16[256,2048]{1,0:T(8,128)(2,1)S(1)}, u32[]{:S(2)}, u32[]{:S(2)}) collective-permute-start(bf16[256,2048]{1,0:T(8,128)(2,1)} %pad_maximum_fusion.2.refs_2_), channel_id=1, source_target_pairs={{0,1},{1,2},{2,3},{3,0},{4,5},{5,6},{6,7},{7,4},{8,9},{9,10},{10,1... | collective-permute-start | bytes 3145736 | tf_op jit(solution)/shard_map/ppermute | solution.py:356
  68.2 23.1 %collective-permute-start.19 = (bf16[256,2048]{1,0:T(8,128)(2,1)S(1)}, bf16[256,2048]{1,0:T(8,128)(2,1)S(1)}, u32[]{:S(2)}, u32[]{:S(2)}) collective-permute-start(bf16[256,2048]{1,0:T(8,128)(2,1)S(1)} %copy-done.5), channel_id=1, source_target_pairs={{0,3},{1,0},{2,1},{3,2},{4,7},{5,4},{6,5},{7,6},{8,11},{9,8},{10,9... | collective-permute-start | bytes 3145736 | tf_op jit(solution)/shard_map/ppermute | solution.py:356
  71.4 28.2 %collective-permute-start.17 = (bf16[256,2176]{1,0:T(8,128)(2,1)S(1)}, bf16[256,2176]{1,0:T(8,128)(2,1)S(1)}, u32[]{:S(2)}, u32[]{:S(2)}) collective-permute-start(bf16[256,2176]{1,0:T(8,128)(2,1)S(1)} %copy-done.1), channel_id=1, source_target_pairs={{0,12},{1,13},{2,14},{3,15},{4,0},{5,1},{6,2},{7,3},{8,4},{9,5},{1... | collective-permute-start | bytes 3342344 | tf_op jit(solution)/shard_map/ppermute | solution.py:356
  74.5 43.8 %collective-permute-start.12 = (bf16[256,2176]{1,0:T(8,128)(2,1)}, bf16[256,2176]{1,0:T(8,128)(2,1)}, u32[]{:S(2)}, u32[]{:S(2)}) collective-permute-start(bf16[256,2176]{1,0:T(8,128)(2,1)} %collective-permute-done.9.refs_2_), channel_id=1, source_target_pairs={{0,12},{1,13},{2,14},{3,15},{4,0},{5,1},{6,2},{7,3},{8,4},{9,5},{1... | collective-permute-start | bytes 3342344 | tf_op jit(solution)/shard_map/ppermute | solution.py:356
  91.3 27.0 %collective-permute-start.13 = (bf16[256,2176]{1,0:T(8,128)(2,1)}, bf16[256,2176]{1,0:T(8,128)(2,1)}, u32[]{:S(2)}, u32[]{:S(2)}) collective-permute-start(bf16[256,2176]{1,0:T(8,128)(2,1)} %collective-permute-done.8.refs_1_), channel_id=1, source_target_pairs={{0,4},{1,5},{2,6},{3,7},{4,8},{5,9},{6,10},{7,11},{8,12},{9,13},{1... | collective-permute-start | bytes 3342344 | tf_op jit(solution)/shard_map/ppermute | solution.py:356
  91.3 26.2 %collective-permute-start.14 = (bf16[256,2048]{1,0:T(8,128)(2,1)}, bf16[256,2048]{1,0:T(8,128)(2,1)S(1)}, u32[]{:S(2)}, u32[]{:S(2)}) collective-permute-start(bf16[256,2048]{1,0:T(8,128)(2,1)} %collective-permute-done.11.refs_6_), channel_id=1, source_target_pairs={{0,3},{1,0},{2,1},{3,2},{4,7},{5,4},{6,5},{7,6},{8,11},{9,8},{10,9... | collective-permute-start | bytes 3145736 | tf_op jit(solution)/shard_map/ppermute | solution.py:356
  94.5 23.1 %collective-permute-start.15 = (bf16[256,2048]{1,0:T(8,128)(2,1)}, bf16[256,2048]{1,0:T(8,128)(2,1)}, u32[]{:S(2)}, u32[]{:S(2)}) collective-permute-start(bf16[256,2048]{1,0:T(8,128)(2,1)} %collective-permute-done.10.refs_5_), channel_id=1, source_target_pairs={{0,1},{1,2},{2,3},{3,0},{4,5},{5,6},{6,7},{7,4},{8,9},{9,10},{10,1... | collective-permute-start | bytes 3145736 | tf_op jit(solution)/shard_map/ppermute | solution.py:356
  156.7 8.3 %collective-permute-start.20 = (bf16[4,2,256,1024]{3,2,1,0:T(8,128)(2,1)}, bf16[4,2,256,1024]{3,2,1,0:T(8,128)(2,1)}, u32[]{:S(2)}, u32[]{:S(2)}) collective-permute-start(bf16[4,2,256,1024]{3,2,1,0:T(8,128)(2,1)} %get-tuple-element.89), channel_id=1, source_target_pairs={{0,16},{16,0},{32,48},{48,32},{64,80},{80,64},{96,112},{112,96},{1... | collective-permute-start | bytes 12582920 | tf_op jit(solution)/shard_map/ppermute | solution.py:326
  164.5 5.3 %collective-permute-start.21 = (bf16[4,2,64,2048]{3,2,1,0:T(8,128)(2,1)}, bf16[4,2,64,2048]{3,2,1,0:T(8,128)(2,1)S(1)}, u32[]{:S(2)}, u32[]{:S(2)}) collective-permute-start(bf16[4,2,64,2048]{3,2,1,0:T(8,128)(2,1)} %get-tuple-element.92), channel_id=1, source_target_pairs={{0,16},{16,0},{32,48},{48,32},{64,80},{80,64},{96,112},{112,96},{1... | collective-permute-start | bytes 6291464 | tf_op jit(solution)/shard_map/ppermute | solution.py:326
  167.7 14.1 %collective-permute-start.22 = (bf16[256,1024]{1,0:T(8,128)(2,1)S(1)}, bf16[256,1024]{1,0:T(8,128)(2,1)S(1)}, u32[]{:S(2)}, u32[]{:S(2)}) collective-permute-start(bf16[256,1024]{1,0:T(8,128)(2,1)S(1)} %get-tuple-element.122), channel_id=1, source_target_pairs={{0,32},{16,48},{32,64},{48,80},{64,96},{80,112},{96,0},{112,16},{1... | collective-permute-start | bytes 1572872 | tf_op jit(solution)/shard_map/ppermute | solution.py:335
  168.2 14.9 %collective-permute-start.23 = (bf16[256,1024]{1,0:T(8,128)(2,1)S(1)}, bf16[256,1024]{1,0:T(8,128)(2,1)S(1)}, u32[]{:S(2)}, u32[]{:S(2)}) collective-permute-start(bf16[256,1024]{1,0:T(8,128)(2,1)S(1)} %get-tuple-element.121), channel_id=1, source_target_pairs={{0,96},{16,112},{32,0},{48,16},{64,32},{80,48},{96,64},{112,80},{1... | collective-permute-start | bytes 1572872 | tf_op jit(solution)/shard_map/ppermute | solution.py:336
  183.6 9.3 %collective-permute-start.26 = (bf16[64,2048]{1,0:T(8,128)(2,1)S(1)}, bf16[64,2048]{1,0:T(8,128)(2,1)S(1)}, u32[]{:S(2)}, u32[]{:S(2)}) collective-permute-start(bf16[64,2048]{1,0:T(8,128)(2,1)S(1)} %get-tuple-element.125), channel_id=1, source_target_pairs={{0,32},{16,48},{32,64},{48,80},{64,96},{80,112},{96,0},{112,16},{1... | collective-permute-start | bytes 786440 | tf_op jit(solution)/shard_map/ppermute | solution.py:335
  183.9 9.3 %collective-permute-start.28 = (bf16[64,2048]{1,0:T(8,128)(2,1)S(1)}, bf16[64,2048]{1,0:T(8,128)(2,1)S(1)}, u32[]{:S(2)}, u32[]{:S(2)}) collective-permute-start(bf16[64,2048]{1,0:T(8,128)(2,1)S(1)} %get-tuple-element.126), channel_id=1, source_target_pairs={{0,96},{16,112},{32,0},{48,16},{64,32},{80,48},{96,64},{112,80},{1... | collective-permute-start | bytes 786440 | tf_op jit(solution)/shard_map/ppermute | solution.py:336
  187.6 39.7 %collective-permute-start.24 = (bf16[2,256,1024]{2,1,0:T(8,128)(2,1)S(1)}, bf16[2,256,1024]{2,1,0:T(8,128)(2,1)S(1)}, u32[]{:S(2)}, u32[]{:S(2)}) collective-permute-start(bf16[2,256,1024]{2,1,0:T(8,128)(2,1)S(1)} %pad_maximum_fusion.4), channel_id=1, source_target_pairs={{0,32},{16,48},{32,64},{48,80},{64,96},{80,112},{96,0},{112,16},{1... | collective-permute-start | bytes 3145736 | tf_op jit(solution)/shard_map/ppermute | solution.py:343
  189.3 38.1 %collective-permute-start.25 = (bf16[2,256,1024]{2,1,0:T(8,128)(2,1)S(1)}, bf16[2,256,1024]{2,1,0:T(8,128)(2,1)S(1)}, u32[]{:S(2)}, u32[]{:S(2)}) collective-permute-start(bf16[2,256,1024]{2,1,0:T(8,128)(2,1)S(1)} %pad_maximum_fusion.5), channel_id=1, source_target_pairs={{0,96},{16,112},{32,0},{48,16},{64,32},{80,48},{96,64},{112,80},{1... | collective-permute-start | bytes 3145736 | tf_op jit(solution)/shard_map/ppermute | solution.py:343
  193.5 31.2 %collective-permute-start.27 = (bf16[2,64,2048]{2,1,0:T(8,128)(2,1)S(1)}, bf16[2,64,2048]{2,1,0:T(8,128)(2,1)S(1)}, u32[]{:S(2)}, u32[]{:S(2)}) collective-permute-start(bf16[2,64,2048]{2,1,0:T(8,128)(2,1)S(1)} %pad_maximum_fusion.7), channel_id=1, source_target_pairs={{0,32},{16,48},{32,64},{48,80},{64,96},{80,112},{96,0},{112,16},{1... | collective-permute-start | bytes 1572872 | tf_op jit(solution)/shard_map/ppermute | solution.py:343
  194.4 31.8 %collective-permute-start.29 = (bf16[2,64,2048]{2,1,0:T(8,128)(2,1)S(1)}, bf16[2,64,2048]{2,1,0:T(8,128)(2,1)S(1)}, u32[]{:S(2)}, u32[]{:S(2)}) collective-permute-start(bf16[2,64,2048]{2,1,0:T(8,128)(2,1)S(1)} %pad_maximum_fusion.8), channel_id=1, source_target_pairs={{0,96},{16,112},{32,0},{48,16},{64,32},{80,48},{96,64},{112,80},{1... | collective-permute-start | bytes 1572872 | tf_op jit(solution)/shard_map/ppermute | solution.py:343
  (14 other events, 124.0 us)
Sparse Core Ops, SparseCore 0:
  144.0 85.6 reduce-scatter.3
